TPU v7x, 32 devices: a whole 2x2x4 slice. The times are simulated.
32 devices in a mesh: node: 16 (over z, y, x), rel: 2 (over core).
Axes of the slice: x: 2, y: 2, z: 4, core: 2. Of those that a mesh axis runs over, the one named last changes fastest.
Arguments:
- features: bfloat16 [8192, 768], P('node'), may hold values from -6 to 6
- history: bfloat16 [8192, 768], P('node'), may hold values from -6 to 6
- history_mean: bfloat16 [6, 4096, 768], P('rel', 'node'), may hold values from -6 to 6
- weights: bfloat16 [6, 768, 768], P('rel'), may hold values from -0.09375 to 0.09375
- source_rows: int32 [6, 8192], P('rel', 'node'), may hold values from 0 to 511
- target_owner: int32 [6, 8192, 1], P('rel', 'node'), may hold values from 0 to 15; in each aligned block of 512 rows (0 to 511, 512 to 1023, ..., all dimensions but the last counted through in order) at most 80 rows name the same one
- target_rows: int32 [6, 8192], P('rel', 'node'), may hold values from 0 to 255
- cotangent: bfloat16 [4096, 768], P('node'), may hold values from -6 to 6
Outputs:
- layer_out: bfloat16 [4096, 768], P('node')
- weight_grads: float32 [6, 768, 768], P('rel')
- feature_grads: bfloat16 [8192, 768], P('node')
Inputs may be any that keep to these rules, and one draw needn't show every extreme that they name: `target_owner`: within each relation, among the 512 edges of one owner's aligned block, at most 80 name the same target owner, and some target owner is named by exactly 80 of them.
All inputs are finite; a program needn't handle non-finite values.
Results may differ from a plain program's by a relative error of at most 0.0055.
Values may be sent and summed in bfloat16 or wider, within the bound.
No kernel may reach another device: no remote copies, remote signals or barrier semaphores. Data moves between devices by JAX's collectives and lax.ppermute only.
A program may use at most 128 MiB of HBM per device.

v0:
```python
import jax
import jax.numpy as jnp
from jax import lax
from jax.sharding import PartitionSpec as P


def body(
    features, history, history_mean, weights, source_rows, target_owner, target_rows, cotangent
):
    deltas = (features.astype(jnp.float32) - history.astype(jnp.float32)).astype(jnp.bfloat16)
    groups = weights.shape[0]
    width = weights.shape[1]
    batch_dev = history_mean.shape[1]
    node_dev = features.shape[0]
    msg_dev = source_rows.shape[1]
    owners = lax.axis_size("node")
    capacity = 5 * msg_dev // (2 * owners)
    slots = owners * capacity
    scale = 1.0 / (msg_dev // batch_dev)
    norm_scale = 1.0 / jnp.sqrt(jnp.float32(batch_dev * owners))
    owner_ids = target_owner[:, :, 0]
    owner_hot = (
        owner_ids[:, :, None] == jnp.arange(owners, dtype=jnp.int32)[None, None, :]
    ).astype(jnp.int32)
    before = jnp.cumsum(owner_hot, axis=1) - owner_hot
    place = jnp.sum(before * owner_hot, axis=2)
    slot_ids = owner_ids * capacity + place
    slot_match = slot_ids[:, None, :] == jnp.arange(slots, dtype=jnp.int32)[None, :, None]
    selector = slot_match.astype(jnp.bfloat16)
    tags = jnp.sum(jnp.where(slot_match, target_rows[:, None, :] + 1, 0), axis=2) - 1
    edge_rows = jnp.take(deltas, source_rows, axis=0)
    outgoing = jnp.einsum(
        "rsm,rmd->rsd", selector, edge_rows, preferred_element_type=jnp.float32
    ).astype(jnp.bfloat16)
    outgoing = outgoing.reshape(groups, owners, capacity, width)
    tags = tags.reshape(groups, owners, capacity)
    rows = lax.all_to_all(outgoing, "node", split_axis=1, concat_axis=1, tiled=True)
    labels = lax.all_to_all(tags, "node", split_axis=1, concat_axis=1, tiled=True)
    count = rows.shape[0]
    flat_rows = rows.reshape(count, -1, width)
    flat_labels = labels.reshape(count, -1)
    picks = (
        flat_labels[:, None, :] == jnp.arange(batch_dev, dtype=jnp.int32)[None, :, None]
    ).astype(jnp.bfloat16)
    summed = jnp.einsum("rbs,rsd->rbd", picks, flat_rows, preferred_element_type=jnp.float32)
    summed, arrived = (summed, flat_labels)
    aggregate = (history_mean.astype(jnp.float32) + scale * summed).astype(jnp.bfloat16)
    partial_out = jnp.einsum("rbd,rde->be", aggregate, weights, preferred_element_type=jnp.float32)
    layer_out = lax.psum(partial_out, "rel").astype(jnp.bfloat16)
    arrived_hot = (
        arrived[:, :, None] == jnp.arange(batch_dev, dtype=jnp.int32)[None, None, :]
    ).astype(jnp.bfloat16)
    node_grads = (
        scale * jnp.einsum("be,rde->rbd", cotangent, weights, preferred_element_type=jnp.float32)
    ).astype(jnp.bfloat16)
    grad_rows = jnp.einsum(
        "rsb,rbd->rsd", arrived_hot, node_grads, preferred_element_type=jnp.float32
    ).astype(jnp.bfloat16)
    returned = lax.all_to_all(
        grad_rows.reshape(groups, owners, capacity, width),
        "node",
        split_axis=1,
        concat_axis=1,
        tiled=True,
    )
    edge_grads = jnp.einsum(
        "rsm,rsd->rmd",
        selector,
        returned.reshape(groups, slots, width),
        preferred_element_type=jnp.float32,
    ).astype(jnp.bfloat16)
    source_hot = (
        source_rows[:, :, None] == jnp.arange(node_dev, dtype=jnp.int32)[None, None, :]
    ).astype(jnp.bfloat16)
    partial_grads = jnp.einsum(
        "rmu,rmd->ud", source_hot, edge_grads, preferred_element_type=jnp.float32
    )
    local_grads = (
        jnp.einsum("rbd,be->rde", aggregate, cotangent, preferred_element_type=jnp.float32)
        * norm_scale
    )
    weight_grads = lax.psum(local_grads, "node")
    feature_grads = lax.psum(partial_grads, "rel").astype(jnp.bfloat16)
    return (layer_out, weight_grads, feature_grads)


def solution(mesh):
    in_specs = (
        P("node", None),
        P("node", None),
        P("rel", "node", None),
        P("rel", None, None),
        P("rel", "node"),
        P("rel", "node", None),
        P("rel", "node"),
        P("node", None),
    )
    out_specs = (P("node", None), P("rel", None, None), P("node", None))
    return jax.shard_map(body, mesh=mesh, in_specs=in_specs, out_specs=out_specs, check_vma=False)
```

profile of v0, /device:TPU:0, one launch (start us, length us, event | category | flops | bytes accessed | tf_op | source)
XLA Modules:
  0.0 555.7 jit_solution(7354062005008364038)
XLA Ops:
  7.2 0.0 copy-start
  7.2 0.8 copy.39
  8.0 1.5 fusion.24
  9.6 7.3 %reduce-window.6 = s32[3,16,4,128]{3,1,2,0:T(8,128)} reduce-window(s32[3,16,4,128]{3,1,2,0:T(8,128)} %fusion.24, s32[]{:T(128)} %constant.12.clone.1), window={size=1x1x1x128 pad=0_0x0_0x0_0x127_0}, to_apply=%region_0.0 | reduce-window | flops 3121152 | bytes 196612 | tf_op jit(solution)/shard_map/reduce-window
  16.8 1.3 slice_reduce_fusion
  18.1 0.6 reduce-window.9
  18.7 0.7 slice.11
  19.4 1.0 fusion.23
  20.4 0.7 multiply_add_fusion
  21.2 0.6 copy-done.5
  21.8 1.2 select_reduce_fusion
  23.0 0.6 broadcast_add_fusion
  23.6 1.4 sub.14
  25.0 1.4 copy.40
  26.4 1.4 reshape.70
  27.8 8.3 %all-to-all-start = ((s32[16,1,240]{2,1,0:T(1,128)}), s32[16,1,240]{2,1,0:T(1,128)S(1)}, u32[]{:S(2)}, u32[]{:S(2)}) async-start(s32[16,1,240]{2,1,0:T(1,128)} %reshape.70), calls=%async_computation | async-start | bytes 32768 | tf_op jit(solution)/shard_map/all_to_all | solution.py:38
  36.2 1.3 compare_and_fusion
  37.5 1.3 compare_select_fusion
  38.8 1.3 reshape.58
  40.1 1.3 pad_clamp_fusion
  41.4 2.4 subtract_convert_fusion
  43.8 8.1 %gather_fusion = bf16[1536,768]{1,0:T(8,128)(2,1)} fusion(bf16[512,768]{1,0:T(8,128)(2,1)} %subtract_convert_fusion, s32[2048]{0:T(1024)} %pad_clamp_fusion), kind=kCustom, calls=%fused_computation | custom fusion | bytes 4724736 | tf_op jit(solution)/shard_map/jit(_take)/gather | solution.py:31
  51.8 5.2 fusion.2
  57.0 3.0 copy.25
  60.0 0.6 copy-done.3
  60.6 7.0 %all-to-all-start.1 = ((bf16[3,16,80,768]{3,2,0,1:T(8,128)(2,1)}), bf16[3,16,80,768]{3,2,0,1:T(8,128)(2,1)}, u32[]{:S(2)}, u32[]{:S(2)}) async-start(bf16[3,16,80,768]{3,2,0,1:T(8,128)(2,1)} %copy.25), calls=%async_computation.1 | async-start | bytes 11796480 | tf_op jit(solution)/shard_map/all_to_all | solution.py:37
  67.5 0.5 broadcast.53
  68.0 1.4 reduce.2
  69.5 0.7 reshape.71
  70.2 1.4 copy.23
  71.5 1.4 eq.87
  73.0 8.6 %convolution_convert_fusion = bf16[3,1280,768]{2,1,0:T(8,128)(2,1)} fusion(s32[3,1280]{1,0:T(4,128)} %eq.87, bf16[3,768,768]{2,1,0:T(8,128)(2,1)S(1)} %copy-done, bf16[256,768]{1,0:T(8,128)(2,1)} %param.15), kind=kOutput, calls=%fused_computation.6 | convolution fusion | flops 2421030912 | bytes 9845760 | tf_op jit(solution)/shard_map/rsb,rbd->rsd/dot_general | solution.py:56
  81.5 5.5 copy.28
  87.1 90.1 %all-to-all-done.1 = bf16[3,16,80,768]{3,2,0,1:T(8,128)(2,1)} async-done(((bf16[3,16,80,768]{3,2,0,1:T(8,128)(2,1)}), bf16[3,16,80,768]{3,2,0,1:T(8,128)(2,1)}, u32[]{:S(2)}, u32[]{:S(2)}) %all-to-all-start.1) | async-done | bytes 5898272 | tf_op jit(solution)/shard_map/all_to_all | solution.py:37
  177.1 27.1 %all-to-all-start.2 = ((bf16[3,16,80,768]{3,2,0,1:T(8,128)(2,1)}), bf16[3,16,80,768]{3,2,0,1:T(8,128)(2,1)}, u32[]{:S(2)}, u32[]{:S(2)}) async-start(bf16[3,16,80,768]{3,2,0,1:T(8,128)(2,1)} %copy.28), calls=%async_computation.2 | async-start | bytes 11796480 | tf_op jit(solution)/shard_map/all_to_all | solution.py:59
  204.3 0.2 all-reduce.4.cloned.1.call-start
  204.5 3.2 copy.26
  207.8 1.9 add_convert_fusion
  209.7 1.0 copy-done.1
  210.7 4.1 broadcast_multiply_fusion
  214.8 0.0 all-reduce.4.cloned.1.call-update
  214.8 3.2 convolution_bitcast_fusion
  218.1 152.0 %all-to-all-done.2 = bf16[3,16,80,768]{3,2,0,1:T(8,128)(2,1)} async-done(((bf16[3,16,80,768]{3,2,0,1:T(8,128)(2,1)}), bf16[3,16,80,768]{3,2,0,1:T(8,128)(2,1)}, u32[]{:S(2)}, u32[]{:S(2)}) %all-to-all-start.2) | async-done | bytes 5898272 | tf_op jit(solution)/shard_map/all_to_all | solution.py:59
  370.1 5.7 %copy.29 = bf16[3,16,80,768]{3,2,1,0:T(8,128)(2,1)} copy(bf16[3,16,80,768]{3,2,0,1:T(8,128)(2,1)} %all-to-all-done.2) | data formatting | bytes 11796480 | tf_op jit(solution)/shard_map/all_to_all | solution.py:59
  375.8 9.1 %fusion.13 = f32[512,768]{1,0:T(8,128)} fusion(s32[3,512]{1,0:T(4,128)S(1)} %copy-done.4, bf16[3,1280,768]{2,1,0:T(8,128)(2,1)} %bitcast.52, s32[3,512]{1,0:T(4,128)S(1)} %copy-done.6), kind=kOutput, calls=%fused_computation.24 | convolution fusion | flops 4231790592 | bytes 7483392 | tf_op jit(solution)/shard_map/rmu,rmd->ud/dot_general | solution.py:75
  384.9 10.5 %all-reduce.5 = (bf16[256,768]{1,0:T(8,128)(2,1)}, bf16[512,768]{1,0:T(8,128)(2,1)}) all-reduce(f32[256,768]{1,0:T(8,128)} %convolution_bitcast_fusion, f32[512,768]{1,0:T(8,128)} %fusion.13), channel_id=1, replica_groups=mesh['node'=16,'rel'=2] {'rel'}, use_global_device_ids=true, to_apply=%region_4.5 | all-reduce | flops 589824 | bytes 3538944 | tf_op jit(solution)/shard_map/psum | solution.py:49
  395.4 147.0 %all-reduce.4.cloned.1.call-done = f32[3,768,768]{2,1,0:T(8,128)} async-done(((f32[3,768,768]{2,1,0:T(8,128)}), f32[3,768,768]{2,1,0:T(8,128)}) %all-reduce.4.cloned.1.call-update) | async-done | bytes 7077904 | tf_op jit(solution)/shard_map/psum | solution.py:82
  542.4 6.4 %copy.46 = f32[3,768,768]{2,1,0:T(8,128)} copy(f32[3,768,768]{2,1,0:T(8,128)} %all-reduce.4.cloned.1.call-done) | data formatting | bytes 14155776
  (15 shorter events, 0.0 us)
Async XLA Ops:
  7.2 65.8 %copy-start = (bf16[3,768,768]{2,1,0:T(8,128)(2,1)S(1)}, bf16[3,768,768]{2,1,0:T(8,128)(2,1)}, u32[]{:S(2)}) copy-start(bf16[3,768,768]{2,1,0:T(8,128)(2,1)} %param.11) | copy-start | bytes 10616836
  21.2 0.6 copy-start.5
  27.8 32.1 %all-to-all-start = ((s32[16,1,240]{2,1,0:T(1,128)}), s32[16,1,240]{2,1,0:T(1,128)S(1)}, u32[]{:S(2)}, u32[]{:S(2)}) async-start(s32[16,1,240]{2,1,0:T(1,128)} %reshape.70), calls=%async_computation | async-start | bytes 32768 | tf_op jit(solution)/shard_map/all_to_all | solution.py:38
  60.0 0.6 copy-start.3
  60.6 116.6 %all-to-all-start.1 = ((bf16[3,16,80,768]{3,2,0,1:T(8,128)(2,1)}), bf16[3,16,80,768]{3,2,0,1:T(8,128)(2,1)}, u32[]{:S(2)}, u32[]{:S(2)}) async-start(bf16[3,16,80,768]{3,2,0,1:T(8,128)(2,1)} %copy.25), calls=%async_computation.1 | async-start | bytes 11796480 | tf_op jit(solution)/shard_map/all_to_all | solution.py:37
  177.1 193.0 %all-to-all-start.2 = ((bf16[3,16,80,768]{3,2,0,1:T(8,128)(2,1)}), bf16[3,16,80,768]{3,2,0,1:T(8,128)(2,1)}, u32[]{:S(2)}, u32[]{:S(2)}) async-start(bf16[3,16,80,768]{3,2,0,1:T(8,128)(2,1)} %copy.28), calls=%async_computation.2 | async-start | bytes 11796480 | tf_op jit(solution)/shard_map/all_to_all | solution.py:59
  204.3 338.1 %all-reduce.4.cloned.1.call-start = ((), (), s32[]{:S(2)}) async-start(), calls=%async_computation.3 | async-start | bytes 14155776 | tf_op jit(solution)/shard_map/psum | solution.py:82
  204.5 3.3 copy-start.7
  204.5 3.3 copy-start.8
  207.8 2.9 copy-start.2
  209.7 1.0 copy-start.1
  218.1 157.8 %copy-start.4 = (s32[3,512]{1,0:T(4,128)S(1)}, s32[3,512]{1,0:T(4,128)}, u32[]{:S(2)}) copy-start(s32[3,512]{1,0:T(4,128)} %param.12) | copy-start | bytes 18436
  218.1 157.8 %copy-start.6 = (s32[3,512]{1,0:T(4,128)S(1)}, s32[3,512]{1,0:T(4,128)}, u32[]{:S(2)}) copy-start(s32[3,512]{1,0:T(4,128)} %copy-done.5) | copy-start | bytes 18436
Sparse Core Ops, SparseCore 0:
  214.9 327.4 all-reduce.3
where the time goes:
time: 558 us; the launch traced here: 556 us
  waiting for transfers between devices  389 us (70%)
  local copies, waits for them, and re-layouts  46.5 us (8%)
  starting transfers between devices  42.6 us (8%)
  matrix products  32 us (6%)
  other arithmetic  20.7 us (4%)
  between operations  14.2 us (3%)
  blocking collectives  10.5 us (2%)
    all_to_all x1, waiting for transfers between devices, body(): lax.all_to_all(grad_rows.reshape(groups, owners, capacity, width), 'node'...  152 us
    psum x1, waiting for transfers between devices, body(): weight_grads = lax.psum(local_grads, 'node')  147 us
    all_to_all x1, waiting for transfers between devices, body(): lax.all_to_all(outgoing, 'node', split_axis=1, concat_axis=1, tiled=True)  90.1 us
    all_to_all x1, starting transfers between devices, body(): lax.all_to_all(grad_rows.reshape(groups, owners, capacity, width), 'node'...  27.1 us
    unnamed x22, local copies, waits for them, and re-layouts  11.7 us
  transfers between devices with their start and end apart: 4, of which 3 were waited for; matrix products, arithmetic and copies ran while one was open for 13% of the time, Pallas kernels for 0%

commit v1 on v0

v1 whole, which is shorter than its diff:
```python
import functools

import jax
import jax.numpy as jnp
from jax import lax
from jax.experimental import pallas as pl
from jax.experimental.pallas import tpu as pltpu
from jax.sharding import PartitionSpec as P

BF = jnp.bfloat16
F32 = jnp.float32
AXES = ("node", "rel")
DEPTH, SIDE = 4, 2
NODES_HERE = DEPTH * SIDE * SIDE


def dot(a, b, dims=((1,), (0,))):
    return lax.dot_general(a, b, (dims, ((), ())), preferred_element_type=F32)


def cost(flops, moved):
    return pl.CostEstimate(flops=int(flops), bytes_accessed=int(moved), transcendentals=0)


def params(steps=1):
    return pltpu.CompilerParams(
        dimension_semantics=("arbitrary",) * steps, vmem_limit_bytes=48 * 1024 * 1024
    )


def pairs(move):
    listed = []
    for node in range(NODES_HERE):
        for core in range(2):
            z, y, x = node // 4, node // 2 % 2, node % 2
            tz, ty, tx, tc = move(z, y, x, core)
            listed.append((node * 2 + core, (tz * 4 + ty * 2 + tx) * 2 + tc))
    return listed


FIRST = pairs(lambda z, y, x, c: (z, y ^ (1 - c), x ^ c, c))
SECOND = pairs(lambda z, y, x, c: (z, y ^ c, x ^ (1 - c), c))
ALONG = [pairs(lambda z, y, x, c, k=k: ((z + k) % DEPTH, y, x, c)) for k in range(DEPTH)]
CORES = pairs(lambda z, y, x, c: (z, y, x, 1 - c))


def hop(array, table):
    return lax.ppermute(array, AXES, table)


def owner_of(pos_ref, core, first, second, depth):
    z, y, x = pos_ref[0], pos_ref[1], pos_ref[2]
    flip_y = jnp.where(core == 0, first, second)
    flip_x = jnp.where(core == 0, second, first)
    y = y + flip_y - 2 * y * flip_y
    x = x + flip_x - 2 * x * flip_x
    return lax.rem(z + depth + DEPTH, DEPTH) * 4 + y * 2 + x


def edges_kernel(scale, feat, hist, mean, weight, src, dst, moved, sent, spread, local):
    step = pl.program_id(0)
    nodes, msgs = feat.shape[0], src.shape[2]
    deltas = (feat[...].astype(F32) - hist[...].astype(F32)).astype(BF)
    column = jnp.transpose(jnp.broadcast_to(src[0], (128, msgs)))
    lanes = lax.broadcasted_iota(jnp.int32, (msgs, 128), 1)
    hot = jnp.concatenate(
        [(column == lanes + n).astype(F32).astype(BF) for n in range(0, nodes, 128)], axis=1
    )
    rows = dot(hot, deltas).astype(BF)
    moved[0] = rows
    sent[0] = (scale * dot(rows, weight[0])).astype(BF)
    spread[0] = jnp.transpose(jnp.broadcast_to(dst[0], (128, msgs)))
    own = dot(mean[0], weight[0])

    @pl.when(step == 0)
    def _():
        local[...] = own

    @pl.when(step > 0)
    def _():
        local[...] += own


def edges(features, history, mean, weights, src, dst, scale):
    groups, width, _ = weights.shape
    nodes, batch, msgs = features.shape[0], mean.shape[1], src.shape[2]
    whole = lambda *shape: pl.BlockSpec(shape, lambda r: (0,) * len(shape))
    by_rel = lambda *shape: pl.BlockSpec((1,) + shape, lambda r: (r, 0, 0))
    return pl.pallas_call(
        functools.partial(edges_kernel, scale),
        grid=(groups,),
        in_specs=[
            whole(nodes, width),
            whole(nodes, width),
            by_rel(batch, width),
            by_rel(width, width),
            by_rel(1, msgs),
            by_rel(1, msgs),
        ],
        out_specs=[
            by_rel(msgs, width),
            by_rel(msgs, width),
            by_rel(msgs, 128),
            whole(batch, width),
        ],
        out_shape=[
            jax.ShapeDtypeStruct((groups, msgs, width), BF),
            jax.ShapeDtypeStruct((groups, msgs, width), BF),
            jax.ShapeDtypeStruct((groups, msgs, 128), jnp.int32),
            jax.ShapeDtypeStruct((batch, width), F32),
        ],
        compiler_params=params(),
        cost_estimate=cost(2 * groups * msgs * width * (nodes + 1.5 * width), 12e6),
        name="edges",
    )(features, history, mean, weights, src, dst)


def partial_kernel(first, theirs, added, batch, pos, dst, sent, local, *rest):
    out = rest[-1]
    second = pl.program_id(0)
    half = batch // 2
    core = 1 - pos[3] if theirs else pos[3]
    rows = lax.broadcasted_iota(jnp.int32, (half, dst.shape[1]), 0)
    hot = []
    for depth in range(DEPTH):
        base = owner_of(pos, core, first, second, depth) * batch + core * half
        hot.append((dst[...] - base == rows).astype(F32).astype(BF))
    total = dot(jnp.concatenate(hot, axis=0), sent[...])
    if added:
        total = total + rest[0][...].astype(F32)
    out[...] = total.astype(out.dtype)
    if first == 0:

        @pl.when(second == 0)
        def _():
            own = local[pl.ds(pl.multiple_of(core * half, half), half), :]
            out[:half, :] = (total[:half] + own).astype(out.dtype)


def partial_rows(pos, dst, sent, local, first, theirs, added, dtype):
    batch, width = local.shape
    count = sent.shape[0]
    rows = DEPTH * batch // 2
    whole = lambda *shape: pl.BlockSpec(shape, lambda s, pos: (0,) * len(shape))
    piece = pl.BlockSpec((rows, width), lambda s, pos: (s, 0))
    more = [] if added is None else [added]
    return pl.pallas_call(
        functools.partial(partial_kernel, first, theirs, added is not None, batch),
        grid_spec=pltpu.PrefetchScalarGridSpec(
            num_scalar_prefetch=1,
            grid=(SIDE,),
            in_specs=[whole(1, count), whole(count, width), whole(batch, width)] + [piece] * len(more),
            out_specs=piece,
        ),
        out_shape=jax.ShapeDtypeStruct((SIDE * rows, width), dtype),
        compiler_params=params(),
        cost_estimate=cost(2 * SIDE * rows * width * count, 8e6),
        name="partial_rows",
    )(pos, dst, sent, local, *more)


def pick_kernel(layout, chained, batch, pos, spread, *rest):
    out = rest[-1]
    half = batch // 2
    lanes = lax.broadcasted_iota(jnp.int32, (spread.shape[1], half), 1)
    total = rest[-2][0].astype(F32) if chained else None
    for ref, (theirs, blocks) in zip(rest, layout):
        core = 1 - pos[3] if theirs else pos[3]
        hot = []
        for first, second, depth in blocks:
            base = owner_of(pos, core, first, second, -depth) * batch + core * half
            hot.append((spread[0] == lanes + base).astype(F32).astype(BF))
        term = dot(jnp.concatenate(hot, axis=1) if len(hot) > 1 else hot[0], ref[...])
        total = term if total is None else total + term
    out[0] = total.astype(BF)


def pick(pos, spread, batch, pieces, layout, before):
    groups, msgs, _ = spread.shape
    width = pieces[0].shape[1]
    by_rel = lambda *shape: pl.BlockSpec((1,) + shape, lambda r, pos: (r, 0, 0))
    more = [] if before is None else [before]
    rows = sum(piece.shape[0] for piece in pieces)
    return pl.pallas_call(
        functools.partial(pick_kernel, layout, before is not None, batch),
        grid_spec=pltpu.PrefetchScalarGridSpec(
            num_scalar_prefetch=1,
            grid=(groups,),
            in_specs=[by_rel(msgs, 128)]
            + [pl.BlockSpec(piece.shape, lambda r, pos: (0, 0)) for piece in pieces]
            + [by_rel(msgs, width)] * len(more),
            out_specs=by_rel(msgs, width),
        ),
        out_shape=jax.ShapeDtypeStruct((groups, msgs, width), BF),
        compiler_params=params(),
        cost_estimate=cost(2 * groups * msgs * width * rows, 6e6),
        name="pick_rows",
    )(pos, spread, *pieces, *more)


def back_kernel(scale, picked, weight, src, out):
    step = pl.program_id(0)
    grads = (scale * dot(picked[0], weight[0], ((1,), (1,)))).astype(BF)
    rows = lax.broadcasted_iota(jnp.int32, (out.shape[0], src.shape[2]), 0)
    term = dot((src[0] == rows).astype(F32).astype(BF), grads)

    @pl.when(step == 0)
    def _():
        out[...] = term

    @pl.when(step > 0)
    def _():
        out[...] += term


def back(picked, weights, src, nodes, scale):
    groups, msgs, width = picked.shape
    by_rel = lambda *shape: pl.BlockSpec((1,) + shape, lambda r: (r, 0, 0))
    return pl.pallas_call(
        functools.partial(back_kernel, scale),
        grid=(groups,),
        in_specs=[by_rel(msgs, width), by_rel(width, width), by_rel(1, msgs)],
        out_specs=pl.BlockSpec((nodes, width), lambda r: (0, 0)),
        out_shape=jax.ShapeDtypeStruct((nodes, width), F32),
        compiler_params=params(),
        cost_estimate=cost(2 * groups * msgs * width * (nodes + width), 8e6),
        name="feature_terms",
    )(picked, weights, src)


def weight_kernel(scale, norm, pos, mean, moved, cot, picked, away, kept):
    width = mean.shape[2]
    half = width // 2
    place = jnp.where(pos[3] == 0, pos[1], pos[2])
    for out, index in ((away, 1 - place), (kept, place)):
        columns = pl.ds(pl.multiple_of(index * half, 128), half)
        near = dot(mean[0, :, columns], cot[...], ((0,), (0,)))
        far = dot(moved[0, :, columns], picked[0], ((0,), (0,)))
        out[...] = (norm * (near + scale * far)).astype(out.dtype)


def weight_terms(pos, mean, moved, cot, picked, rel, scale, norm):
    _, batch, width = mean.shape
    msgs = moved.shape[1]
    by_rel = lambda *shape: pl.BlockSpec((1,) + shape, lambda s, pos: (rel, 0, 0))
    whole = lambda *shape: pl.BlockSpec(shape, lambda s, pos: (0,) * len(shape))
    return pl.pallas_call(
        functools.partial(weight_kernel, scale, norm),
        grid_spec=pltpu.PrefetchScalarGridSpec(
            num_scalar_prefetch=1,
            grid=(1,),
            in_specs=[by_rel(batch, width), by_rel(msgs, width), whole(batch, width), by_rel(msgs, width)],
            out_specs=[whole(width // 2, width), whole(width // 2, width)],
        ),
        out_shape=[
            jax.ShapeDtypeStruct((width // 2, width), BF),
            jax.ShapeDtypeStruct((width // 2, width), F32),
        ],
        compiler_params=params(),
        cost_estimate=cost(2 * width * width * (batch + msgs), 5e6),
        name="weight_terms",
    )(pos, mean, moved, cot, picked)


def assemble_kernel(pos, *refs):
    out = refs[-1]
    z, y, x, core = pos[0], pos[1], pos[2], pos[3]
    first = jnp.where(core == 0, y, x)
    second = jnp.where(core == 0, x, y)
    block = refs[0].shape[0]

    def put(row, value):
        out[0, pl.ds(pl.multiple_of(row, 16), value.shape[0]), :] = value.astype(F32)

    for ref, (flip_a, flip_b) in zip(refs[:4], ((0, 0), (0, 1), (1, 0), (1, 1))):
        a = first if flip_a == 0 else 1 - first
        b = second if flip_b == 0 else 1 - second
        for k in range(DEPTH):
            row = ((a * 2 + b) * DEPTH + lax.rem(z - k + DEPTH, DEPTH)) * (block // DEPTH)
            put(row, ref[k * (block // DEPTH) : (k + 1) * (block // DEPTH), :])


def assemble(pos, pieces, rel, groups, before):
    block, width = pieces[0].shape
    whole = lambda *shape: pl.BlockSpec(shape, lambda s, pos: (0,) * len(shape))
    more = [] if before is None else [before]
    return pl.pallas_call(
        assemble_kernel,
        grid_spec=pltpu.PrefetchScalarGridSpec(
            num_scalar_prefetch=1,
            grid=(1,),
            in_specs=[whole(block, width)] * 4 + [pl.BlockSpec(memory_space=pl.ANY)] * len(more),
            out_specs=pl.BlockSpec((1, width, width), lambda s, pos: (rel, 0, 0)),
        ),
        out_shape=jax.ShapeDtypeStruct((groups, width, width), F32),
        input_output_aliases={5: 0} if more else {},
        compiler_params=params(),
        cost_estimate=cost(0, 4e6),
        name="assemble",
    )(pos, *pieces, *more)


def body(
    features, history, history_mean, weights, source_rows, target_owner, target_rows, cotangent
):
    groups, width, _ = weights.shape
    batch = history_mean.shape[1]
    nodes = features.shape[0]
    msgs = source_rows.shape[1]
    owners = lax.axis_size("node")
    scale = 1.0 / (msgs // batch)
    dst = target_owner[:, :, 0] * batch + target_rows
    if owners != NODES_HERE:
        return anywhere(
            features, history, history_mean, weights, source_rows, dst, cotangent, scale
        )
    norm = (batch * owners) ** -0.5
    node = lax.axis_index("node")
    core = lax.axis_index("rel")
    z = node // 4
    pos = jnp.stack([z, node // 2 % 2, node % 2, core]).astype(jnp.int32)
    half = batch // 2
    src3, dst3 = source_rows[:, None, :], dst[:, None, :]

    mine = lax.dynamic_slice_in_dim(cotangent, core * half, half)
    other = lax.dynamic_slice_in_dim(cotangent, (1 - core) * half, half)
    deep = jnp.concatenate([hop(mine, ALONG[k]) for k in range(1, DEPTH)])
    near_b = hop(mine, SECOND)
    near_a = hop(mine, FIRST)
    near_ab = hop(near_b, FIRST)
    near = jnp.concatenate([near_a, near_b, near_ab])
    deep_b = hop(deep, SECOND)
    deep_a = hop(deep, FIRST)
    deep_ab = hop(deep_b, FIRST)

    moved, sent, spread, local = edges(
        features, history, history_mean, weights, src3, dst3, scale
    )
    flat = sent.reshape(groups * msgs, width)
    flat_dst = dst.reshape(1, groups * msgs)
    part = functools.partial(partial_rows, pos, flat_dst, flat, local)
    from_1 = hop(part(1, True, None, BF), CORES)
    from_0 = hop(part(0, True, None, BF), CORES)
    away = part(1, False, from_1, BF)
    kept = part(0, False, from_0, F32)

    swap = lambda array: hop(array, CORES)
    depths = tuple(range(1, DEPTH))
    near_blocks = ((1, 0, 0), (0, 1, 0), (1, 1, 0))
    at = lambda a, b: tuple((a, b, k) for k in depths)
    choose = functools.partial(pick, pos, spread, batch)
    picked = choose(
        [mine, other, near, swap(near)],
        ((False, ((0, 0, 0),)), (True, ((0, 0, 0),)), (False, near_blocks), (True, near_blocks)),
        None,
    )
    picked = choose([deep, swap(deep)], ((False, at(0, 0)), (True, at(0, 0))), picked)
    picked = choose(
        [deep_a, deep_b, swap(deep_a), swap(deep_b)],
        ((False, at(1, 0)), (False, at(0, 1)), (True, at(1, 0)), (True, at(0, 1))),
        picked,
    )
    picked = choose([deep_ab, swap(deep_ab)], ((False, at(1, 1)), (True, at(1, 1))), picked)

    kept = kept + hop(away, FIRST).astype(F32)
    rows = DEPTH * half
    kept = kept[:rows] + hop(kept[rows:].astype(BF), SECOND).astype(F32)
    total = kept[:half]
    for k in range(1, DEPTH):
        total = total + hop(kept[k * half : (k + 1) * half].astype(BF), ALONG[k]).astype(F32)
    total = total.astype(BF)
    opposite = hop(total, CORES)
    layer_out = jnp.where(
        core == 0, jnp.concatenate([total, opposite]), jnp.concatenate([opposite, total])
    )

    grads = None
    quarter = width // 4
    block = quarter // DEPTH
    place_b = jnp.where(core == 0, node % 2, node // 2 % 2)
    for rel in range(groups):
        away, kept = weight_terms(
            pos, history_mean, moved, cotangent, picked, rel, scale, norm
        )
        kept = kept + hop(away, FIRST).astype(F32)
        away = lax.dynamic_slice_in_dim(kept, (1 - place_b) * quarter, quarter).astype(BF)
        kept = lax.dynamic_slice_in_dim(kept, place_b * quarter, quarter)
        kept = kept + hop(away, SECOND).astype(F32)
        take = lambda k: lax.dynamic_slice_in_dim(kept, (z + k) % DEPTH * block, block)
        total = take(0)
        for k in range(1, DEPTH):
            total = total + hop(take(k).astype(BF), ALONG[k]).astype(F32)
        total = total.astype(BF)
        line = jnp.concatenate([total] + [hop(total, ALONG[k]) for k in range(1, DEPTH)])
        line_b = hop(line, SECOND)
        line_a = hop(line, FIRST)
        line_ab = hop(line_b, FIRST)
        grads = assemble(pos, [line, line_b, line_a, line_ab], rel, groups, grads)

    terms = back(picked, weights, src3, nodes, scale)
    feature_grads = (terms + hop(terms, CORES)).astype(BF)
    return layer_out, grads, feature_grads


def anywhere(features, history, history_mean, weights, source_rows, dst, cotangent, scale):
    groups, width, _ = weights.shape
    batch, nodes = cotangent.shape[0], features.shape[0]
    total_batch = batch * lax.axis_size("node")
    deltas = (features.astype(F32) - history.astype(F32)).astype(BF)
    every = lax.all_gather(cotangent, "node", tiled=True)
    out = jnp.zeros((total_batch, width), F32)
    local = jnp.zeros((batch, width), F32)
    terms = jnp.zeros((nodes, width), F32)
    grads = []
    for rel in range(groups):
        rows = jnp.take(deltas, source_rows[rel], axis=0)
        picked = jnp.take(every, dst[rel], axis=0)
        out = out.at[dst[rel]].add(scale * dot(rows, weights[rel]))
        local = local + dot(history_mean[rel], weights[rel])
        edge = (scale * dot(picked, weights[rel], ((1,), (1,)))).astype(BF)
        terms = terms.at[source_rows[rel]].add(edge.astype(F32))
        grads.append(
            dot(history_mean[rel], cotangent, ((0,), (0,)))
            + scale * dot(rows, picked, ((0,), (0,)))
        )
    layer_out = lax.psum(lax.psum_scatter(out, "node", tiled=True) + local, "rel").astype(BF)
    weight_grads = lax.psum(jnp.stack(grads) * total_batch**-0.5, "node")
    return layer_out, weight_grads, lax.psum(terms, "rel").astype(BF)


def solution(mesh):
    in_specs = (
        P("node", None),
        P("node", None),
        P("rel", "node", None),
        P("rel", None, None),
        P("rel", "node"),
        P("rel", "node", None),
        P("rel", "node"),
        P("node", None),
    )
    out_specs = (P("node", None), P("rel", None, None), P("node", None))
    return jax.shard_map(body, mesh=mesh, in_specs=in_specs, out_specs=out_specs, check_vma=False)
```

time: 558 us -> 220 us (0.39)
  waiting for transfers between devices: 389 us -> 49 us
  Pallas kernels: 0 us -> 70.9 us
  matrix products: 32 us -> 0 us
  starting transfers between devices: 42.6 us -> 66.6 us
  local copies, waits for them, and re-layouts: 46.5 us -> 23.8 us
  other arithmetic: 20.7 us -> 6.39 us
  between operations: 14.2 us -> 1.14 us
  blocking collectives: 10.5 us -> 0 us
    all_to_all x3 -> x0, waiting for transfers between devices: 242 us -> none  [the longest x1 152 us: body(): lax.all_to_all(grad_rows.reshape(groups, owners, capacity, width), 'node'...]
    psum x1 -> x0, waiting for transfers between devices: 147 us -> none  [body(): weight_grads = lax.psum(local_grads, 'node')]
    pallas_call x0 -> x16, Pallas kernels: none -> 70.9 us  [the longest x4 22.4 us: pick(): pl.pallas_call(functools.partial(pick_kernel, layout, before is not None,...]
    ppermute x0 -> x56, starting transfers between devices: none -> 66.6 us  [hop(): return lax.ppermute(array, AXES, table)]
    ppermute x0 -> x56, waiting for transfers between devices: none -> 49 us  [hop(): return lax.ppermute(array, AXES, table)]
    all_to_all x3 -> x0, starting transfers between devices: 42.4 us -> none  [the longest x1 27.1 us: body(): lax.all_to_all(grad_rows.reshape(groups, owners, capacity, width), 'node'...]
    dot_general x6 -> x0, matrix products: 32 us -> none  [the longest x1 9.09 us: body(): jnp.einsum('rmu,rmd->ud', source_hot, edge_grads, preferred_element_type=...]
    all_to_all x4 -> x0, local copies, waits for them, and re-layouts: 10.8 us -> none  [the longest x1 5.73 us: body(): lax.all_to_all(grad_rows.reshape(groups, owners, capacity, width), 'node'...]
  transfers between devices with their start and end apart: 4 -> 56, of which waited for: 3 -> 17; matrix products, arithmetic and copies ran while one was open for 13% -> 5% of each run, Pallas kernels for 0% -> 33%
where the time goes in v1:
time: 220 us; the launch traced here: 218 us
  Pallas kernels  70.9 us (32%)
  starting transfers between devices  66.6 us (30%)
  waiting for transfers between devices  49 us (22%)
  local copies, waits for them, and re-layouts  23.8 us (11%)
  other arithmetic  6.39 us (3%)
    ppermute x56, starting transfers between devices, hop(): return lax.ppermute(array, AXES, table)  66.6 us
    ppermute x56, waiting for transfers between devices, hop(): return lax.ppermute(array, AXES, table)  49 us
    pallas_call x4, Pallas kernels, pick(): pl.pallas_call(functools.partial(pick_kernel, layout, before is not None,...  22.4 us
    unnamed x55, local copies, waits for them, and re-layouts  20.7 us
    pallas_call x4, Pallas kernels, partial_rows(): pl.pallas_call(functools.partial(partial_kernel, first, theirs, added is...  20.3 us
    pallas_call x3, Pallas kernels, weight_terms(): pl.pallas_call(functools.partial(weight_kernel, scale, norm), grid_spec=p...  8.76 us
    pallas_call x1, Pallas kernels, edges(): pl.pallas_call(functools.partial(edges_kernel, scale), grid=(groups,), in...  7.51 us
    pallas_call x3, Pallas kernels, assemble(): pl.pallas_call(assemble_kernel, grid_spec=pltpu.PrefetchScalarGridSpec(nu...  6.32 us
  transfers between devices with their start and end apart: 56, of which 17 were waited for; matrix products, arithmetic and copies ran while one was open for 5% of the time, Pallas kernels for 33%

profile of v1, /device:TPU:0, one launch (start us, length us, event | category | flops | bytes accessed | tf_op | source)
XLA Modules:
  0.0 217.8 jit_solution(7243442879122932767)
XLA Ops:
  1.7 3.0 %collective-permute-start.19 = (bf16[128,768]{1,0:T(8,128)(2,1)S(1)}, bf16[128,768]{1,0:T(8,128)(2,1)S(1)}, u32[]{:S(2)}, u32[]{:S(2)}) collective-permute-start(bf16[128,768]{1,0:T(8,128)(2,1)S(1)} %get-tuple-element.38.rest_0_), channel_id=1, source_target_pairs={{0,2},{1,5},{2,0},{3,7},{4,6},{5,1},{6,4},{7,3},{8,10},{9,13},{10,... | collective-permute-start | bytes 589832 | tf_op jit(solution)/shard_map/ppermute | solution.py:48
  6.2 3.6 %collective-permute-start.10 = (bf16[128,768]{1,0:T(8,128)(2,1)S(1)}, bf16[128,768]{1,0:T(8,128)(2,1)}, u32[]{:S(2)}, u32[]{:S(2)}) collective-permute-start(bf16[128,768]{1,0:T(8,128)(2,1)S(1)} %get-tuple-element.38.rest_0_), channel_id=1, source_target_pairs={{0,24},{1,25},{2,26},{3,27},{4,28},{5,29},{6,30},{7,31},{8,0},{9,1... | collective-permute-start | bytes 589832 | tf_op jit(solution)/shard_map/ppermute | solution.py:48
  15.8 7.5 %edges.1 = (bf16[3,512,768]{2,1,0:T(8,128)(2,1)}, bf16[3,512,768]{2,1,0:T(8,128)(2,1)}, s32[3,512,128]{2,1,0:T(8,128)S(1)}, f32[256,768]{1,0:T(8,128)S(1)}) custom-call(bf16[512,768]{1,0:T(8,128)(2,1)S(1)} %copy-done.6, bf16[512,768]{1,0:T(8,128)(2,1)S(1)} %copy-done.7, bf16[3,256,768]{2,1,0:T(8,128)(2,1)S(1)} %copy-done.3, bf16[3,768,768]{2,1,0:T(8,128)(2,1)} %weight.3, ...), custom_call_target="tpu_custom_call" | custom-call | flops 3925868544 | bytes 12000000 | tf_op jit(solution)/shard_map/edges/pallas_call | solution.py:89
  28.6 1.7 copy-done.12
  30.2 4.2 %partial_rows.6 = bf16[1024,768]{1,0:T(8,128)(2,1)} custom-call(s32[4]{0:T(128)S(1)} %pad_add_fusion.pos, s32[1,1536]{1,0:T(1,128)S(1)} %bitcast.10, bf16[1536,768]{1,0:T(8,128)(2,1)S(1)} %bitcast.15, f32[256,768]{1,0:T(8,128)S(1)} %get-tuple-element.14.local), custom_call_target="tpu_custom_call" | custom-call | flops 2415919104 | bytes 8000000 | tf_op jit(solution)/shard_map/partial_rows/pallas_call | solution.py:147
  38.7 8.3 %collective-permute-done.20 = bf16[128,768]{1,0:T(8,128)(2,1)S(1)} collective-permute-done((bf16[128,768]{1,0:T(8,128)(2,1)S(1)}, bf16[128,768]{1,0:T(8,128)(2,1)S(1)}, u32[]{:S(2)}, u32[]{:S(2)}) %collective-permute-start.20) | collective-permute-done | bytes 196640 | tf_op jit(solution)/shard_map/ppermute | solution.py:48
  48.8 4.3 %partial_rows.4 = bf16[1024,768]{1,0:T(8,128)(2,1)} custom-call(s32[4]{0:T(128)S(1)} %pad_add_fusion.pos, s32[1,1536]{1,0:T(1,128)S(1)} %bitcast.11, bf16[1536,768]{1,0:T(8,128)(2,1)S(1)} %bitcast.16, f32[256,768]{1,0:T(8,128)S(1)} %copy-done.21), custom_call_target="tpu_custom_call" | custom-call | flops 2415919104 | bytes 8000000 | tf_op jit(solution)/shard_map/partial_rows/pallas_call | solution.py:147
  58.7 4.7 %pick_rows.4.rest_2_ = bf16[3,512,768]{2,1,0:T(8,128)(2,1)S(1)} custom-call(s32[4]{0:T(128)S(1)} %pad_add_fusion.pos, s32[3,512,128]{2,1,0:T(8,128)S(1)} %copy-done.18, bf16[128,768]{1,0:T(8,128)(2,1)S(1)} %get-tuple-element.38.rest_0_, bf16[128,768]{1,0:T(8,128)(2,1)S(1)} %get-tuple-element.37.rest_1_, ...), custom_call_target="tpu_custom_call" | custom-call | flops 2415919104 | bytes 6000000 | tf_op jit(solution)/shard_map/pick_rows/pallas_call | solution.py:184
  64.8 4.8 %pick_rows.5.rest_4_ = bf16[3,512,768]{2,1,0:T(8,128)(2,1)S(1)} custom-call(s32[4]{0:T(128)S(1)} %pad_add_fusion.pos, s32[3,512,128]{2,1,0:T(8,128)S(1)} %copy-done.18, bf16[384,768]{1,0:T(8,128)(2,1)S(1)} %constant_dynamic-update-slice_fusion.rest_0_, bf16[384,768]{1,0:T(8,128)(2,1)S(1)} %copy-done.9, bf16[3,512,768]{2,1,0:T(8,128)(2,1)} %copy-done.15), custom_call_target="tpu_custom_call" | custom-call | flops 1811939328 | bytes 6000000 | tf_op jit(solution)/shard_map/pick_rows/pallas_call | solution.py:184
  71.1 7.8 %pick_rows.6.rest_2_ = bf16[3,512,768]{2,1,0:T(8,128)(2,1)S(1)} custom-call(s32[4]{0:T(128)S(1)} %pad_add_fusion.pos, s32[3,512,128]{2,1,0:T(8,128)S(1)} %copy-done.18, bf16[384,768]{1,0:T(8,128)(2,1)} %collective-permute-done.14.rest_0_, bf16[384,768]{1,0:T(8,128)(2,1)} %collective-permute-done.11.rest_1_, ...), custom_call_target="tpu_custom_call" | custom-call | flops 3623878656 | bytes 6000000 | tf_op jit(solution)/shard_map/pick_rows/pallas_call | solution.py:184
  78.9 1.5 copy-done.14
  80.4 5.9 %partial_rows.7 = bf16[1024,768]{1,0:T(8,128)(2,1)} custom-call(s32[4]{0:T(128)S(1)} %pad_add_fusion.pos, s32[1,1536]{1,0:T(1,128)S(1)} %bitcast.12, bf16[1536,768]{1,0:T(8,128)(2,1)} %bitcast.14, f32[256,768]{1,0:T(8,128)S(1)} %copy-done.22, bf16[1024,768]{1,0:T(8,128)(2,1)S(1)} %collective-permute-done.1.rest_0_), custom_call_target="tpu_custom_call" | custom-call | flops 2415919104 | bytes 8000000 | tf_op jit(solution)/shard_map/partial_rows/pallas_call | solution.py:147
  87.2 5.1 %pick_rows.7.picked = bf16[3,512,768]{2,1,0:T(8,128)(2,1)S(1)} custom-call(s32[4]{0:T(128)S(1)} %pad_add_fusion.pos, s32[3,512,128]{2,1,0:T(8,128)S(1)} %copy-done.19, bf16[384,768]{1,0:T(8,128)(2,1)} %collective-permute-done.12.rest_0_, bf16[384,768]{1,0:T(8,128)(2,1)S(1)} %collective-permute-done.13.rest_1_, bf16[3,512,768]{2,1,0:T(8,128)(2,1)} %copy-done.14), custom_call_target="tpu_custom_call" | custom-call | flops 1811939328 | bytes 6000000 | tf_op jit(solution)/shard_map/pick_rows/pallas_call | solution.py:184
  93.9 3.0 %weight_terms.5 = (bf16[384,768]{1,0:T(8,128)(2,1)S(1)}, f32[384,768]{1,0:T(8,128)S(1)}) custom-call(s32[4]{0:T(128)S(1)} %pad_add_fusion.pos, bf16[3,256,768]{2,1,0:T(8,128)(2,1)S(1)} %copy-done.4, bf16[3,512,768]{2,1,0:T(8,128)(2,1)S(1)} %copy-done, bf16[256,768]{1,0:T(8,128)(2,1)S(1)} %copy-done.5, bf16[3,512,768]{2,1,0:T(8,128)(2,1)} %copy-done.1), custom_call_target="tpu_custom_call" | custom-call | flops 905969664 | bytes 5000000 | tf_op jit(solution)/shard_map/weight_terms/pallas_call | solution.py:247
  98.1 5.8 %partial_rows.5 = f32[1024,768]{1,0:T(8,128)} custom-call(s32[4]{0:T(128)S(1)} %pad_add_fusion.pos, s32[1,1536]{1,0:T(1,128)S(1)} %bitcast.13, bf16[1536,768]{1,0:T(8,128)(2,1)S(1)} %bitcast.17, f32[256,768]{1,0:T(8,128)S(1)} %copy-done.22, bf16[1024,768]{1,0:T(8,128)(2,1)} %collective-permute-done.rest_0_), custom_call_target="tpu_custom_call" | custom-call | flops 2415919104 | bytes 8000000 | tf_op jit(solution)/shard_map/partial_rows/pallas_call | solution.py:147
  103.9 3.0 %weight_terms.4 = (bf16[384,768]{1,0:T(8,128)(2,1)S(1)}, f32[384,768]{1,0:T(8,128)S(1)}) custom-call(s32[4]{0:T(128)S(1)} %pad_add_fusion.pos, bf16[3,256,768]{2,1,0:T(8,128)(2,1)S(1)} %copy-done.4, bf16[3,512,768]{2,1,0:T(8,128)(2,1)S(1)} %copy-done, bf16[256,768]{1,0:T(8,128)(2,1)S(1)} %copy-done.5, bf16[3,512,768]{2,1,0:T(8,128)(2,1)} %copy-done.1), custom_call_target="tpu_custom_call" | custom-call | flops 905969664 | bytes 5000000 | tf_op jit(solution)/shard_map/weight_terms/pallas_call | solution.py:247
  107.9 5.6 %feature_terms.1 = f32[512,768]{1,0:T(8,128)S(1)} custom-call(bf16[3,512,768]{2,1,0:T(8,128)(2,1)S(1)} %copy-done.2, bf16[3,768,768]{2,1,0:T(8,128)(2,1)} %weight.3, s32[3,1,512]{2,1,0:T(1,128)S(1)} %broadcast_in_dim.6.src), custom_call_target="tpu_custom_call" | custom-call | flops 3019898880 | bytes 8000000 | tf_op jit(solution)/shard_map/feature_terms/pallas_call | solution.py:219
  113.6 2.8 %weight_terms.3 = (bf16[384,768]{1,0:T(8,128)(2,1)S(1)}, f32[384,768]{1,0:T(8,128)S(1)}) custom-call(s32[4]{0:T(128)S(1)} %pad_add_fusion.pos, bf16[3,256,768]{2,1,0:T(8,128)(2,1)S(1)} %copy-done.4, bf16[3,512,768]{2,1,0:T(8,128)(2,1)S(1)} %copy-done, bf16[256,768]{1,0:T(8,128)(2,1)S(1)} %copy-done.5, bf16[3,512,768]{2,1,0:T(8,128)(2,1)} %copy-done.1), custom_call_target="tpu_custom_call" | custom-call | flops 905969664 | bytes 5000000 | tf_op jit(solution)/shard_map/weight_terms/pallas_call | solution.py:247
  121.1 9.4 %collective-permute-done.22 = bf16[384,768]{1,0:T(8,128)(2,1)S(1)} collective-permute-done((bf16[384,768]{1,0:T(8,128)(2,1)S(1)}, bf16[384,768]{1,0:T(8,128)(2,1)S(1)}, u32[]{:S(2)}, u32[]{:S(2)}) %collective-permute-start.22) | collective-permute-done | bytes 589856 | tf_op jit(solution)/shard_map/ppermute | solution.py:48
  130.7 2.6 %collective-permute-start.23 = (bf16[192,768]{1,0:T(8,128)(2,1)S(1)}, bf16[192,768]{1,0:T(8,128)(2,1)S(1)}, u32[]{:S(2)}, u32[]{:S(2)}) collective-permute-start(bf16[192,768]{1,0:T(8,128)(2,1)S(1)} %dynamic-slice_convert_fusion.2), channel_id=1, source_target_pairs={{0,2},{1,5},{2,0},{3,7},{4,6},{5,1},{6,4},{7,3},{8,10},{9,13},{10,... | collective-permute-start | bytes 884744 | tf_op jit(solution)/shard_map/ppermute | solution.py:48
  133.4 1.9 collective-permute-start.46
  135.3 2.0 collective-permute-start.48
  138.0 3.8 %collective-permute-start.47 = (bf16[48,768]{1,0:T(8,128)(2,1)S(1)}, bf16[48,768]{1,0:T(8,128)(2,1)S(1)}, u32[]{:S(2)}, u32[]{:S(2)}) collective-permute-start(bf16[48,768]{1,0:T(8,128)(2,1)S(1)} %get-tuple-element.30), channel_id=1, source_target_pairs={{0,16},{1,17},{2,18},{3,19},{4,20},{5,21},{6,22},{7,23},{8,24},{9,... | collective-permute-start | bytes 221192 | tf_op jit(solution)/shard_map/ppermute | solution.py:48
  141.9 1.7 convert_add_fusion
  143.7 3.9 %collective-permute-start.37 = (bf16[48,768]{1,0:T(8,128)(2,1)S(1)}, bf16[48,768]{1,0:T(8,128)(2,1)S(1)}, u32[]{:S(2)}, u32[]{:S(2)}) collective-permute-start(bf16[48,768]{1,0:T(8,128)(2,1)S(1)} %get-tuple-element.32), channel_id=1, source_target_pairs={{0,24},{1,25},{2,26},{3,27},{4,28},{5,29},{6,30},{7,31},{8,0},{9,1... | collective-permute-start | bytes 221192 | tf_op jit(solution)/shard_map/ppermute | solution.py:48
  147.6 2.1 collective-permute-start.3
  150.4 3.5 %collective-permute-start.26 = (bf16[48,768]{1,0:T(8,128)(2,1)S(1)}, bf16[48,768]{1,0:T(8,128)(2,1)S(1)}, u32[]{:S(2)}, u32[]{:S(2)}) collective-permute-start(bf16[48,768]{1,0:T(8,128)(2,1)S(1)} %get-tuple-element.35), channel_id=1, source_target_pairs={{0,24},{1,25},{2,26},{3,27},{4,28},{5,29},{6,30},{7,31},{8,0},{9,1... | collective-permute-start | bytes 221192 | tf_op jit(solution)/shard_map/ppermute | solution.py:48
  156.1 1.8 collective-permute-start.51
  157.9 2.8 %collective-permute-start.50 = (bf16[48,768]{1,0:T(8,128)(2,1)S(1)}, bf16[48,768]{1,0:T(8,128)(2,1)S(1)}, u32[]{:S(2)}, u32[]{:S(2)}) collective-permute-start(bf16[48,768]{1,0:T(8,128)(2,1)S(1)} %add_convert_fusion.1), channel_id=1, source_target_pairs={{0,16},{1,17},{2,18},{3,19},{4,20},{5,21},{6,22},{7,23},{8,24},{9,... | collective-permute-start | bytes 221192 | tf_op jit(solution)/shard_map/ppermute | solution.py:48
  160.7 2.0 collective-permute-start.49
  162.8 1.9 collective-permute-start.40
  164.7 4.0 %collective-permute-done.50 = bf16[48,768]{1,0:T(8,128)(2,1)S(1)} collective-permute-done((bf16[48,768]{1,0:T(8,128)(2,1)S(1)}, bf16[48,768]{1,0:T(8,128)(2,1)S(1)}, u32[]{:S(2)}, u32[]{:S(2)}) %collective-permute-start.50) | collective-permute-done | bytes 73760 | tf_op jit(solution)/shard_map/ppermute | solution.py:48
  168.7 1.6 collective-permute-start.38
  170.4 2.2 %collective-permute-start.29 = (bf16[48,768]{1,0:T(8,128)(2,1)S(1)}, bf16[48,768]{1,0:T(8,128)(2,1)S(1)}, u32[]{:S(2)}, u32[]{:S(2)}) collective-permute-start(bf16[48,768]{1,0:T(8,128)(2,1)S(1)} %add_convert_fusion.3), channel_id=1, source_target_pairs={{0,24},{1,25},{2,26},{3,27},{4,28},{5,29},{6,30},{7,31},{8,0},{9,1... | collective-permute-start | bytes 221192 | tf_op jit(solution)/shard_map/ppermute | solution.py:48
  172.9 2.0 collective-permute-start.28
  174.8 4.1 %collective-permute-done.39 = bf16[48,768]{1,0:T(8,128)(2,1)S(1)} collective-permute-done((bf16[48,768]{1,0:T(8,128)(2,1)S(1)}, bf16[48,768]{1,0:T(8,128)(2,1)S(1)}, u32[]{:S(2)}, u32[]{:S(2)}) %collective-permute-start.39) | collective-permute-done | bytes 73760 | tf_op jit(solution)/shard_map/ppermute | solution.py:48
  179.2 1.9 collective-permute-start.4
  181.0 3.1 %collective-permute-done.28 = bf16[48,768]{1,0:T(8,128)(2,1)S(1)} collective-permute-done((bf16[48,768]{1,0:T(8,128)(2,1)S(1)}, bf16[48,768]{1,0:T(8,128)(2,1)S(1)}, u32[]{:S(2)}, u32[]{:S(2)}) %collective-permute-start.28) | collective-permute-done | bytes 73760 | tf_op jit(solution)/shard_map/ppermute | solution.py:48
  184.2 1.7 collective-permute-start.6
  188.7 2.4 %collective-permute-done.6 = bf16[128,768]{1,0:T(8,128)(2,1)S(1)} collective-permute-done((bf16[128,768]{1,0:T(8,128)(2,1)S(1)}, bf16[128,768]{1,0:T(8,128)(2,1)S(1)}, u32[]{:S(2)}, u32[]{:S(2)}) %collective-permute-start.6) | collective-permute-done | bytes 196640 | tf_op jit(solution)/shard_map/ppermute | solution.py:48
  191.4 4.1 %collective-permute-done.5 = bf16[128,768]{1,0:T(8,128)(2,1)S(1)} collective-permute-done((bf16[128,768]{1,0:T(8,128)(2,1)S(1)}, bf16[128,768]{1,0:T(8,128)(2,1)S(1)}, u32[]{:S(2)}, u32[]{:S(2)}) %collective-permute-start.5) | collective-permute-done | bytes 196640 | tf_op jit(solution)/shard_map/ppermute | solution.py:48
  196.1 1.7 collective-permute-start.42
  198.2 1.8 collective-permute-done.30.refs_1_
  199.9 2.0 collective-permute-start.32
  203.3 2.1 assemble.3.refs_4_
  205.4 6.3 %collective-permute-done.43.refs_3_ = bf16[192,768]{1,0:T(8,128)(2,1)S(1)} collective-permute-done((bf16[192,768]{1,0:T(8,128)(2,1)S(1)}, bf16[192,768]{1,0:T(8,128)(2,1)S(1)}, u32[]{:S(2)}, u32[]{:S(2)}) %collective-permute-start.43) | collective-permute-done | bytes 294944 | tf_op jit(solution)/shard_map/ppermute | solution.py:48
  211.7 2.1 assemble.4.refs_4_
  214.9 2.1 assemble.5
  (167 shorter events, 49.5 us)
Async XLA Ops:
  1.7 33.3 %collective-permute-start.19 = (bf16[128,768]{1,0:T(8,128)(2,1)S(1)}, bf16[128,768]{1,0:T(8,128)(2,1)S(1)}, u32[]{:S(2)}, u32[]{:S(2)}) collective-permute-start(bf16[128,768]{1,0:T(8,128)(2,1)S(1)} %get-tuple-element.38.rest_0_), channel_id=1, source_target_pairs={{0,2},{1,5},{2,0},{3,7},{4,6},{5,1},{6,4},{7,3},{8,10},{9,13},{10,... | collective-permute-start | bytes 589832 | tf_op jit(solution)/shard_map/ppermute | solution.py:48
  4.7 30.8 %collective-permute-start.18 = (bf16[128,768]{1,0:T(8,128)(2,1)S(1)}, bf16[128,768]{1,0:T(8,128)(2,1)S(1)}, u32[]{:S(2)}, u32[]{:S(2)}) collective-permute-start(bf16[128,768]{1,0:T(8,128)(2,1)S(1)} %get-tuple-element.38.rest_0_), channel_id=1, source_target_pairs={{0,4},{1,3},{2,6},{3,1},{4,0},{5,7},{6,2},{7,5},{8,12},{9,11},{10,... | collective-permute-start | bytes 589832 | tf_op jit(solution)/shard_map/ppermute | solution.py:48
  6.2 20.8 %collective-permute-start.10 = (bf16[128,768]{1,0:T(8,128)(2,1)S(1)}, bf16[128,768]{1,0:T(8,128)(2,1)}, u32[]{:S(2)}, u32[]{:S(2)}) collective-permute-start(bf16[128,768]{1,0:T(8,128)(2,1)S(1)} %get-tuple-element.38.rest_0_), channel_id=1, source_target_pairs={{0,24},{1,25},{2,26},{3,27},{4,28},{5,29},{6,30},{7,31},{8,0},{9,1... | collective-permute-start | bytes 589832 | tf_op jit(solution)/shard_map/ppermute | solution.py:48
  9.8 16.2 %collective-permute-start.9 = (bf16[128,768]{1,0:T(8,128)(2,1)S(1)}, bf16[128,768]{1,0:T(8,128)(2,1)}, u32[]{:S(2)}, u32[]{:S(2)}) collective-permute-start(bf16[128,768]{1,0:T(8,128)(2,1)S(1)} %get-tuple-element.38.rest_0_), channel_id=1, source_target_pairs={{0,16},{1,17},{2,18},{3,19},{4,20},{5,21},{6,22},{7,23},{8,24},{9,... | collective-permute-start | bytes 589832 | tf_op jit(solution)/shard_map/ppermute | solution.py:48
  9.8 14.5 %collective-permute-start.8 = (bf16[128,768]{1,0:T(8,128)(2,1)S(1)}, bf16[128,768]{1,0:T(8,128)(2,1)}, u32[]{:S(2)}, u32[]{:S(2)}) collective-permute-start(bf16[128,768]{1,0:T(8,128)(2,1)S(1)} %get-tuple-element.38.rest_0_), channel_id=1, source_target_pairs={{0,8},{1,9},{2,10},{3,11},{4,12},{5,13},{6,14},{7,15},{8,16},{9,17... | collective-permute-start | bytes 589832 | tf_op jit(solution)/shard_map/ppermute | solution.py:48
  28.0 19.1 %collective-permute-start.11 = (bf16[384,768]{1,0:T(8,128)(2,1)S(1)}, bf16[384,768]{1,0:T(8,128)(2,1)}, u32[]{:S(2)}, u32[]{:S(2)}) collective-permute-start(bf16[384,768]{1,0:T(8,128)(2,1)S(1)} %constant_dynamic-update-slice_fusion.rest_0_), channel_id=1, source_target_pairs={{0,2},{1,5},{2,0},{3,7},{4,6},{5,1},{6,4},{7,3},{8,10},{9,13},{10,... | collective-permute-start | bytes 1769480 | tf_op jit(solution)/shard_map/ppermute | solution.py:48
  34.5 45.9 %collective-permute-start.1 = (bf16[1024,768]{1,0:T(8,128)(2,1)}, bf16[1024,768]{1,0:T(8,128)(2,1)S(1)}, u32[]{:S(2)}, u32[]{:S(2)}) collective-permute-start(bf16[1024,768]{1,0:T(8,128)(2,1)} %partial_rows.6), channel_id=1, source_target_pairs={{0,1},{1,0},{2,3},{3,2},{4,5},{5,4},{6,7},{7,6},{8,9},{9,8},{10,11... | collective-permute-start | bytes 4718600 | tf_op jit(solution)/shard_map/ppermute | solution.py:48
  34.5 18.6 %collective-permute-start.17 = (bf16[384,768]{1,0:T(8,128)(2,1)S(1)}, bf16[384,768]{1,0:T(8,128)(2,1)S(1)}, u32[]{:S(2)}, u32[]{:S(2)}) collective-permute-start(bf16[384,768]{1,0:T(8,128)(2,1)S(1)} %constant_dynamic-update-slice_fusion.rest_0_), channel_id=1, source_target_pairs={{0,1},{1,0},{2,3},{3,2},{4,5},{5,4},{6,7},{7,6},{8,9},{9,8},{10,11... | collective-permute-start | bytes 1769480 | tf_op jit(solution)/shard_map/ppermute | solution.py:48
  35.0 20.1 %collective-permute-start.14 = (bf16[384,768]{1,0:T(8,128)(2,1)S(1)}, bf16[384,768]{1,0:T(8,128)(2,1)}, u32[]{:S(2)}, u32[]{:S(2)}) collective-permute-start(bf16[384,768]{1,0:T(8,128)(2,1)S(1)} %constant_dynamic-update-slice_fusion.rest_0_), channel_id=1, source_target_pairs={{0,4},{1,3},{2,6},{3,1},{4,0},{5,7},{6,2},{7,5},{8,12},{9,11},{10,... | collective-permute-start | bytes 1769480 | tf_op jit(solution)/shard_map/ppermute | solution.py:48
  36.2 10.8 %collective-permute-start.20 = (bf16[128,768]{1,0:T(8,128)(2,1)S(1)}, bf16[128,768]{1,0:T(8,128)(2,1)S(1)}, u32[]{:S(2)}, u32[]{:S(2)}) collective-permute-start(bf16[128,768]{1,0:T(8,128)(2,1)S(1)} %collective-permute-done.19), channel_id=1, source_target_pairs={{0,4},{1,3},{2,6},{3,1},{4,0},{5,7},{6,2},{7,5},{8,12},{9,11},{10,... | collective-permute-start | bytes 589832 | tf_op jit(solution)/shard_map/ppermute | solution.py:48
  47.0 8.1 %collective-permute-start.21 = (bf16[384,768]{1,0:T(8,128)(2,1)S(1)}, bf16[384,768]{1,0:T(8,128)(2,1)S(1)}, u32[]{:S(2)}, u32[]{:S(2)}) collective-permute-start(bf16[384,768]{1,0:T(8,128)(2,1)S(1)} %constant_dynamic-update-slice_fusion.3.rest_2_), channel_id=1, source_target_pairs={{0,1},{1,0},{2,3},{3,2},{4,5},{5,4},{6,7},{7,6},{8,9},{9,8},{10,11... | collective-permute-start | bytes 1769480 | tf_op jit(solution)/shard_map/ppermute | solution.py:48
  47.1 17.7 %collective-permute-start.12 = (bf16[384,768]{1,0:T(8,128)(2,1)}, bf16[384,768]{1,0:T(8,128)(2,1)}, u32[]{:S(2)}, u32[]{:S(2)}) collective-permute-start(bf16[384,768]{1,0:T(8,128)(2,1)} %collective-permute-done.11.rest_1_), channel_id=1, source_target_pairs={{0,4},{1,3},{2,6},{3,1},{4,0},{5,7},{6,2},{7,5},{8,12},{9,11},{10,... | collective-permute-start | bytes 1769480 | tf_op jit(solution)/shard_map/ppermute | solution.py:48
  53.9 44.1 %collective-permute-start = (bf16[1024,768]{1,0:T(8,128)(2,1)}, bf16[1024,768]{1,0:T(8,128)(2,1)}, u32[]{:S(2)}, u32[]{:S(2)}) collective-permute-start(bf16[1024,768]{1,0:T(8,128)(2,1)} %partial_rows.4), channel_id=1, source_target_pairs={{0,1},{1,0},{2,3},{3,2},{4,5},{5,4},{6,7},{7,6},{8,9},{9,8},{10,11... | collective-permute-start | bytes 4718600 | tf_op jit(solution)/shard_map/ppermute | solution.py:48
  55.1 16.0 %collective-permute-start.15 = (bf16[384,768]{1,0:T(8,128)(2,1)}, bf16[384,768]{1,0:T(8,128)(2,1)}, u32[]{:S(2)}, u32[]{:S(2)}) collective-permute-start(bf16[384,768]{1,0:T(8,128)(2,1)} %collective-permute-done.14.rest_0_), channel_id=1, source_target_pairs={{0,1},{1,0},{2,3},{3,2},{4,5},{5,4},{6,7},{7,6},{8,9},{9,8},{10,11... | collective-permute-start | bytes 1769480 | tf_op jit(solution)/shard_map/ppermute | solution.py:48
  56.0 15.1 %collective-permute-start.16 = (bf16[384,768]{1,0:T(8,128)(2,1)}, bf16[384,768]{1,0:T(8,128)(2,1)}, u32[]{:S(2)}, u32[]{:S(2)}) collective-permute-start(bf16[384,768]{1,0:T(8,128)(2,1)} %collective-permute-done.11.rest_1_), channel_id=1, source_target_pairs={{0,1},{1,0},{2,3},{3,2},{4,5},{5,4},{6,7},{7,6},{8,9},{9,8},{10,11... | collective-permute-start | bytes 1769480 | tf_op jit(solution)/shard_map/ppermute | solution.py:48
  64.8 22.4 %collective-permute-start.13 = (bf16[384,768]{1,0:T(8,128)(2,1)}, bf16[384,768]{1,0:T(8,128)(2,1)S(1)}, u32[]{:S(2)}, u32[]{:S(2)}) collective-permute-start(bf16[384,768]{1,0:T(8,128)(2,1)} %collective-permute-done.12.rest_0_), channel_id=1, source_target_pairs={{0,1},{1,0},{2,3},{3,2},{4,5},{5,4},{6,7},{7,6},{8,9},{9,8},{10,11... | collective-permute-start | bytes 1769480 | tf_op jit(solution)/shard_map/ppermute | solution.py:48
  86.3 55.5 %collective-permute-start.2 = (bf16[1024,768]{1,0:T(8,128)(2,1)}, bf16[1024,768]{1,0:T(8,128)(2,1)}, u32[]{:S(2)}, u32[]{:S(2)}) collective-permute-start(bf16[1024,768]{1,0:T(8,128)(2,1)} %partial_rows.7), channel_id=1, source_target_pairs={{0,4},{1,3},{2,6},{3,1},{4,0},{5,7},{6,2},{7,5},{8,12},{9,11},{10,... | collective-permute-start | bytes 4718600 | tf_op jit(solution)/shard_map/ppermute | solution.py:48
  96.9 20.7 %collective-permute-start.44 = (bf16[384,768]{1,0:T(8,128)(2,1)S(1)}, bf16[384,768]{1,0:T(8,128)(2,1)}, u32[]{:S(2)}, u32[]{:S(2)}) collective-permute-start(bf16[384,768]{1,0:T(8,128)(2,1)S(1)} %get-tuple-element.22), channel_id=1, source_target_pairs={{0,4},{1,3},{2,6},{3,1},{4,0},{5,7},{6,2},{7,5},{8,12},{9,11},{10,... | collective-permute-start | bytes 1769480 | tf_op jit(solution)/shard_map/ppermute | solution.py:48
  106.9 12.8 %collective-permute-start.33 = (bf16[384,768]{1,0:T(8,128)(2,1)S(1)}, bf16[384,768]{1,0:T(8,128)(2,1)S(1)}, u32[]{:S(2)}, u32[]{:S(2)}) collective-permute-start(bf16[384,768]{1,0:T(8,128)(2,1)S(1)} %get-tuple-element.20), channel_id=1, source_target_pairs={{0,4},{1,3},{2,6},{3,1},{4,0},{5,7},{6,2},{7,5},{8,12},{9,11},{10,... | collective-permute-start | bytes 1769480 | tf_op jit(solution)/shard_map/ppermute | solution.py:48
  113.5 86.5 %collective-permute-start.55 = (f32[512,768]{1,0:T(8,128)S(1)}, f32[512,768]{1,0:T(8,128)S(1)}, u32[]{:S(2)}, u32[]{:S(2)}) collective-permute-start(f32[512,768]{1,0:T(8,128)S(1)} %feature_terms.1), channel_id=1, source_target_pairs={{0,1},{1,0},{2,3},{3,2},{4,5},{5,4},{6,7},{7,6},{8,9},{9,8},{10,11... | collective-permute-start | bytes 4718600 | tf_op jit(solution)/shard_map/ppermute | solution.py:48
  116.4 14.2 %collective-permute-start.22 = (bf16[384,768]{1,0:T(8,128)(2,1)S(1)}, bf16[384,768]{1,0:T(8,128)(2,1)S(1)}, u32[]{:S(2)}, u32[]{:S(2)}) collective-permute-start(bf16[384,768]{1,0:T(8,128)(2,1)S(1)} %get-tuple-element.18), channel_id=1, source_target_pairs={{0,4},{1,3},{2,6},{3,1},{4,0},{5,7},{6,2},{7,5},{8,12},{9,11},{10,... | collective-permute-start | bytes 1769480 | tf_op jit(solution)/shard_map/ppermute | solution.py:48
  118.8 14.4 %collective-permute-start.45 = (bf16[192,768]{1,0:T(8,128)(2,1)S(1)}, bf16[192,768]{1,0:T(8,128)(2,1)S(1)}, u32[]{:S(2)}, u32[]{:S(2)}) collective-permute-start(bf16[192,768]{1,0:T(8,128)(2,1)S(1)} %dynamic-slice_convert_fusion), channel_id=1, source_target_pairs={{0,2},{1,5},{2,0},{3,7},{4,6},{5,1},{6,4},{7,3},{8,10},{9,13},{10,... | collective-permute-start | bytes 884744 | tf_op jit(solution)/shard_map/ppermute | solution.py:48
  119.9 15.4 %collective-permute-start.34 = (bf16[192,768]{1,0:T(8,128)(2,1)S(1)}, bf16[192,768]{1,0:T(8,128)(2,1)S(1)}, u32[]{:S(2)}, u32[]{:S(2)}) collective-permute-start(bf16[192,768]{1,0:T(8,128)(2,1)S(1)} %dynamic-slice_convert_fusion.1), channel_id=1, source_target_pairs={{0,2},{1,5},{2,0},{3,7},{4,6},{5,1},{6,4},{7,3},{8,10},{9,13},{10,... | collective-permute-start | bytes 884744 | tf_op jit(solution)/shard_map/ppermute | solution.py:48
  130.7 7.3 %collective-permute-start.23 = (bf16[192,768]{1,0:T(8,128)(2,1)S(1)}, bf16[192,768]{1,0:T(8,128)(2,1)S(1)}, u32[]{:S(2)}, u32[]{:S(2)}) collective-permute-start(bf16[192,768]{1,0:T(8,128)(2,1)S(1)} %dynamic-slice_convert_fusion.2), channel_id=1, source_target_pairs={{0,2},{1,5},{2,0},{3,7},{4,6},{5,1},{6,4},{7,3},{8,10},{9,13},{10,... | collective-permute-start | bytes 884744 | tf_op jit(solution)/shard_map/ppermute | solution.py:48
  133.4 10.4 %collective-permute-start.46 = (bf16[48,768]{1,0:T(8,128)(2,1)S(1)}, bf16[48,768]{1,0:T(8,128)(2,1)S(1)}, u32[]{:S(2)}, u32[]{:S(2)}) collective-permute-start(bf16[48,768]{1,0:T(8,128)(2,1)S(1)} %get-tuple-element.28), channel_id=1, source_target_pairs={{0,8},{1,9},{2,10},{3,11},{4,12},{5,13},{6,14},{7,15},{8,16},{9,17... | collective-permute-start | bytes 221192 | tf_op jit(solution)/shard_map/ppermute | solution.py:48
  135.3 12.3 %collective-permute-start.48 = (bf16[48,768]{1,0:T(8,128)(2,1)S(1)}, bf16[48,768]{1,0:T(8,128)(2,1)S(1)}, u32[]{:S(2)}, u32[]{:S(2)}) collective-permute-start(bf16[48,768]{1,0:T(8,128)(2,1)S(1)} %get-tuple-element.29), channel_id=1, source_target_pairs={{0,24},{1,25},{2,26},{3,27},{4,28},{5,29},{6,30},{7,31},{8,0},{9,1... | collective-permute-start | bytes 221192 | tf_op jit(solution)/shard_map/ppermute | solution.py:48
  138.0 9.6 %collective-permute-start.47 = (bf16[48,768]{1,0:T(8,128)(2,1)S(1)}, bf16[48,768]{1,0:T(8,128)(2,1)S(1)}, u32[]{:S(2)}, u32[]{:S(2)}) collective-permute-start(bf16[48,768]{1,0:T(8,128)(2,1)S(1)} %get-tuple-element.30), channel_id=1, source_target_pairs={{0,16},{1,17},{2,18},{3,19},{4,20},{5,21},{6,22},{7,23},{8,24},{9,... | collective-permute-start | bytes 221192 | tf_op jit(solution)/shard_map/ppermute | solution.py:48
  141.8 7.9 %collective-permute-start.35 = (bf16[48,768]{1,0:T(8,128)(2,1)S(1)}, bf16[48,768]{1,0:T(8,128)(2,1)S(1)}, u32[]{:S(2)}, u32[]{:S(2)}) collective-permute-start(bf16[48,768]{1,0:T(8,128)(2,1)S(1)} %get-tuple-element.31), channel_id=1, source_target_pairs={{0,8},{1,9},{2,10},{3,11},{4,12},{5,13},{6,14},{7,15},{8,16},{9,17... | collective-permute-start | bytes 221192 | tf_op jit(solution)/shard_map/ppermute | solution.py:48
  147.6 22.8 %collective-permute-start.3 = (bf16[512,768]{1,0:T(8,128)(2,1)S(1)}, bf16[512,768]{1,0:T(8,128)(2,1)S(1)}, u32[]{:S(2)}, u32[]{:S(2)}) collective-permute-start(bf16[512,768]{1,0:T(8,128)(2,1)S(1)} %slice.43), channel_id=1, source_target_pairs={{0,2},{1,5},{2,0},{3,7},{4,6},{5,1},{6,4},{7,3},{8,10},{9,13},{10,... | collective-permute-start | bytes 2359304 | tf_op jit(solution)/shard_map/ppermute | solution.py:48
  150.4 7.5 %collective-permute-start.26 = (bf16[48,768]{1,0:T(8,128)(2,1)S(1)}, bf16[48,768]{1,0:T(8,128)(2,1)S(1)}, u32[]{:S(2)}, u32[]{:S(2)}) collective-permute-start(bf16[48,768]{1,0:T(8,128)(2,1)S(1)} %get-tuple-element.35), channel_id=1, source_target_pairs={{0,24},{1,25},{2,26},{3,27},{4,28},{5,29},{6,30},{7,31},{8,0},{9,1... | collective-permute-start | bytes 221192 | tf_op jit(solution)/shard_map/ppermute | solution.py:48
  157.9 10.8 %collective-permute-start.50 = (bf16[48,768]{1,0:T(8,128)(2,1)S(1)}, bf16[48,768]{1,0:T(8,128)(2,1)S(1)}, u32[]{:S(2)}, u32[]{:S(2)}) collective-permute-start(bf16[48,768]{1,0:T(8,128)(2,1)S(1)} %add_convert_fusion.1), channel_id=1, source_target_pairs={{0,16},{1,17},{2,18},{3,19},{4,20},{5,21},{6,22},{7,23},{8,24},{9,... | collective-permute-start | bytes 221192 | tf_op jit(solution)/shard_map/ppermute | solution.py:48
  160.7 8.0 %collective-permute-start.49 = (bf16[48,768]{1,0:T(8,128)(2,1)S(1)}, bf16[48,768]{1,0:T(8,128)(2,1)S(1)}, u32[]{:S(2)}, u32[]{:S(2)}) collective-permute-start(bf16[48,768]{1,0:T(8,128)(2,1)S(1)} %add_convert_fusion.1), channel_id=1, source_target_pairs={{0,8},{1,9},{2,10},{3,11},{4,12},{5,13},{6,14},{7,15},{8,16},{9,17... | collective-permute-start | bytes 221192 | tf_op jit(solution)/shard_map/ppermute | solution.py:48
  162.8 10.1 %collective-permute-start.40 = (bf16[48,768]{1,0:T(8,128)(2,1)S(1)}, bf16[48,768]{1,0:T(8,128)(2,1)S(1)}, u32[]{:S(2)}, u32[]{:S(2)}) collective-permute-start(bf16[48,768]{1,0:T(8,128)(2,1)S(1)} %add_convert_fusion.2), channel_id=1, source_target_pairs={{0,24},{1,25},{2,26},{3,27},{4,28},{5,29},{6,30},{7,31},{8,0},{9,1... | collective-permute-start | bytes 221192 | tf_op jit(solution)/shard_map/ppermute | solution.py:48
  168.7 10.2 %collective-permute-start.39 = (bf16[48,768]{1,0:T(8,128)(2,1)S(1)}, bf16[48,768]{1,0:T(8,128)(2,1)S(1)}, u32[]{:S(2)}, u32[]{:S(2)}) collective-permute-start(bf16[48,768]{1,0:T(8,128)(2,1)S(1)} %add_convert_fusion.2), channel_id=1, source_target_pairs={{0,16},{1,17},{2,18},{3,19},{4,20},{5,21},{6,22},{7,23},{8,24},{9,... | collective-permute-start | bytes 221192 | tf_op jit(solution)/shard_map/ppermute | solution.py:48
  168.7 10.2 %collective-permute-start.38 = (bf16[48,768]{1,0:T(8,128)(2,1)S(1)}, bf16[48,768]{1,0:T(8,128)(2,1)S(1)}, u32[]{:S(2)}, u32[]{:S(2)}) collective-permute-start(bf16[48,768]{1,0:T(8,128)(2,1)S(1)} %add_convert_fusion.2), channel_id=1, source_target_pairs={{0,8},{1,9},{2,10},{3,11},{4,12},{5,13},{6,14},{7,15},{8,16},{9,17... | collective-permute-start | bytes 221192 | tf_op jit(solution)/shard_map/ppermute | solution.py:48
  170.4 8.8 %collective-permute-start.29 = (bf16[48,768]{1,0:T(8,128)(2,1)S(1)}, bf16[48,768]{1,0:T(8,128)(2,1)S(1)}, u32[]{:S(2)}, u32[]{:S(2)}) collective-permute-start(bf16[48,768]{1,0:T(8,128)(2,1)S(1)} %add_convert_fusion.3), channel_id=1, source_target_pairs={{0,24},{1,25},{2,26},{3,27},{4,28},{5,29},{6,30},{7,31},{8,0},{9,1... | collective-permute-start | bytes 221192 | tf_op jit(solution)/shard_map/ppermute | solution.py:48
  172.9 11.3 %collective-permute-start.28 = (bf16[48,768]{1,0:T(8,128)(2,1)S(1)}, bf16[48,768]{1,0:T(8,128)(2,1)S(1)}, u32[]{:S(2)}, u32[]{:S(2)}) collective-permute-start(bf16[48,768]{1,0:T(8,128)(2,1)S(1)} %add_convert_fusion.3), channel_id=1, source_target_pairs={{0,16},{1,17},{2,18},{3,19},{4,20},{5,21},{6,22},{7,23},{8,24},{9,... | collective-permute-start | bytes 221192 | tf_op jit(solution)/shard_map/ppermute | solution.py:48
  178.9 7.7 %collective-permute-start.52 = (bf16[192,768]{1,0:T(8,128)(2,1)S(1)}, bf16[192,768]{1,0:T(8,128)(2,1)S(1)}, u32[]{:S(2)}, u32[]{:S(2)}) collective-permute-start(bf16[192,768]{1,0:T(8,128)(2,1)S(1)} %pad_maximum_fusion.2.refs_0_), channel_id=1, source_target_pairs={{0,2},{1,5},{2,0},{3,7},{4,6},{5,1},{6,4},{7,3},{8,10},{9,13},{10,... | collective-permute-start | bytes 884744 | tf_op jit(solution)/shard_map/ppermute | solution.py:48
  179.2 8.1 %collective-permute-start.4 = (bf16[128,768]{1,0:T(8,128)(2,1)S(1)}, bf16[128,768]{1,0:T(8,128)(2,1)S(1)}, u32[]{:S(2)}, u32[]{:S(2)}) collective-permute-start(bf16[128,768]{1,0:T(8,128)(2,1)S(1)} %get-tuple-element.25), channel_id=1, source_target_pairs={{0,8},{1,9},{2,10},{3,11},{4,12},{5,13},{6,14},{7,15},{8,16},{9,17... | collective-permute-start | bytes 589832 | tf_op jit(solution)/shard_map/ppermute | solution.py:48
  185.9 9.7 %collective-permute-start.5 = (bf16[128,768]{1,0:T(8,128)(2,1)S(1)}, bf16[128,768]{1,0:T(8,128)(2,1)S(1)}, u32[]{:S(2)}, u32[]{:S(2)}) collective-permute-start(bf16[128,768]{1,0:T(8,128)(2,1)S(1)} %get-tuple-element.27), channel_id=1, source_target_pairs={{0,16},{1,17},{2,18},{3,19},{4,20},{5,21},{6,22},{7,23},{8,24},{9,... | collective-permute-start | bytes 589832 | tf_op jit(solution)/shard_map/ppermute | solution.py:48
  186.6 9.4 %collective-permute-start.53 = (bf16[192,768]{1,0:T(8,128)(2,1)S(1)}, bf16[192,768]{1,0:T(8,128)(2,1)S(1)}, u32[]{:S(2)}, u32[]{:S(2)}) collective-permute-start(bf16[192,768]{1,0:T(8,128)(2,1)S(1)} %pad_maximum_fusion.2.refs_0_), channel_id=1, source_target_pairs={{0,4},{1,3},{2,6},{3,1},{4,0},{5,7},{6,2},{7,5},{8,12},{9,11},{10,... | collective-permute-start | bytes 884744 | tf_op jit(solution)/shard_map/ppermute | solution.py:48
  187.2 10.5 %collective-permute-start.41 = (bf16[192,768]{1,0:T(8,128)(2,1)S(1)}, bf16[192,768]{1,0:T(8,128)(2,1)S(1)}, u32[]{:S(2)}, u32[]{:S(2)}) collective-permute-start(bf16[192,768]{1,0:T(8,128)(2,1)S(1)} %pad_maximum_fusion.1.refs_0_), channel_id=1, source_target_pairs={{0,2},{1,5},{2,0},{3,7},{4,6},{5,1},{6,4},{7,3},{8,10},{9,13},{10,... | collective-permute-start | bytes 884744 | tf_op jit(solution)/shard_map/ppermute | solution.py:48
  191.1 8.9 %collective-permute-start.30 = (bf16[192,768]{1,0:T(8,128)(2,1)S(1)}, bf16[192,768]{1,0:T(8,128)(2,1)S(1)}, u32[]{:S(2)}, u32[]{:S(2)}) collective-permute-start(bf16[192,768]{1,0:T(8,128)(2,1)S(1)} %pad_maximum_fusion.refs_0_), channel_id=1, source_target_pairs={{0,2},{1,5},{2,0},{3,7},{4,6},{5,1},{6,4},{7,3},{8,10},{9,13},{10,... | collective-permute-start | bytes 884744 | tf_op jit(solution)/shard_map/ppermute | solution.py:48
  196.1 9.3 %collective-permute-start.42 = (bf16[192,768]{1,0:T(8,128)(2,1)S(1)}, bf16[192,768]{1,0:T(8,128)(2,1)S(1)}, u32[]{:S(2)}, u32[]{:S(2)}) collective-permute-start(bf16[192,768]{1,0:T(8,128)(2,1)S(1)} %pad_maximum_fusion.1.refs_0_), channel_id=1, source_target_pairs={{0,4},{1,3},{2,6},{3,1},{4,0},{5,7},{6,2},{7,5},{8,12},{9,11},{10,... | collective-permute-start | bytes 884744 | tf_op jit(solution)/shard_map/ppermute | solution.py:48
  197.7 16.1 %collective-permute-start.31 = (bf16[192,768]{1,0:T(8,128)(2,1)S(1)}, bf16[192,768]{1,0:T(8,128)(2,1)S(1)}, u32[]{:S(2)}, u32[]{:S(2)}) collective-permute-start(bf16[192,768]{1,0:T(8,128)(2,1)S(1)} %pad_maximum_fusion.refs_0_), channel_id=1, source_target_pairs={{0,4},{1,3},{2,6},{3,1},{4,0},{5,7},{6,2},{7,5},{8,12},{9,11},{10,... | collective-permute-start | bytes 884744 | tf_op jit(solution)/shard_map/ppermute | solution.py:48
  199.9 11.8 %collective-permute-start.43 = (bf16[192,768]{1,0:T(8,128)(2,1)S(1)}, bf16[192,768]{1,0:T(8,128)(2,1)S(1)}, u32[]{:S(2)}, u32[]{:S(2)}) collective-permute-start(bf16[192,768]{1,0:T(8,128)(2,1)S(1)} %collective-permute-done.41.refs_1_), channel_id=1, source_target_pairs={{0,4},{1,3},{2,6},{3,1},{4,0},{5,7},{6,2},{7,5},{8,12},{9,11},{10,... | collective-permute-start | bytes 884744 | tf_op jit(solution)/shard_map/ppermute | solution.py:48
  199.9 15.0 %collective-permute-start.32 = (bf16[192,768]{1,0:T(8,128)(2,1)S(1)}, bf16[192,768]{1,0:T(8,128)(2,1)S(1)}, u32[]{:S(2)}, u32[]{:S(2)}) collective-permute-start(bf16[192,768]{1,0:T(8,128)(2,1)S(1)} %collective-permute-done.30.refs_1_), channel_id=1, source_target_pairs={{0,4},{1,3},{2,6},{3,1},{4,0},{5,7},{6,2},{7,5},{8,12},{9,11},{10,... | collective-permute-start | bytes 884744 | tf_op jit(solution)/shard_map/ppermute | solution.py:48
  202.3 14.8 %collective-permute-start.7 = (bf16[128,768]{1,0:T(8,128)(2,1)S(1)}, bf16[128,768]{1,0:T(8,128)(2,1)S(1)}, u32[]{:S(2)}, u32[]{:S(2)}) collective-permute-start(bf16[128,768]{1,0:T(8,128)(2,1)S(1)} %fusion.2), channel_id=1, source_target_pairs={{0,1},{1,0},{2,3},{3,2},{4,5},{5,4},{6,7},{7,6},{8,9},{9,8},{10,11... | collective-permute-start | bytes 589832 | tf_op jit(solution)/shard_map/ppermute | solution.py:48
  (33 other events, 134.4 us)

commit v2 on v0

v2 whole, which is shorter than its diff:
```python
import functools

import jax
import jax.numpy as jnp
from jax import lax
from jax.experimental import pallas as pl
from jax.experimental.pallas import tpu as pltpu
from jax.sharding import PartitionSpec as P

BF = jnp.bfloat16
F32 = jnp.float32
AXES = ("node", "rel")
DEPTH, SIDE = 4, 2
CHUNKS = 2
ORDER = (
    (0, 0),
    ("back", 0),
    (1, 0),
    (0, 1),
    ("rows", -1),
    (0, 2),
    (1, 1),
    (0, 3),
    (1, 2),
    (0, 4),
    (1, 3),
    ("rows", 0),
    (0, 5),
    (1, 4),
    ("rows", 1),
    (0, 6),
    (1, 5),
    ("rows", 2),
    (1, 6),
    (0, 7),
    ("rows", 3),
    ("back", 1),
    ("rows", 4),
    (1, 7),
)
NODES_HERE = DEPTH * SIDE * SIDE


def dot(a, b, dims=((1,), (0,))):
    return lax.dot_general(a, b, (dims, ((), ())), preferred_element_type=F32)


def call(name, kernel, pos, ins, outs, grid=(1,), after=(), alias=None, limit=24):
    def spec(block, index):
        if block is None:
            return pl.BlockSpec(memory_space=pl.ANY)
        if index is None:
            return pl.BlockSpec(block, lambda *_: (0,) * len(block))
        return pl.BlockSpec(block, index)

    many = len(ins)

    def run(pos_ref, *refs):
        kernel(pos_ref, *refs[:many], *refs[many + len(after) :])

    return pl.pallas_call(
        run,
        grid_spec=pltpu.PrefetchScalarGridSpec(
            num_scalar_prefetch=1,
            grid=grid,
            in_specs=[spec(block, index) for _, block, index in ins]
            + [pl.BlockSpec(memory_space=pl.ANY)] * len(after),
            out_specs=[spec(block, index) for _, _, block, index in outs],
        ),
        out_shape=[jax.ShapeDtypeStruct(shape, dtype) for shape, dtype, _, _ in outs],
        input_output_aliases=alias or {},
        compiler_params=pltpu.CompilerParams(
            dimension_semantics=("arbitrary",) * len(grid), vmem_limit_bytes=limit * 1024 * 1024
        ),
        cost_estimate=pl.CostEstimate(flops=1000, bytes_accessed=1000, transcendentals=0),
        name=name,
    )(pos, *[array for array, _, _ in ins], *after)


def full(array):
    return (array, array.shape, None)


def out(shape, dtype):
    return (shape, dtype, shape, None)


def gate(pos, arrays, after):
    return call(
        "gate",
        lambda *_: None,
        pos,
        [(array, None, None) for array in arrays],
        [(array.shape, array.dtype, None, None) for array in arrays],
        after=after,
        alias={i + 1: i for i in range(len(arrays))},
        limit=24,
    )


def pairs(move):
    listed = []
    for node in range(NODES_HERE):
        for core in range(2):
            z, y, x = node // 4, node // 2 % 2, node % 2
            tz, ty, tx, tc = move(z, y, x, core)
            listed.append((node * 2 + core, (tz * 4 + ty * 2 + tx) * 2 + tc))
    return listed


FIRST = pairs(lambda z, y, x, c: (z, y ^ (1 - c), x ^ c, c))
SECOND = pairs(lambda z, y, x, c: (z, y ^ c, x ^ (1 - c), c))
ALONG = [pairs(lambda z, y, x, c, k=k: (z ^ k, y, x, c)) for k in range(DEPTH)]
LINE = (0, 2, 1, 3)
CORES = pairs(lambda z, y, x, c: (z, y, x, 1 - c))


def hop(array, table):
    return lax.ppermute(array, AXES, table)


def owner_of(pos_ref, core, first, second, depth):
    y = pos_ref[1] ^ jnp.where(core == 0, first, second)
    x = pos_ref[2] ^ jnp.where(core == 0, second, first)
    return (pos_ref[0] ^ depth) * 4 + y * 2 + x


def by_rel(array):
    return (array, (1,) + array.shape[1:], lambda r, pos: (r, 0, 0))


def out_by_rel(groups, rows, width, dtype):
    return ((groups, rows, width), dtype, (1, rows, width), lambda r, pos: (r, 0, 0))


def split_kernel(pos, cot, mine):
    half = mine.shape[0]
    mine[...] = cot[pl.ds(pl.multiple_of(pos[3] * half, half), half), :]


def split(pos, cot):
    shape = (cot.shape[0] // 2, cot.shape[1])
    return call("split", split_kernel, pos, [full(cot)], [out(shape, BF)], limit=24)[0]


def join_kernel(pos, *refs):
    start = 0
    for ref in refs[:-1]:
        refs[-1][start : start + ref.shape[0], :] = ref[...]
        start += ref.shape[0]


def join(pos, pieces, after=()):
    shape = (sum(piece.shape[0] for piece in pieces), pieces[0].shape[1])
    return call(
        "join", join_kernel, pos, [full(p) for p in pieces], [out(shape, BF)], after=after, limit=8
    )[0]


def one_hot(values, places):
    return (values == places).astype(F32).astype(BF)


def partial_step(pos, core, first, second, batch, dst, sent, local):
    half = batch // 2
    rows = lax.broadcasted_iota(jnp.int32, (half, dst.shape[1]), 0)
    hot = []
    for depth in LINE:
        base = owner_of(pos, core, first, second, depth) * batch + core * half
        hot.append(one_hot(dst[...] - base, rows))
    total = dot(jnp.concatenate(hot, axis=0), sent[...])
    own = local[pl.ds(pl.multiple_of(core * half, half), half), :]
    here = (first + second == 0).astype(F32)
    return jnp.concatenate([total[:half] + here * own, total[half:]], axis=0)


def edges_kernel(scale, groups, batch, pos, feat, hist, mean, weight, src, dst, moved, sent, local, theirs):
    step = pl.program_id(0)
    nodes, msgs = feat.shape[0], src.shape[2]

    @pl.when(step < groups)
    def _():
        deltas = (feat[...].astype(F32) - hist[...].astype(F32)).astype(BF)
        column = jnp.transpose(jnp.broadcast_to(src[0], (128, msgs)))
        lanes = lax.broadcasted_iota(jnp.int32, (msgs, 128), 1)
        hot = jnp.concatenate([one_hot(column, lanes + n) for n in range(0, nodes, 128)], axis=1)
        rows = dot(hot, deltas).astype(BF)
        moved[0] = rows
        span = pl.ds(pl.multiple_of(step * msgs, msgs), msgs)
        sent[span, :] = (scale * dot(rows, weight[0])).astype(BF)
        own = dot(mean[0], weight[0])
        local[...] = jnp.where(step == 0, own, local[...] + own)

    @pl.when(step >= groups)
    def _():
        part = step - groups
        total = partial_step(pos, 1 - pos[3], 1 - part // 2, part % 2, batch, dst, sent, local)
        theirs[...] = total.astype(BF)


def edges(pos, features, history, mean, weights, src, dst, scale, after):
    groups, width, _ = weights.shape
    batch, msgs = mean.shape[1], src.shape[2]
    rows = DEPTH * batch // 2
    rel = lambda *shape: ((1,) + shape, lambda s, pos: (jnp.minimum(s, groups - 1), 0, 0))
    return call(
        "edges",
        functools.partial(edges_kernel, scale, groups, batch),
        pos,
        [
            full(features),
            full(history),
            (mean,) + rel(batch, width),
            (weights,) + rel(width, width),
            (src,) + rel(1, msgs),
            full(dst),
        ],
        [
            ((groups, msgs, width), BF) + rel(msgs, width),
            out((groups * msgs, width), BF),
            out((batch, width), F32),
            ((4 * rows, width), BF, (rows, width), lambda s, pos: (jnp.maximum(s - groups, 0), 0)),
        ],
        grid=(groups + 4,),
        after=after,
    )


def pick_step(pos, core, batch, column, pieces, layout):
    half = batch // 2
    lanes = lax.broadcasted_iota(jnp.int32, (column.shape[0], half), 1)
    total = None
    for ref, blocks in zip(pieces, layout):
        hot = []
        for first, second, depth in blocks:
            base = owner_of(pos, core, first, second, depth) * batch + core * half
            hot.append(one_hot(column, lanes + base))
        term = dot(jnp.concatenate(hot, axis=1) if len(hot) > 1 else hot[0], ref[...])
        total = term if total is None else total + term
    return total


def early_kernel(layout, groups, batch, pos, dst, flat, sent, local, *refs):
    pieces, (spread, theirs, own, part) = refs[: len(layout)], refs[len(layout) :]
    step = pl.program_id(0)
    msgs = dst.shape[2]

    @pl.when(step < 2 * groups)
    def _():
        column = jnp.transpose(jnp.broadcast_to(dst[0], (128, msgs)))
        spread[0] = column
        rows = pick_step(pos, pos[3], batch, column, pieces, layout).astype(BF)

        @pl.when(step < groups)
        def _():
            theirs[0] = rows

        @pl.when(step >= groups)
        def _():
            own[0] = rows

    @pl.when(step >= 2 * groups)
    def _():
        at = step - 2 * groups
        part[...] = partial_step(pos, pos[3], 1 - at // 2, at % 2, batch, flat, sent, local)


def halves(groups, msgs, width):
    return (
        ((1, msgs, width), lambda s, pos: (jnp.clip(s, 0, groups - 1), 0, 0)),
        ((1, msgs, width), lambda s, pos: (jnp.clip(s - groups, 0, groups - 1), 0, 0)),
    )


def pick_early(pos, dst, flat, sent, local, pieces, layout, after):
    count, _, msgs = dst.shape
    groups = count // 2
    batch, width = local.shape
    rows = DEPTH * batch // 2
    every = lambda *shape: ((1,) + shape, lambda s, pos: (jnp.minimum(s, count - 1), 0, 0))
    theirs, own = halves(groups, msgs, width)
    return call(
        "pick_early",
        functools.partial(early_kernel, layout, groups, batch),
        pos,
        [(dst,) + every(1, msgs), full(flat), full(sent), full(local)] + [full(p) for p in pieces],
        [
            ((count, msgs, 128), jnp.int32) + every(msgs, 128),
            ((groups, msgs, width), BF) + theirs,
            ((groups, msgs, width), BF) + own,
            ((4 * rows, width), F32, (rows, width), lambda s, pos: (jnp.maximum(s - count, 0), 0)),
        ],
        grid=(count + 4,),
        after=after,
    )


def middle_kernel(layout, groups, batch, pos, spread, theirs, own, *refs):
    pieces, (theirs_out, own_out) = refs[: len(layout)], refs[len(layout) :]
    step = pl.program_id(0)
    rows = pick_step(pos, pos[3], batch, spread[0], pieces, layout)

    @pl.when(step < groups)
    def _():
        theirs_out[0] = (rows + theirs[0].astype(F32)).astype(BF)

    @pl.when(step >= groups)
    def _():
        own_out[0] = (rows + own[0].astype(F32)).astype(BF)


def pick_middle(pos, spread, theirs, own, batch, pieces, layout, after):
    groups, msgs, width = own.shape
    a, b = halves(groups, msgs, width)
    return call(
        "pick_middle",
        functools.partial(middle_kernel, layout, groups, batch),
        pos,
        [by_rel(spread), (theirs,) + a, (own,) + b] + [full(p) for p in pieces],
        [(own.shape, BF) + a, (own.shape, BF) + b],
        grid=(2 * groups,),
        after=after,
    )


def last_kernel(blocks, batch, pos, spread, own, piece, result):
    rows = pick_step(pos, pos[3], batch, spread[0], [piece], [blocks])
    result[0] = (rows + own[0].astype(F32)).astype(BF)


def pick_last(pos, spread, own, batch, piece, blocks, after):
    groups, msgs, _ = own.shape
    return call(
        "pick_last",
        functools.partial(last_kernel, blocks, batch),
        pos,
        [(spread, (1, msgs, 128), lambda s, pos: (groups + s, 0, 0)), by_rel(own), full(piece)],
        [(own.shape, BF) + by_rel(own)[1:]],
        grid=(groups,),
        after=after,
    )[0]


def back_kernel(scale, pos, picked, weight, src, result):
    step = pl.program_id(0)
    grads = (scale * dot(picked[0], weight[0], ((1,), (1,)))).astype(BF)
    rows = lax.broadcasted_iota(jnp.int32, (result.shape[0], src.shape[2]), 0)
    term = dot((src[0] == rows).astype(F32).astype(BF), grads)

    @pl.when(step == 0)
    def _():
        result[...] = term

    @pl.when(step > 0)
    def _():
        result[...] += term


def back(pos, picked, weights, src, nodes, scale, after):
    groups, _, width = picked.shape
    return call(
        "feature_terms",
        functools.partial(back_kernel, scale),
        pos,
        [by_rel(picked), by_rel(weights), by_rel(src)],
        [out((nodes, width), F32)],
        grid=(groups,),
        after=after,
    )[0]


def sum_kernel(pos, one, two, result):
    result[...] = (one[...].astype(F32) + two[...].astype(F32)).astype(result.dtype)


def rows_zero_kernel(pos, part, came, *away):
    total = (part[...] + came[...].astype(F32)).astype(BF)

    @pl.when(pl.program_id(0) == 0)
    def _():
        away[0][...] = total

    @pl.when(pl.program_id(0) == 1)
    def _():
        away[1][...] = total


def rows_zero(pos, part, came, after):
    rows = (part.shape[0] // 4, part.shape[1])
    block = (rows, lambda s, pos: (s, 0))
    return call(
        "rows_zero",
        rows_zero_kernel,
        pos,
        [(part,) + block, (came,) + block],
        [out(rows, BF), out(rows, BF)],
        grid=(2,),
        after=after,
    )


def rows_first_kernel(pos, part, passed, came, come, stay, away):
    rows = stay.shape[0]
    for ref, one, span in ((stay, came, slice(0, rows)), (away, come, slice(rows, 2 * rows))):
        total = part[span, :] + passed[span, :].astype(F32) + one[...].astype(F32)
        ref[...] = total.astype(ref.dtype)


def rows_first(pos, part, passed, came, after):
    rows = part.shape[0] // 2
    last = lambda array: (array, (rows, array.shape[1]), lambda s, pos: (1, 0))
    shape = (rows // 2, part.shape[1])
    return call(
        "rows_first",
        rows_first_kernel,
        pos,
        [last(part), last(passed), full(came[0]), full(came[1])],
        [out(shape, F32), out(shape, BF)],
        after=after,
    )


def rows_fold_kernel(pos, kept, came, stay, away):
    rows = stay.shape[0]
    for ref, span in ((stay, slice(0, rows)), (away, slice(rows, 2 * rows))):
        ref[...] = (kept[span, :] + came[span, :].astype(F32)).astype(ref.dtype)


def rows_fold(pos, kept, came, after):
    shape = (kept.shape[0] // 2, kept.shape[1])
    return call(
        "rows_fold",
        rows_fold_kernel,
        pos,
        [full(kept), full(came)],
        [out(shape, F32), out(shape, BF)],
        after=after,
    )


def line_sum_kernel(pos, kept, *refs):
    total = kept[...]
    for ref in refs[:-1]:
        total = total + ref[...].astype(F32)
    refs[-1][...] = total.astype(BF)


def line_sum(pos, kept, came, after):
    return call(
        "line_sum",
        line_sum_kernel,
        pos,
        [full(kept)] + [full(piece) for piece in came],
        [out(kept.shape, BF)],
        after=after,
        limit=24,
    )[0]


def finish_kernel(pos, total, opposite, result):
    half = total.shape[0]
    result[pl.ds(pl.multiple_of(pos[3] * half, half), half), :] = total[...]
    result[pl.ds(pl.multiple_of((1 - pos[3]) * half, half), half), :] = opposite[...]


def finish(pos, total, opposite, after):
    shape = (total.shape[0] * 2, total.shape[1])
    return call(
        "finish", finish_kernel, pos, [full(total), full(opposite)], [out(shape, BF)], after=after, limit=8
    )[0]


def weight_kernel(scale, norm, blocks, batch, pos, spread, own, came, far, mean, moved, cot, *refs):
    picked, away, kept = refs[-3:]
    total = pick_step(pos, 1 - pos[3], batch, spread[0], [far], [blocks])
    total = total + own[0].astype(F32) + came[0].astype(F32)
    rows = total.astype(BF)
    picked[0] = rows
    half = mean.shape[2] // 2
    place = jnp.where(pos[3] == 0, pos[1], pos[2])
    for ref, index in ((away, 1 - place), (kept, place)):
        columns = pl.ds(pl.multiple_of(index * half, 128), half)
        one = dot(mean[0, :, columns], cot[...], ((0,), (0,)))
        two = dot(moved[0, :, columns], rows, ((0,), (0,)))
        ref[0] = (norm * (one + scale * two)).astype(ref.dtype)


def weight_terms(pos, spread, own, came, far, blocks, mean, moved, cot, chunk, before, scale, norm, after):
    groups, msgs, width = moved.shape
    span = width // CHUNKS
    shape = (groups, width // 2, span)
    columns = lambda array: (array, (1, array.shape[1], span), lambda s, pos: (s, 0, chunk))
    flat = lambda array: (array, (array.shape[0], span), lambda s, pos: (0, chunk))
    block = ((1,) + shape[1:], lambda s, pos: (s, 0, 0))
    more = [] if before is None else [(before, None, None)]
    return call(
        "weight_terms",
        functools.partial(weight_kernel, scale, norm, blocks, cot.shape[0]),
        pos,
        [
            (spread, (1, msgs, 128), lambda s, pos: (groups + s, 0, 0)),
            columns(own),
            columns(came),
            flat(far),
            by_rel(mean),
            by_rel(moved),
            flat(cot),
        ]
        + more,
        [(own.shape, BF) + columns(own)[1:], (shape, BF) + block, (shape, F32) + block],
        grid=(groups,),
        after=after,
        alias={8: 0} if more else None,
    )


PLACES = (
    lambda pos: jnp.where(pos[3] == 0, pos[2], pos[1]),
    lambda pos: pos[0] % 2,
    lambda pos: pos[0] // 2,
)


def weight_fold_kernel(place, pos, kept, came, stay, away):
    rows = stay.shape[1]
    for ref, index in ((stay, place(pos)), (away, 1 - place(pos))):
        span = pl.ds(pl.multiple_of(index * rows, 16), rows)
        ref[...] = (kept[:, span, :] + came[:, span, :].astype(F32)).astype(ref.dtype)


def weight_fold(pos, kept, came, place, after):
    shape = (kept.shape[0], kept.shape[1] // 2, kept.shape[2])
    return call(
        "weight_fold",
        functools.partial(weight_fold_kernel, place),
        pos,
        [full(kept), full(came)],
        [out(shape, F32), out(shape, BF)],
        after=after,
    )


def assemble_kernel(pos, *refs):
    result = refs[-1]
    z, y, x, core = pos[0], pos[1], pos[2], pos[3]
    first = jnp.where(core == 0, y, x)
    second = jnp.where(core == 0, x, y)
    count = pl.num_programs(0)
    rows = result.shape[1] // NODES_HERE
    for flip_a, ref in enumerate(refs[:2]):
        for index in range(2 * DEPTH):
            flip_b, k = index // DEPTH, LINE[index % DEPTH]
            block = ((first ^ flip_a) * 2 + (second ^ flip_b)) * DEPTH + z % 2 * 2 + z // 2
            place = block ^ (k % 2 * 2 + k // 2)
            start = (index * count + pl.program_id(0)) * rows
            result[0, pl.ds(pl.multiple_of(place * rows, 16), rows), :] = ref[
                pl.ds(pl.multiple_of(start, 16), rows), :
            ].astype(F32)


def assemble(pos, pieces, chunk, groups, width, before, after):
    span = pieces[0].shape[1]
    more = [] if before is None else [(before, None, None)]
    return call(
        "assemble",
        assemble_kernel,
        pos,
        [full(piece) for piece in pieces] + more,
        [((groups, width, width), F32, (1, width, span), lambda s, pos: (s, 0, chunk))],
        grid=(groups,),
        after=[] if after[0] is before else after,
        alias={3: 0} if more else None,
    )[0]


def body(
    features, history, history_mean, weights, source_rows, target_owner, target_rows, cotangent
):
    groups, width, _ = weights.shape
    batch = history_mean.shape[1]
    nodes = features.shape[0]
    msgs = source_rows.shape[1]
    owners = lax.axis_size("node")
    scale = 1.0 / (msgs // batch)
    dst = target_owner[:, :, 0] * batch + target_rows
    if owners != NODES_HERE:
        return anywhere(
            features, history, history_mean, weights, source_rows, dst, cotangent, scale
        )
    norm = (batch * owners) ** -0.5
    node = lax.axis_index("node")
    core = lax.axis_index("rel")
    z = node // 4
    pos = jnp.stack([z, node // 2 % 2, node % 2, core]).astype(jnp.int32)
    half = batch // 2
    src3 = source_rows[:, None, :]
    flat = dst.reshape(1, groups * msgs)
    swap = lambda array: hop(array, CORES)
    at = lambda a, b: tuple((a, b, k) for k in range(DEPTH))

    both = jnp.concatenate([swap(dst), dst])[:, None, :]
    mine = split(pos, cotangent)
    deep = [mine] + [hop(mine, ALONG[k]) for k in range(1, DEPTH)]
    moved, sent, local, theirs = edges(
        pos, features, history, history_mean, weights, src3, flat, scale, [mine, both]
    )
    deep = join(pos, deep, [theirs])
    (theirs,) = gate(pos, [theirs], [deep])

    deep_b, deep_a, came = hop(deep, SECOND), hop(deep, FIRST), swap(theirs)
    spread, pick_o, pick_m, part = pick_early(
        pos, both, flat, sent, local, [deep], (at(0, 0),), [deep]
    )
    deep_b, deep_a, came = gate(pos, [deep_b, deep_a, came], [part])

    deep_ab = hop(deep_b, FIRST)
    pick_o, pick_m = pick_middle(
        pos, spread, pick_o, pick_m, batch, [deep_a, deep_b], (at(1, 0), at(0, 1)), [deep_b]
    )
    deep_ab, pick_o = gate(pos, [deep_ab, pick_o], [pick_m])
    deep_abo = swap(deep_ab)
    pick_c = swap(pick_o)
    pick_m = pick_last(pos, spread, pick_m, batch, deep_ab, at(1, 1), [deep_ab])

    chunks = [{"index": index} for index in range(CHUNKS)]
    last, picked = pick_m, None
    for chunk in chunks:
        picked, chunk["away"], chunk["kept"] = weight_terms(
            pos,
            spread,
            pick_m,
            pick_c,
            deep_abo,
            at(1, 1),
            history_mean,
            moved,
            cotangent,
            chunk["index"],
            picked,
            scale,
            norm,
            [last],
        )
        last = chunk["away"]
        chunk["came"] = hop(chunk["away"], FIRST)
    state = {"grads": None}
    FOLDS = (SECOND, ALONG[1], ALONG[2])

    def weight_step(chunk, step, last):
        if step < 3:
            chunk["kept"], away = weight_fold(
                pos, chunk["kept"], chunk["came"], PLACES[step], [last]
            )
            chunk["came"] = hop(away, FOLDS[step])
            return away
        if step == 3:
            total = line_sum(pos, chunk["kept"], [chunk["came"]], [last])
            total = total.reshape(-1, total.shape[2])
            chunk["line"] = [total, hop(total, ALONG[2])]
            return total
        if step < 7:
            line = join(pos, chunk["line"], [last])
            chunk["line"] = [line, hop(line, (ALONG[1], SECOND, FIRST)[step - 4])]
            return line
        state["grads"] = assemble(
            pos, chunk["line"], chunk["index"], groups, width, state["grads"], [last]
        )
        return state["grads"]

    def rows_step(step, last):
        if step == -1:
            aways = rows_zero(pos, part, came, [last])
            state["came"] = [hop(away, FIRST) for away in aways]
            return aways[0]
        if step == 0:
            state["kept"], away = rows_first(pos, part, came, state["came"], [last])
        elif step < 3:
            state["kept"], away = rows_fold(pos, state["kept"], state["came"], [last])
        if step < 3:
            state["came"] = hop(away, FOLDS[step])
            return away
        if step == 3:
            state["total"] = line_sum(pos, state["kept"], [state["came"]], [last])
            state["opposite"] = swap(state["total"])
            return state["total"]
        state["out"] = finish(pos, state["total"], state["opposite"], [last])
        return state["out"]

    def back_step(step, last):
        if step == 0:
            state["terms"] = back(pos, picked, weights, src3, nodes, scale, [last])
            state["terms_o"] = swap(state["terms"])
            return state["terms"]
        state["back"] = call(
            "sum",
            sum_kernel,
            pos,
            [full(state["terms"]), full(state["terms_o"])],
            [out((nodes, width), BF)],
            after=[last],
        )[0]
        return state["back"]

    for what, step in ORDER:
        if what == "rows":
            last = rows_step(step, last)
        elif what == "back":
            last = back_step(step, last)
        else:
            last = weight_step(chunks[what], step, last)
    return state["out"], state["grads"], state["back"]


def anywhere(features, history, history_mean, weights, source_rows, dst, cotangent, scale):
    groups, width, _ = weights.shape
    batch, nodes = cotangent.shape[0], features.shape[0]
    total_batch = batch * lax.axis_size("node")
    deltas = (features.astype(F32) - history.astype(F32)).astype(BF)
    every = lax.all_gather(cotangent, "node", tiled=True)
    out = jnp.zeros((total_batch, width), F32)
    local = jnp.zeros((batch, width), F32)
    terms = jnp.zeros((nodes, width), F32)
    grads = []
    for rel in range(groups):
        rows = jnp.take(deltas, source_rows[rel], axis=0)
        picked = jnp.take(every, dst[rel], axis=0)
        out = out.at[dst[rel]].add(scale * dot(rows, weights[rel]))
        local = local + dot(history_mean[rel], weights[rel])
        edge = (scale * dot(picked, weights[rel], ((1,), (1,)))).astype(BF)
        terms = terms.at[source_rows[rel]].add(edge.astype(F32))
        grads.append(
            dot(history_mean[rel], cotangent, ((0,), (0,)))
            + scale * dot(rows, picked, ((0,), (0,)))
        )
    layer_out = lax.psum(lax.psum_scatter(out, "node", tiled=True) + local, "rel").astype(BF)
    weight_grads = lax.psum(jnp.stack(grads) * total_batch**-0.5, "node")
    return layer_out, weight_grads, lax.psum(terms, "rel").astype(BF)


def solution(mesh):
    in_specs = (
        P("node", None),
        P("node", None),
        P("rel", "node", None),
        P("rel", None, None),
        P("rel", "node"),
        P("rel", "node", None),
        P("rel", "node"),
        P("node", None),
    )
    out_specs = (P("node", None), P("rel", None, None), P("node", None))
    return jax.shard_map(body, mesh=mesh, in_specs=in_specs, out_specs=out_specs, check_vma=False)
```

time: 558 us -> 197 us (0.35)
  waiting for transfers between devices: 389 us -> 71.6 us
  Pallas kernels: 0 us -> 69.4 us
  local copies, waits for them, and re-layouts: 46.5 us -> 12.4 us
  matrix products: 32 us -> 0 us
  other arithmetic: 20.7 us -> 0.8 us
  between operations: 14.2 us -> 1.03 us
  blocking collectives: 10.5 us -> 0 us
    all_to_all x3 -> x0, waiting for transfers between devices: 242 us -> none  [the longest x1 152 us: body(): lax.all_to_all(grad_rows.reshape(groups, owners, capacity, width), 'node'...]
    psum x1 -> x0, waiting for transfers between devices: 147 us -> none  [body(): weight_grads = lax.psum(local_grads, 'node')]
    ppermute x0 -> x33, waiting for transfers between devices: none -> 71.6 us  [hop(): return lax.ppermute(array, AXES, table)]
    pallas_call x0 -> x35, Pallas kernels: none -> 69.4 us  [call(): pl.pallas_call(run, grid_spec=pltpu.PrefetchScalarGridSpec(num_scalar_pre...]
    all_to_all x3 -> x0, starting transfers between devices: 42.4 us -> none  [the longest x1 27.1 us: body(): lax.all_to_all(grad_rows.reshape(groups, owners, capacity, width), 'node'...]
    ppermute x0 -> x33, starting transfers between devices: none -> 40.8 us  [hop(): return lax.ppermute(array, AXES, table)]
    dot_general x6 -> x0, matrix products: 32 us -> none  [the longest x1 9.09 us: body(): jnp.einsum('rmu,rmd->ud', source_hot, edge_grads, preferred_element_type=...]
    all_to_all x4 -> x0, local copies, waits for them, and re-layouts: 10.8 us -> none  [the longest x1 5.73 us: body(): lax.all_to_all(grad_rows.reshape(groups, owners, capacity, width), 'node'...]
  transfers between devices with their start and end apart: 4 -> 33, of which waited for: 3 -> 19; matrix products, arithmetic and copies ran while one was open for 13% -> 1% of each run, Pallas kernels for 0% -> 29%
where the time goes in v2:
time: 197 us; the launch traced here: 196 us
  waiting for transfers between devices  71.6 us (36%)
  Pallas kernels  69.4 us (35%)
  starting transfers between devices  40.8 us (21%)
  local copies, waits for them, and re-layouts  12.4 us (6%)
    ppermute x33, waiting for transfers between devices, hop(): return lax.ppermute(array, AXES, table)  71.6 us
    pallas_call x35, Pallas kernels, call(): pl.pallas_call(run, grid_spec=pltpu.PrefetchScalarGridSpec(num_scalar_pre...  69.4 us
    ppermute x33, starting transfers between devices, hop(): return lax.ppermute(array, AXES, table)  40.8 us
    unnamed x23, local copies, waits for them, and re-layouts  11.7 us
  transfers between devices with their start and end apart: 33, of which 19 were waited for; matrix products, arithmetic and copies ran while one was open for 1% of the time, Pallas kernels for 29%

profile of v2, /device:TPU:0, one launch (start us, length us, event | category | flops | bytes accessed | tf_op | source)
XLA Modules:
  0.0 196.0 jit_solution(17470066054215326350)
XLA Ops:
  2.3 5.1 %collective-permute-start.3 = (bf16[128,768]{1,0:T(8,128)(2,1)S(1)}, bf16[128,768]{1,0:T(8,128)(2,1)S(1)}, u32[]{:S(2)}, u32[]{:S(2)}) collective-permute-start(bf16[128,768]{1,0:T(8,128)(2,1)S(1)} %split.1.refs_6_.refs_0_), channel_id=1, source_target_pairs={{0,24},{1,25},{2,26},{3,27},{4,28},{5,29},{6,30},{7,31},{8,16},{9,... | collective-permute-start | bytes 589832 | tf_op jit(solution)/shard_map/ppermute | solution.py:119
  10.0 2.0 %copy-done.1 = bf16[3,768,768]{2,1,0:T(8,128)(2,1)S(1)} copy-done((bf16[3,768,768]{2,1,0:T(8,128)(2,1)S(1)}, bf16[3,768,768]{2,1,0:T(8,128)(2,1)}, u32[]{:S(2)}) %copy-start.1) | copy-done | bytes 3538968
  12.0 1.3 copy-done.3
  15.5 11.0 %edges.1 = (bf16[3,512,768]{2,1,0:T(8,128)(2,1)S(1)}, bf16[1536,768]{1,0:T(8,128)(2,1)S(1)}, f32[256,768]{1,0:T(8,128)S(1)}, bf16[2048,768]{1,0:T(8,128)(2,1)S(1)}) custom-call(s32[4]{0:T(128)S(1)} %pad_add_fusion.1.pos_ref, bf16[512,768]{1,0:T(8,128)(2,1)S(1)} %copy-done.9, bf16[512,768]{1,0:T(8,128)(2,1)S(1)} %copy-done.10, ...), custom_call_target="tpu_custom_call" | custom-call | flops 1000 | bytes 1000 | tf_op jit(solution)/shard_map/edges/pallas_call | solution.py:61
  27.9 1.7 collective-permute-start.5
  29.6 1.5 collective-permute-start.4
  31.1 10.5 %pick_early.1 = (s32[6,512,128]{2,1,0:T(8,128)S(1)}, bf16[3,512,768]{2,1,0:T(8,128)(2,1)S(1)}, bf16[3,512,768]{2,1,0:T(8,128)(2,1)S(1)}, f32[2048,768]{1,0:T(8,128)S(1)}) custom-call(s32[4]{0:T(128)S(1)} %pad_add_fusion.1.pos_ref, s32[6,1,512]{2,1,0:T(1,128)S(1)} %broadcast_in_dim.6.refs_7_.refs_0_, s32[1,1536]{1,0:T(1,128)S(1)} %bitcast.18, ...), custom_call_target="tpu_custom_call" | custom-call | flops 1000 | bytes 1000 | tf_op jit(solution)/shard_map/pick_early/pallas_call | solution.py:61
  41.6 6.0 %collective-permute-done.5.refs_1_ = bf16[512,768]{1,0:T(8,128)(2,1)S(1)} collective-permute-done((bf16[512,768]{1,0:T(8,128)(2,1)S(1)}, bf16[512,768]{1,0:T(8,128)(2,1)S(1)}, u32[]{:S(2)}, u32[]{:S(2)}) %collective-permute-start.5) | collective-permute-done | bytes 786464 | tf_op jit(solution)/shard_map/ppermute | solution.py:119
  48.2 1.8 collective-permute-start.7
  50.1 7.6 %pick_middle.1 = (bf16[3,512,768]{2,1,0:T(8,128)(2,1)S(1)}, bf16[3,512,768]{2,1,0:T(8,128)(2,1)S(1)}) custom-call(s32[4]{0:T(128)S(1)} %pad_add_fusion.1.pos_ref, s32[6,512,128]{2,1,0:T(8,128)S(1)} %get-tuple-element.49.refs_0_, bf16[3,512,768]{2,1,0:T(8,128)(2,1)S(1)} %get-tuple-element.50.refs_1_, bf16[3,512,768]{2,1,0:T(8,128)(2,1)S(1)} %get-tuple-element.51.refs_2_, ...), custom_call_target="tpu_custom_call" | custom-call | flops 1000 | bytes 1000 | tf_op jit(solution)/shard_map/pick_middle/pallas_call | solution.py:61
  57.6 2.7 %collective-permute-done.7.refs_0_ = bf16[512,768]{1,0:T(8,128)(2,1)S(1)} collective-permute-done((bf16[512,768]{1,0:T(8,128)(2,1)S(1)}, bf16[512,768]{1,0:T(8,128)(2,1)S(1)}, u32[]{:S(2)}, u32[]{:S(2)}) %collective-permute-start.7) | collective-permute-done | bytes 786464 | tf_op jit(solution)/shard_map/ppermute | solution.py:119
  61.4 2.3 %pick_last.1.refs_1_.refs_7_ = bf16[3,512,768]{2,1,0:T(8,128)(2,1)S(1)} custom-call(s32[4]{0:T(128)S(1)} %pad_add_fusion.1.pos_ref, s32[6,512,128]{2,1,0:T(8,128)S(1)} %get-tuple-element.49.refs_0_, bf16[3,512,768]{2,1,0:T(8,128)(2,1)S(1)} %get-tuple-element.54.refs_2_.refs_1_, bf16[512,768]{1,0:T(8,128)(2,1)S(1)} %get-tuple-element.56.refs_2_.refs_3_, ...), custom_call_target="tpu_custom_call" | custom-call | flops 1000 | bytes 1000 | tf_op jit(solution)/shard_map/pick_last/pallas_call | solution.py:61
  63.7 2.8 %collective-permute-done.9.refs_3_ = bf16[512,768]{1,0:T(8,128)(2,1)S(1)} collective-permute-done((bf16[512,768]{1,0:T(8,128)(2,1)S(1)}, bf16[512,768]{1,0:T(8,128)(2,1)S(1)}, u32[]{:S(2)}, u32[]{:S(2)}) %collective-permute-start.9) | collective-permute-done | bytes 786464 | tf_op jit(solution)/shard_map/ppermute | solution.py:119
  66.6 4.5 %weight_terms.2 = (bf16[3,512,768]{2,1,0:T(8,128)(2,1)S(1)}, bf16[3,384,384]{2,1,0:T(8,128)(2,1)S(1)}, f32[3,384,384]{2,1,0:T(8,128)S(1)}) custom-call(s32[4]{0:T(128)S(1)} %pad_add_fusion.1.pos_ref, s32[6,512,128]{2,1,0:T(8,128)S(1)} %get-tuple-element.49.refs_0_, bf16[3,512,768]{2,1,0:T(8,128)(2,1)S(1)} %pick_last.1.refs_1_.refs_7_, ...), custom_call_target="tpu_custom_call" | custom-call | flops 1000 | bytes 1000 | tf_op jit(solution)/shard_map/weight_terms/pallas_call | solution.py:61
  71.1 1.8 collective-permute-start.10
  72.9 4.5 %weight_terms.3 = (bf16[3,512,768]{2,1,0:T(8,128)(2,1)S(1)}, bf16[3,384,384]{2,1,0:T(8,128)(2,1)S(1)}, f32[3,384,384]{2,1,0:T(8,128)S(1)}) custom-call(s32[4]{0:T(128)S(1)} %pad_add_fusion.1.pos_ref, s32[6,512,128]{2,1,0:T(8,128)S(1)} %get-tuple-element.49.refs_0_, ...), custom_call_target="tpu_custom_call", output_to_operand_aliasing={{0}: (8, {})} | custom-call | flops 1000 | bytes 1000 | tf_op jit(solution)/shard_map/weight_terms/pallas_call | solution.py:61
  77.7 6.5 %collective-permute-done.10.refs_1_ = bf16[3,384,384]{2,1,0:T(8,128)(2,1)S(1)} collective-permute-done((bf16[3,384,384]{2,1,0:T(8,128)(2,1)S(1)}, bf16[3,384,384]{2,1,0:T(8,128)(2,1)S(1)}, u32[]{:S(2)}, u32[]{:S(2)}) %collective-permute-start.10) | collective-permute-done | bytes 884768 | tf_op jit(solution)/shard_map/ppermute | solution.py:119
  84.9 1.8 collective-permute-start.11
  86.7 4.9 %feature_terms.1.refs_2_.refs_0_ = f32[512,768]{1,0:T(8,128)S(1)} custom-call(s32[4]{0:T(128)S(1)} %pad_add_fusion.1.pos_ref, bf16[3,512,768]{2,1,0:T(8,128)(2,1)S(1)} %get-tuple-element.66.refs_0_, bf16[3,768,768]{2,1,0:T(8,128)(2,1)S(1)} %copy-done.2, s32[3,1,512]{2,1,0:T(1,128)S(1)} %broadcast_in_dim.7.refs_4_.refs_2_, ...), custom_call_target="tpu_custom_call" | custom-call | flops 1000 | bytes 1000 | tf_op jit(solution)/shard_map/feature_terms/pallas_call | solution.py:61
  91.6 6.8 %collective-permute-done.12.refs_1_ = bf16[3,384,384]{2,1,0:T(8,128)(2,1)S(1)} collective-permute-done((bf16[3,384,384]{2,1,0:T(8,128)(2,1)S(1)}, bf16[3,384,384]{2,1,0:T(8,128)(2,1)S(1)}, u32[]{:S(2)}, u32[]{:S(2)}) %collective-permute-start.12) | collective-permute-done | bytes 884768 | tf_op jit(solution)/shard_map/ppermute | solution.py:119
  99.8 1.4 rows_zero.1
  101.2 1.8 collective-permute-start.14
  103.3 1.8 collective-permute-start.15
  105.1 1.4 collective-permute-start.16
  106.5 4.5 %collective-permute-done.16.refs_1_ = bf16[3,96,384]{2,1,0:T(8,128)(2,1)S(1)} collective-permute-done((bf16[3,96,384]{2,1,0:T(8,128)(2,1)S(1)}, bf16[3,96,384]{2,1,0:T(8,128)(2,1)S(1)}, u32[]{:S(2)}, u32[]{:S(2)}) %collective-permute-start.16) | collective-permute-done | bytes 221216 | tf_op jit(solution)/shard_map/ppermute | solution.py:119
  111.6 4.8 %collective-permute-done.15.refs_1_ = bf16[3,192,384]{2,1,0:T(8,128)(2,1)S(1)} collective-permute-done((bf16[3,192,384]{2,1,0:T(8,128)(2,1)S(1)}, bf16[3,192,384]{2,1,0:T(8,128)(2,1)S(1)}, u32[]{:S(2)}, u32[]{:S(2)}) %collective-permute-start.15) | collective-permute-done | bytes 442400 | tf_op jit(solution)/shard_map/ppermute | solution.py:119
  117.1 1.5 collective-permute-start.17
  118.6 2.9 %collective-permute-start.18 = (bf16[3,48,384]{2,1,0:T(8,128)(2,1)S(1)}, bf16[3,48,384]{2,1,0:T(8,128)(2,1)S(1)}, u32[]{:S(2)}, u32[]{:S(2)}) collective-permute-start(bf16[3,48,384]{2,1,0:T(8,128)(2,1)S(1)} %get-tuple-element.73.refs_2_), channel_id=1, source_target_pairs={{0,16},{1,17},{2,18},{3,19},{4,20},{5,21},{6,22},{7,23},{8,24},{9,... | collective-permute-start | bytes 331784 | tf_op jit(solution)/shard_map/ppermute | solution.py:119
  121.6 3.0 %collective-permute-done.18.refs_1_ = bf16[3,48,384]{2,1,0:T(8,128)(2,1)S(1)} collective-permute-done((bf16[3,48,384]{2,1,0:T(8,128)(2,1)S(1)}, bf16[3,48,384]{2,1,0:T(8,128)(2,1)S(1)}, u32[]{:S(2)}, u32[]{:S(2)}) %collective-permute-start.18) | collective-permute-done | bytes 110624 | tf_op jit(solution)/shard_map/ppermute | solution.py:119
  125.2 3.4 %collective-permute-start.20 = (bf16[144,384]{1,0:T(8,128)(2,1)S(1)}, bf16[144,384]{1,0:T(8,128)(2,1)S(1)}, u32[]{:S(2)}, u32[]{:S(2)}) collective-permute-start(bf16[144,384]{1,0:T(8,128)(2,1)S(1)} %bitcast.14), channel_id=1, source_target_pairs={{0,16},{1,17},{2,18},{3,19},{4,20},{5,21},{6,22},{7,23},{8,24},{9,... | collective-permute-start | bytes 331784 | tf_op jit(solution)/shard_map/ppermute | solution.py:119
  129.3 2.1 %collective-permute-done.20.refs_1_ = bf16[144,384]{1,0:T(8,128)(2,1)S(1)} collective-permute-done((bf16[144,384]{1,0:T(8,128)(2,1)S(1)}, bf16[144,384]{1,0:T(8,128)(2,1)S(1)}, u32[]{:S(2)}, u32[]{:S(2)}) %collective-permute-start.20) | collective-permute-done | bytes 110624 | tf_op jit(solution)/shard_map/ppermute | solution.py:119
  132.0 3.0 %collective-permute-done.19.refs_1_ = bf16[3,48,384]{2,1,0:T(8,128)(2,1)S(1)} collective-permute-done((bf16[3,48,384]{2,1,0:T(8,128)(2,1)S(1)}, bf16[3,48,384]{2,1,0:T(8,128)(2,1)S(1)}, u32[]{:S(2)}, u32[]{:S(2)}) %collective-permute-start.19) | collective-permute-done | bytes 110624 | tf_op jit(solution)/shard_map/ppermute | solution.py:119
  136.6 1.7 collective-permute-start.21
  138.3 7.1 %collective-permute-done.23.refs_1_ = bf16[288,384]{1,0:T(8,128)(2,1)S(1)} collective-permute-done((bf16[288,384]{1,0:T(8,128)(2,1)S(1)}, bf16[288,384]{1,0:T(8,128)(2,1)S(1)}, u32[]{:S(2)}, u32[]{:S(2)}) %collective-permute-start.23) | collective-permute-done | bytes 221216 | tf_op jit(solution)/shard_map/ppermute | solution.py:119
  147.3 4.9 %collective-permute-done.22.refs_1_ = bf16[144,384]{1,0:T(8,128)(2,1)S(1)} collective-permute-done((bf16[144,384]{1,0:T(8,128)(2,1)S(1)}, bf16[144,384]{1,0:T(8,128)(2,1)S(1)}, u32[]{:S(2)}, u32[]{:S(2)}) %collective-permute-start.22) | collective-permute-done | bytes 110624 | tf_op jit(solution)/shard_map/ppermute | solution.py:119
  155.0 3.7 %collective-permute-done.25.refs_1_ = bf16[288,384]{1,0:T(8,128)(2,1)S(1)} collective-permute-done((bf16[288,384]{1,0:T(8,128)(2,1)S(1)}, bf16[288,384]{1,0:T(8,128)(2,1)S(1)}, u32[]{:S(2)}, u32[]{:S(2)}) %collective-permute-start.25) | collective-permute-done | bytes 221216 | tf_op jit(solution)/shard_map/ppermute | solution.py:119
  159.4 1.9 collective-permute-start.29
  161.3 2.5 %collective-permute-start.28 = (bf16[1152,384]{1,0:T(8,128)(2,1)S(1)}, bf16[1152,384]{1,0:T(8,128)(2,1)S(1)}, u32[]{:S(2)}, u32[]{:S(2)}) collective-permute-start(bf16[1152,384]{1,0:T(8,128)(2,1)S(1)} %join.11.refs_2_.refs_0_), channel_id=1, source_target_pairs={{0,4},{1,3},{2,6},{3,1},{4,0},{5,7},{6,2},{7,5},{8,12},{9,11},{10,... | collective-permute-start | bytes 2654216 | tf_op jit(solution)/shard_map/ppermute | solution.py:119
  163.8 5.3 %collective-permute-done.24.refs_1_ = bf16[256,768]{1,0:T(8,128)(2,1)S(1)} collective-permute-done((bf16[256,768]{1,0:T(8,128)(2,1)S(1)}, bf16[256,768]{1,0:T(8,128)(2,1)S(1)}, u32[]{:S(2)}, u32[]{:S(2)}) %collective-permute-start.24) | collective-permute-done | bytes 393248 | tf_op jit(solution)/shard_map/ppermute | solution.py:119
  169.7 2.9 %collective-permute-done.29.refs_1_ = bf16[576,384]{1,0:T(8,128)(2,1)S(1)} collective-permute-done((bf16[576,384]{1,0:T(8,128)(2,1)S(1)}, bf16[576,384]{1,0:T(8,128)(2,1)S(1)}, u32[]{:S(2)}, u32[]{:S(2)}) %collective-permute-start.29) | collective-permute-done | bytes 442400 | tf_op jit(solution)/shard_map/ppermute | solution.py:119
  173.2 2.7 %collective-permute-start.32 = (bf16[1152,384]{1,0:T(8,128)(2,1)S(1)}, bf16[1152,384]{1,0:T(8,128)(2,1)S(1)}, u32[]{:S(2)}, u32[]{:S(2)}) collective-permute-start(bf16[1152,384]{1,0:T(8,128)(2,1)S(1)} %join.13.refs_2_.refs_0_), channel_id=1, source_target_pairs={{0,4},{1,3},{2,6},{3,1},{4,0},{5,7},{6,2},{7,5},{8,12},{9,11},{10,... | collective-permute-start | bytes 2654216 | tf_op jit(solution)/shard_map/ppermute | solution.py:119
  175.8 1.9 collective-permute-start.27
  177.7 2.8 %assemble.2.refs_2_ = f32[3,768,768]{2,1,0:T(8,128)} custom-call(s32[4]{0:T(128)S(1)} %pad_add_fusion.1.pos_ref, bf16[1152,384]{1,0:T(8,128)(2,1)S(1)} %join.11.refs_2_.refs_0_, bf16[1152,384]{1,0:T(8,128)(2,1)S(1)} %collective-permute-done.28.refs_1_, bf16[1152,384]{1,0:T(8,128)(2,1)S(1)} %join.13.refs_2_.refs_0_), custom_call_target="tpu_custom_call" | custom-call | flops 1000 | bytes 1000 | tf_op jit(solution)/shard_map/assemble/pallas_call | solution.py:61
  180.5 4.0 %collective-permute-done.27.refs_1_ = bf16[128,768]{1,0:T(8,128)(2,1)S(1)} collective-permute-done((bf16[128,768]{1,0:T(8,128)(2,1)S(1)}, bf16[128,768]{1,0:T(8,128)(2,1)S(1)}, u32[]{:S(2)}, u32[]{:S(2)}) %collective-permute-start.27) | collective-permute-done | bytes 196640 | tf_op jit(solution)/shard_map/ppermute | solution.py:119
  184.5 3.0 %copy-done = f32[3,768,768]{2,1,0:T(8,128)S(1)} copy-done((f32[3,768,768]{2,1,0:T(8,128)S(1)}, f32[3,768,768]{2,1,0:T(8,128)}, u32[]{:S(2)}) %copy-start) | copy-done | bytes 7077912
  188.2 1.6 sum.1.refs_2_
  190.9 1.3 finish.1.refs_3_
  193.2 2.8 %assemble.3 = f32[3,768,768]{2,1,0:T(8,128)} custom-call(s32[4]{0:T(128)S(1)} %pad_add_fusion.1.pos_ref, bf16[1152,384]{1,0:T(8,128)(2,1)S(1)} %join.13.refs_2_.refs_0_, bf16[1152,384]{1,0:T(8,128)(2,1)S(1)} %collective-permute-done.32.refs_1_, f32[3,768,768]{2,1,0:T(8,128)} %assemble.2.refs_2_, ...), custom_call_target="tpu_custom_call", output_to_operand_aliasing={{}: (3, {})} | custom-call | flops 1000 | bytes 1000 | tf_op jit(solution)/shard_map/assemble/pallas_call | solution.py:61
  (81 shorter events, 26.1 us)
Async XLA Ops:
  0.7 1.0 copy-start.5
  2.3 24.2 %collective-permute-start.3 = (bf16[128,768]{1,0:T(8,128)(2,1)S(1)}, bf16[128,768]{1,0:T(8,128)(2,1)S(1)}, u32[]{:S(2)}, u32[]{:S(2)}) collective-permute-start(bf16[128,768]{1,0:T(8,128)(2,1)S(1)} %split.1.refs_6_.refs_0_), channel_id=1, source_target_pairs={{0,24},{1,25},{2,26},{3,27},{4,28},{5,29},{6,30},{7,31},{8,16},{9,... | collective-permute-start | bytes 589832 | tf_op jit(solution)/shard_map/ppermute | solution.py:119
  7.4 19.1 %collective-permute-start.2 = (bf16[128,768]{1,0:T(8,128)(2,1)S(1)}, bf16[128,768]{1,0:T(8,128)(2,1)S(1)}, u32[]{:S(2)}, u32[]{:S(2)}) collective-permute-start(bf16[128,768]{1,0:T(8,128)(2,1)S(1)} %split.1.refs_6_.refs_0_), channel_id=1, source_target_pairs={{0,16},{1,17},{2,18},{3,19},{4,20},{5,21},{6,22},{7,23},{8,24},{9,... | collective-permute-start | bytes 589832 | tf_op jit(solution)/shard_map/ppermute | solution.py:119
  7.4 19.1 %collective-permute-start.1 = (bf16[128,768]{1,0:T(8,128)(2,1)S(1)}, bf16[128,768]{1,0:T(8,128)(2,1)S(1)}, u32[]{:S(2)}, u32[]{:S(2)}) collective-permute-start(bf16[128,768]{1,0:T(8,128)(2,1)S(1)} %split.1.refs_6_.refs_0_), channel_id=1, source_target_pairs={{0,8},{1,9},{2,10},{3,11},{4,12},{5,13},{6,14},{7,15},{8,0},{9,1},... | collective-permute-start | bytes 589832 | tf_op jit(solution)/shard_map/ppermute | solution.py:119
  8.8 1.2 collective-permute-start
  10.0 2.0 %copy-start.1 = (bf16[3,768,768]{2,1,0:T(8,128)(2,1)S(1)}, bf16[3,768,768]{2,1,0:T(8,128)(2,1)}, u32[]{:S(2)}) copy-start(bf16[3,768,768]{2,1,0:T(8,128)(2,1)} %refs_1_.3) | copy-start | bytes 10616836
  12.0 1.3 copy-start.3
  13.3 1.1 copy-start.9
  14.4 1.1 copy-start.10
  27.7 20.0 %collective-permute-start.6 = (bf16[2048,768]{1,0:T(8,128)(2,1)S(1)}, bf16[2048,768]{1,0:T(8,128)(2,1)S(1)}, u32[]{:S(2)}, u32[]{:S(2)}) collective-permute-start(bf16[2048,768]{1,0:T(8,128)(2,1)S(1)} %gate.3), channel_id=1, source_target_pairs={{0,1},{1,0},{2,3},{3,2},{4,5},{5,4},{6,7},{7,6},{8,9},{9,8},{10,11... | collective-permute-start | bytes 9437192 | tf_op jit(solution)/shard_map/ppermute | solution.py:119
  27.9 19.7 %collective-permute-start.5 = (bf16[512,768]{1,0:T(8,128)(2,1)S(1)}, bf16[512,768]{1,0:T(8,128)(2,1)S(1)}, u32[]{:S(2)}, u32[]{:S(2)}) collective-permute-start(bf16[512,768]{1,0:T(8,128)(2,1)S(1)} %join.7.refs_4_.refs_5_.refs_1_), channel_id=1, source_target_pairs={{0,4},{1,3},{2,6},{3,1},{4,0},{5,7},{6,2},{7,5},{8,12},{9,11},{10,... | collective-permute-start | bytes 2359304 | tf_op jit(solution)/shard_map/ppermute | solution.py:119
  29.6 18.1 %collective-permute-start.4 = (bf16[512,768]{1,0:T(8,128)(2,1)S(1)}, bf16[512,768]{1,0:T(8,128)(2,1)S(1)}, u32[]{:S(2)}, u32[]{:S(2)}) collective-permute-start(bf16[512,768]{1,0:T(8,128)(2,1)S(1)} %join.7.refs_4_.refs_5_.refs_1_), channel_id=1, source_target_pairs={{0,2},{1,5},{2,0},{3,7},{4,6},{5,1},{6,4},{7,3},{8,10},{9,13},{10,... | collective-permute-start | bytes 2359304 | tf_op jit(solution)/shard_map/ppermute | solution.py:119
  48.2 12.1 %collective-permute-start.7 = (bf16[512,768]{1,0:T(8,128)(2,1)S(1)}, bf16[512,768]{1,0:T(8,128)(2,1)S(1)}, u32[]{:S(2)}, u32[]{:S(2)}) collective-permute-start(bf16[512,768]{1,0:T(8,128)(2,1)S(1)} %get-tuple-element.53.refs_4_.refs_5_), channel_id=1, source_target_pairs={{0,4},{1,3},{2,6},{3,1},{4,0},{5,7},{6,2},{7,5},{8,12},{9,11},{10,... | collective-permute-start | bytes 2359304 | tf_op jit(solution)/shard_map/ppermute | solution.py:119
  60.9 5.7 %collective-permute-start.8 = (bf16[3,512,768]{2,1,0:T(8,128)(2,1)S(1)}, bf16[3,512,768]{2,1,0:T(8,128)(2,1)S(1)}, u32[]{:S(2)}, u32[]{:S(2)}) collective-permute-start(bf16[3,512,768]{2,1,0:T(8,128)(2,1)S(1)} %get-tuple-element.57), channel_id=1, source_target_pairs={{0,1},{1,0},{2,3},{3,2},{4,5},{5,4},{6,7},{7,6},{8,9},{9,8},{10,11... | collective-permute-start | bytes 7077896 | tf_op jit(solution)/shard_map/ppermute | solution.py:119
  60.9 5.7 %copy-start.4 = (bf16[3,256,768]{2,1,0:T(8,128)(2,1)S(1)}, bf16[3,256,768]{2,1,0:T(8,128)(2,1)}, u32[]{:S(2)}) copy-start(bf16[3,256,768]{2,1,0:T(8,128)(2,1)} %refs_4_.3) | copy-start | bytes 3538948
  60.9 5.6 %copy-start.6 = (bf16[256,768]{1,0:T(8,128)(2,1)S(1)}, bf16[256,768]{1,0:T(8,128)(2,1)}, u32[]{:S(2)}) copy-start(bf16[256,768]{1,0:T(8,128)(2,1)} %refs_6_.3) | copy-start | bytes 1179652
  61.0 5.6 %collective-permute-start.9 = (bf16[512,768]{1,0:T(8,128)(2,1)S(1)}, bf16[512,768]{1,0:T(8,128)(2,1)S(1)}, u32[]{:S(2)}, u32[]{:S(2)}) collective-permute-start(bf16[512,768]{1,0:T(8,128)(2,1)S(1)} %get-tuple-element.56.refs_2_.refs_3_), channel_id=1, source_target_pairs={{0,1},{1,0},{2,3},{3,2},{4,5},{5,4},{6,7},{7,6},{8,9},{9,8},{10,11... | collective-permute-start | bytes 2359304 | tf_op jit(solution)/shard_map/ppermute | solution.py:119
  71.1 13.1 %collective-permute-start.10 = (bf16[3,384,384]{2,1,0:T(8,128)(2,1)S(1)}, bf16[3,384,384]{2,1,0:T(8,128)(2,1)S(1)}, u32[]{:S(2)}, u32[]{:S(2)}) collective-permute-start(bf16[3,384,384]{2,1,0:T(8,128)(2,1)S(1)} %get-tuple-element.60.refs_8_), channel_id=1, source_target_pairs={{0,4},{1,3},{2,6},{3,1},{4,0},{5,7},{6,2},{7,5},{8,12},{9,11},{10,... | collective-permute-start | bytes 2654216 | tf_op jit(solution)/shard_map/ppermute | solution.py:119
  77.4 9.3 %copy-start.2 = (bf16[3,768,768]{2,1,0:T(8,128)(2,1)S(1)}, bf16[3,768,768]{2,1,0:T(8,128)(2,1)}, u32[]{:S(2)}) copy-start(bf16[3,768,768]{2,1,0:T(8,128)(2,1)} %refs_1_.3) | copy-start | bytes 10616836
  77.4 21.0 %collective-permute-start.12 = (bf16[3,384,384]{2,1,0:T(8,128)(2,1)S(1)}, bf16[3,384,384]{2,1,0:T(8,128)(2,1)S(1)}, u32[]{:S(2)}, u32[]{:S(2)}) collective-permute-start(bf16[3,384,384]{2,1,0:T(8,128)(2,1)S(1)} %get-tuple-element.62.refs_2_), channel_id=1, source_target_pairs={{0,4},{1,3},{2,6},{3,1},{4,0},{5,7},{6,2},{7,5},{8,12},{9,11},{10,... | collective-permute-start | bytes 2654216 | tf_op jit(solution)/shard_map/ppermute | solution.py:119
  84.9 14.3 %collective-permute-start.11 = (bf16[3,192,384]{2,1,0:T(8,128)(2,1)S(1)}, bf16[3,192,384]{2,1,0:T(8,128)(2,1)S(1)}, u32[]{:S(2)}, u32[]{:S(2)}) collective-permute-start(bf16[3,192,384]{2,1,0:T(8,128)(2,1)S(1)} %get-tuple-element.64.refs_3_), channel_id=1, source_target_pairs={{0,2},{1,5},{2,0},{3,7},{4,6},{5,1},{6,4},{7,3},{8,10},{9,13},{10,... | collective-permute-start | bytes 1327112 | tf_op jit(solution)/shard_map/ppermute | solution.py:119
  101.2 34.3 %collective-permute-start.14 = (bf16[512,768]{1,0:T(8,128)(2,1)S(1)}, bf16[512,768]{1,0:T(8,128)(2,1)S(1)}, u32[]{:S(2)}, u32[]{:S(2)}) collective-permute-start(bf16[512,768]{1,0:T(8,128)(2,1)S(1)} %get-tuple-element.70), channel_id=1, source_target_pairs={{0,4},{1,3},{2,6},{3,1},{4,0},{5,7},{6,2},{7,5},{8,12},{9,11},{10,... | collective-permute-start | bytes 2359304 | tf_op jit(solution)/shard_map/ppermute | solution.py:119
  103.1 32.5 %collective-permute-start.13 = (bf16[512,768]{1,0:T(8,128)(2,1)S(1)}, bf16[512,768]{1,0:T(8,128)(2,1)S(1)}, u32[]{:S(2)}, u32[]{:S(2)}) collective-permute-start(bf16[512,768]{1,0:T(8,128)(2,1)S(1)} %get-tuple-element.69.refs_2_), channel_id=1, source_target_pairs={{0,4},{1,3},{2,6},{3,1},{4,0},{5,7},{6,2},{7,5},{8,12},{9,11},{10,... | collective-permute-start | bytes 2359304 | tf_op jit(solution)/shard_map/ppermute | solution.py:119
  103.3 13.1 %collective-permute-start.15 = (bf16[3,192,384]{2,1,0:T(8,128)(2,1)S(1)}, bf16[3,192,384]{2,1,0:T(8,128)(2,1)S(1)}, u32[]{:S(2)}, u32[]{:S(2)}) collective-permute-start(bf16[3,192,384]{2,1,0:T(8,128)(2,1)S(1)} %get-tuple-element.67.refs_2_), channel_id=1, source_target_pairs={{0,2},{1,5},{2,0},{3,7},{4,6},{5,1},{6,4},{7,3},{8,10},{9,13},{10,... | collective-permute-start | bytes 1327112 | tf_op jit(solution)/shard_map/ppermute | solution.py:119
  105.1 5.9 %collective-permute-start.16 = (bf16[3,96,384]{2,1,0:T(8,128)(2,1)S(1)}, bf16[3,96,384]{2,1,0:T(8,128)(2,1)S(1)}, u32[]{:S(2)}, u32[]{:S(2)}) collective-permute-start(bf16[3,96,384]{2,1,0:T(8,128)(2,1)S(1)} %get-tuple-element.68.refs_2_), channel_id=1, source_target_pairs={{0,8},{1,9},{2,10},{3,11},{4,12},{5,13},{6,14},{7,15},{8,0},{9,1},... | collective-permute-start | bytes 663560 | tf_op jit(solution)/shard_map/ppermute | solution.py:119
  117.1 11.5 %collective-permute-start.17 = (bf16[3,96,384]{2,1,0:T(8,128)(2,1)S(1)}, bf16[3,96,384]{2,1,0:T(8,128)(2,1)S(1)}, u32[]{:S(2)}, u32[]{:S(2)}) collective-permute-start(bf16[3,96,384]{2,1,0:T(8,128)(2,1)S(1)} %get-tuple-element.75.refs_2_), channel_id=1, source_target_pairs={{0,8},{1,9},{2,10},{3,11},{4,12},{5,13},{6,14},{7,15},{8,0},{9,1},... | collective-permute-start | bytes 663560 | tf_op jit(solution)/shard_map/ppermute | solution.py:119
  118.6 6.0 %collective-permute-start.18 = (bf16[3,48,384]{2,1,0:T(8,128)(2,1)S(1)}, bf16[3,48,384]{2,1,0:T(8,128)(2,1)S(1)}, u32[]{:S(2)}, u32[]{:S(2)}) collective-permute-start(bf16[3,48,384]{2,1,0:T(8,128)(2,1)S(1)} %get-tuple-element.73.refs_2_), channel_id=1, source_target_pairs={{0,16},{1,17},{2,18},{3,19},{4,20},{5,21},{6,22},{7,23},{8,24},{9,... | collective-permute-start | bytes 331784 | tf_op jit(solution)/shard_map/ppermute | solution.py:119
  125.2 6.2 %collective-permute-start.20 = (bf16[144,384]{1,0:T(8,128)(2,1)S(1)}, bf16[144,384]{1,0:T(8,128)(2,1)S(1)}, u32[]{:S(2)}, u32[]{:S(2)}) collective-permute-start(bf16[144,384]{1,0:T(8,128)(2,1)S(1)} %bitcast.14), channel_id=1, source_target_pairs={{0,16},{1,17},{2,18},{3,19},{4,20},{5,21},{6,22},{7,23},{8,24},{9,... | collective-permute-start | bytes 331784 | tf_op jit(solution)/shard_map/ppermute | solution.py:119
  129.2 5.8 %collective-permute-start.19 = (bf16[3,48,384]{2,1,0:T(8,128)(2,1)S(1)}, bf16[3,48,384]{2,1,0:T(8,128)(2,1)S(1)}, u32[]{:S(2)}, u32[]{:S(2)}) collective-permute-start(bf16[3,48,384]{2,1,0:T(8,128)(2,1)S(1)} %get-tuple-element.78.refs_2_), channel_id=1, source_target_pairs={{0,16},{1,17},{2,18},{3,19},{4,20},{5,21},{6,22},{7,23},{8,24},{9,... | collective-permute-start | bytes 331784 | tf_op jit(solution)/shard_map/ppermute | solution.py:119
  136.6 16.3 %collective-permute-start.21 = (bf16[512,768]{1,0:T(8,128)(2,1)S(1)}, bf16[512,768]{1,0:T(8,128)(2,1)S(1)}, u32[]{:S(2)}, u32[]{:S(2)}) collective-permute-start(bf16[512,768]{1,0:T(8,128)(2,1)S(1)} %get-tuple-element.80.refs_2_), channel_id=1, source_target_pairs={{0,2},{1,5},{2,0},{3,7},{4,6},{5,1},{6,4},{7,3},{8,10},{9,13},{10,... | collective-permute-start | bytes 2359304 | tf_op jit(solution)/shard_map/ppermute | solution.py:119
  138.3 7.1 %collective-permute-start.23 = (bf16[288,384]{1,0:T(8,128)(2,1)S(1)}, bf16[288,384]{1,0:T(8,128)(2,1)S(1)}, u32[]{:S(2)}, u32[]{:S(2)}) collective-permute-start(bf16[288,384]{1,0:T(8,128)(2,1)S(1)} %join.8.refs_2_.refs_0_), channel_id=1, source_target_pairs={{0,8},{1,9},{2,10},{3,11},{4,12},{5,13},{6,14},{7,15},{8,0},{9,1},... | collective-permute-start | bytes 663560 | tf_op jit(solution)/shard_map/ppermute | solution.py:119
  146.0 8.4 %collective-permute-start.26 = (bf16[576,384]{1,0:T(8,128)(2,1)S(1)}, bf16[576,384]{1,0:T(8,128)(2,1)S(1)}, u32[]{:S(2)}, u32[]{:S(2)}) collective-permute-start(bf16[576,384]{1,0:T(8,128)(2,1)S(1)} %join.9.refs_2_.refs_0_), channel_id=1, source_target_pairs={{0,2},{1,5},{2,0},{3,7},{4,6},{5,1},{6,4},{7,3},{8,10},{9,13},{10,... | collective-permute-start | bytes 1327112 | tf_op jit(solution)/shard_map/ppermute | solution.py:119
  146.4 5.8 %collective-permute-start.22 = (bf16[144,384]{1,0:T(8,128)(2,1)S(1)}, bf16[144,384]{1,0:T(8,128)(2,1)S(1)}, u32[]{:S(2)}, u32[]{:S(2)}) collective-permute-start(bf16[144,384]{1,0:T(8,128)(2,1)S(1)} %bitcast.12), channel_id=1, source_target_pairs={{0,16},{1,17},{2,18},{3,19},{4,20},{5,21},{6,22},{7,23},{8,24},{9,... | collective-permute-start | bytes 331784 | tf_op jit(solution)/shard_map/ppermute | solution.py:119
  147.3 40.9 %collective-permute-start.31 = (f32[512,768]{1,0:T(8,128)S(1)}, f32[512,768]{1,0:T(8,128)S(1)}, u32[]{:S(2)}, u32[]{:S(2)}) collective-permute-start(f32[512,768]{1,0:T(8,128)S(1)} %feature_terms.1.refs_2_.refs_0_), channel_id=1, source_target_pairs={{0,1},{1,0},{2,3},{3,2},{4,5},{5,4},{6,7},{7,6},{8,9},{9,8},{10,11... | collective-permute-start | bytes 4718600 | tf_op jit(solution)/shard_map/ppermute | solution.py:119
  152.8 6.0 %collective-permute-start.25 = (bf16[288,384]{1,0:T(8,128)(2,1)S(1)}, bf16[288,384]{1,0:T(8,128)(2,1)S(1)}, u32[]{:S(2)}, u32[]{:S(2)}) collective-permute-start(bf16[288,384]{1,0:T(8,128)(2,1)S(1)} %join.10.refs_2_.refs_0_), channel_id=1, source_target_pairs={{0,8},{1,9},{2,10},{3,11},{4,12},{5,13},{6,14},{7,15},{8,0},{9,1},... | collective-permute-start | bytes 663560 | tf_op jit(solution)/shard_map/ppermute | solution.py:119
  159.4 13.2 %collective-permute-start.29 = (bf16[576,384]{1,0:T(8,128)(2,1)S(1)}, bf16[576,384]{1,0:T(8,128)(2,1)S(1)}, u32[]{:S(2)}, u32[]{:S(2)}) collective-permute-start(bf16[576,384]{1,0:T(8,128)(2,1)S(1)} %join.12.refs_2_.refs_0_), channel_id=1, source_target_pairs={{0,2},{1,5},{2,0},{3,7},{4,6},{5,1},{6,4},{7,3},{8,10},{9,13},{10,... | collective-permute-start | bytes 1327112 | tf_op jit(solution)/shard_map/ppermute | solution.py:119
  161.3 7.8 %collective-permute-start.24 = (bf16[256,768]{1,0:T(8,128)(2,1)S(1)}, bf16[256,768]{1,0:T(8,128)(2,1)S(1)}, u32[]{:S(2)}, u32[]{:S(2)}) collective-permute-start(bf16[256,768]{1,0:T(8,128)(2,1)S(1)} %get-tuple-element.82.refs_2_), channel_id=1, source_target_pairs={{0,8},{1,9},{2,10},{3,11},{4,12},{5,13},{6,14},{7,15},{8,0},{9,1},... | collective-permute-start | bytes 1179656 | tf_op jit(solution)/shard_map/ppermute | solution.py:119
  161.3 16.4 %collective-permute-start.28 = (bf16[1152,384]{1,0:T(8,128)(2,1)S(1)}, bf16[1152,384]{1,0:T(8,128)(2,1)S(1)}, u32[]{:S(2)}, u32[]{:S(2)}) collective-permute-start(bf16[1152,384]{1,0:T(8,128)(2,1)S(1)} %join.11.refs_2_.refs_0_), channel_id=1, source_target_pairs={{0,4},{1,3},{2,6},{3,1},{4,0},{5,7},{6,2},{7,5},{8,12},{9,11},{10,... | collective-permute-start | bytes 2654216 | tf_op jit(solution)/shard_map/ppermute | solution.py:119
  173.2 19.0 %collective-permute-start.32 = (bf16[1152,384]{1,0:T(8,128)(2,1)S(1)}, bf16[1152,384]{1,0:T(8,128)(2,1)S(1)}, u32[]{:S(2)}, u32[]{:S(2)}) collective-permute-start(bf16[1152,384]{1,0:T(8,128)(2,1)S(1)} %join.13.refs_2_.refs_0_), channel_id=1, source_target_pairs={{0,4},{1,3},{2,6},{3,1},{4,0},{5,7},{6,2},{7,5},{8,12},{9,11},{10,... | collective-permute-start | bytes 2654216 | tf_op jit(solution)/shard_map/ppermute | solution.py:119
  175.8 8.7 %collective-permute-start.27 = (bf16[128,768]{1,0:T(8,128)(2,1)S(1)}, bf16[128,768]{1,0:T(8,128)(2,1)S(1)}, u32[]{:S(2)}, u32[]{:S(2)}) collective-permute-start(bf16[128,768]{1,0:T(8,128)(2,1)S(1)} %get-tuple-element.84.refs_2_), channel_id=1, source_target_pairs={{0,16},{1,17},{2,18},{3,19},{4,20},{5,21},{6,22},{7,23},{8,24},{9,... | collective-permute-start | bytes 589832 | tf_op jit(solution)/shard_map/ppermute | solution.py:119
  184.5 3.0 %copy-start = (f32[3,768,768]{2,1,0:T(8,128)S(1)}, f32[3,768,768]{2,1,0:T(8,128)}, u32[]{:S(2)}) copy-start(f32[3,768,768]{2,1,0:T(8,128)} %assemble.2.refs_2_) | copy-start | bytes 21233668
  188.1 1.7 collective-permute-start.30
  189.7 1.1 copy-start.7
  192.2 1.0 copy-start.8

commit v3 on v0

v3 whole, which is shorter than its diff:
```python
import functools

import jax
import jax.numpy as jnp
from jax import lax
from jax.experimental import pallas as pl
from jax.experimental.pallas import tpu as pltpu
from jax.sharding import PartitionSpec as P

BF = jnp.bfloat16
F32 = jnp.float32
AXES = ("node", "rel")
DEPTH, SIDE = 4, 2
CHUNKS = 2
LIMIT = 24
ROUNDS = (
    (((0, 0),), (2,)),
    (((1, 0), (0, 1),), (3,)),
    (((0, 2), (1, 1), ("back", 0),), (1,)),
    (((0, 3), (1, 2), ("back", 2), ("back", 1),), (0,)),
    (((0, 4), (1, 3), ("back", 3), ("back", 4), ("rows", 0),), ()),
    (((0, 5), (1, 4), ("back", 5),), ()),
    (((0, 6), (1, 5), ("back", 6), ("rows", 1),), ()),
    (((1, 6), ("rows", 2),), ()),
    ((("rows", 3),), ()),
    ((("rows", 4),), ()),
)
NODES_HERE = DEPTH * SIDE * SIDE


def dot(a, b, dims=((1,), (0,))):
    return lax.dot_general(a, b, (dims, ((), ())), preferred_element_type=F32)


def call(name, kernel, pos, ins, outs, grid=(1,), after=(), alias=None, limit=24, scratch=()):
    def spec(block, index):
        if block is None:
            return pl.BlockSpec(memory_space=pl.ANY)
        if index is None:
            return pl.BlockSpec(block, lambda *_: (0,) * len(block))
        return pl.BlockSpec(block, index)

    many = len(ins)

    def run(pos_ref, *refs):
        kernel(pos_ref, *refs[:many], *refs[many + len(after) :])

    return pl.pallas_call(
        run,
        grid_spec=pltpu.PrefetchScalarGridSpec(
            num_scalar_prefetch=1,
            grid=grid,
            in_specs=[spec(block, index) for _, block, index in ins]
            + [pl.BlockSpec(memory_space=pl.ANY)] * len(after),
            out_specs=[spec(block, index) for _, _, block, index in outs],
            scratch_shapes=scratch,
        ),
        out_shape=[jax.ShapeDtypeStruct(shape, dtype) for shape, dtype, _, _ in outs],
        input_output_aliases=alias or {},
        compiler_params=pltpu.CompilerParams(
            dimension_semantics=("arbitrary",) * len(grid), vmem_limit_bytes=limit * 1024 * 1024
        ),
        cost_estimate=pl.CostEstimate(flops=1000, bytes_accessed=1000, transcendentals=0),
        name=name,
    )(pos, *[array for array, _, _ in ins], *after)


def full(array):
    return (array, array.shape, None)


def out(shape, dtype):
    return (shape, dtype, shape, None)


def together(pos, jobs, after):
    ins = [entry for _, job_ins, _, _ in jobs for entry in job_ins]
    outs = [entry for _, _, job_outs, _ in jobs for entry in job_outs]
    spans, alias, i, o = [], {}, 0, 0
    for _, job_ins, job_outs, job_alias in jobs:
        spans.append((i, i + len(job_ins), o, o + len(job_outs)))
        alias.update({1 + i + source: o + target for source, target in job_alias.items()})
        i, o = spans[-1][1], spans[-1][3]

    def kernel(pos_ref, *refs):
        for (work, _, _, _), (a, b, c, d) in zip(jobs, spans):
            work(pos_ref, *refs[a:b], *refs[len(ins) + c : len(ins) + d])

    results = call("step", kernel, pos, ins, outs, after=after, alias=alias, limit=LIMIT)
    return [results[c:d] for _, _, c, d in spans]


def gate_job(arrays):
    return (
        lambda *_: None,
        [(array, None, None) for array in arrays],
        [(array.shape, array.dtype, None, None) for array in arrays],
        {i: i for i in range(len(arrays))},
    )


def pairs(move):
    listed = []
    for node in range(NODES_HERE):
        for core in range(2):
            z, y, x = node // 4, node // 2 % 2, node % 2
            tz, ty, tx, tc = move(z, y, x, core)
            listed.append((node * 2 + core, (tz * 4 + ty * 2 + tx) * 2 + tc))
    return listed


FIRST = pairs(lambda z, y, x, c: (z, y ^ (1 - c), x ^ c, c))
SECOND = pairs(lambda z, y, x, c: (z, y ^ c, x ^ (1 - c), c))
ALONG = [pairs(lambda z, y, x, c, k=k: (z ^ k, y, x, c)) for k in range(DEPTH)]
LINE = (0, 2, 1, 3)
CORES = pairs(lambda z, y, x, c: (z, y, x, 1 - c))


def hop(array, table):
    return lax.ppermute(array, AXES, table)


def by_rel(array):
    return (array, (1,) + array.shape[1:], lambda r, pos: (r, 0, 0))


def out_by_rel(groups, rows, width, dtype):
    return ((groups, rows, width), dtype, (1, rows, width), lambda r, pos: (r, 0, 0))


def join_kernel(pos, *refs):
    start = 0
    for ref in refs[:-1]:
        refs[-1][start : start + ref.shape[0], :] = ref[...]
        start += ref.shape[0]


def copy_kernel(pos, source, target):
    target[...] = source[...]


def join_job(pieces):
    shape = (sum(piece.shape[0] for piece in pieces), pieces[0].shape[1])
    return (join_kernel, [full(piece) for piece in pieces], [out(shape, BF)], {})


def one_hot(values, places):
    return (values == places).astype(F32).astype(BF)


def partial_step(pos, core, first, second, batch, dst, sent, local):
    half = batch // 2
    rows = lax.broadcasted_iota(jnp.int32, (half, dst.shape[1]), 0)
    hot = []
    for depth in LINE:
        base = owner_of(pos, core, first, second, depth) * batch + core * half
        hot.append(one_hot(dst[...] - base, rows))
    total = dot(jnp.concatenate(hot, axis=0), sent[...])
    own = local[pl.ds(pl.multiple_of(core * half, half), half), :]
    here = (first + second == 0).astype(F32)
    return jnp.concatenate([total[:half] + here * own, total[half:]], axis=0)


def one_hot(values, places):
    return (values == places).astype(F32).astype(BF)


FIELDS = 4
EXTRA = 16
PART = 256


def fields(block, rel, count):
    places = lax.broadcasted_iota(jnp.int32, block.shape, 0)
    rows = [
        jnp.sum(jnp.where(places == rel * FIELDS + f, block, 0.0), axis=0, keepdims=True)
        for f in range(FIELDS)
    ]
    return [row[:, :count].astype(jnp.int32) for row in rows]


def prepare_kernel(pos, feat, hist, numbers, cot, mine, theirs, line):
    half = feat.shape[0] // 2
    for ref, core in ((mine, pos[3]), (theirs, 1 - pos[3])):
        span = pl.ds(pl.multiple_of(core * half, half), half)
        deltas = feat[span, :].astype(F32) - hist[span, :].astype(F32)
        ref[:half, :] = deltas.astype(BF)
        ref[half:, :] = jnp.zeros((EXTRA, ref.shape[1]), BF)
        ref[half:, : numbers.shape[1]] = numbers[...]
    half = line.shape[0]
    line[...] = cot[pl.ds(pl.multiple_of(pos[3] * half, half), half), :]


def prepare(pos, features, history, numbers, cot):
    nodes, width = features.shape
    shape = (nodes // 2 + EXTRA, width)
    return call(
        "prepare",
        prepare_kernel,
        pos,
        [full(features), full(history), full(numbers), full(cot)],
        [out(shape, BF), out(shape, BF), out((cot.shape[0] // 2, width), BF)],
        limit=24,
    )


def gather_step(pos, rel, msgs, mine, theirs):
    half = mine.shape[0] - EXTRA
    _, _, low, high = fields(mine[half:, :].astype(F32), rel, msgs)
    column = jnp.transpose(jnp.broadcast_to(low + PART * high, (128, msgs)))
    lanes = lax.broadcasted_iota(jnp.int32, (msgs, 128), 1)
    total = None
    for ref, core in ((mine, pos[3]), (theirs, 1 - pos[3])):
        hot = [one_hot(column, lanes + (core * half + n)) for n in range(0, half, 128)]
        term = dot(jnp.concatenate(hot, axis=1), ref[:half, :])
        total = term if total is None else total + term
    return total.astype(BF)


def gather_kernel(msgs, pos, *refs):
    result = refs[-1]
    for n in range(len(refs) // 2):
        result[0, n * msgs : (n + 1) * msgs, :] = gather_step(
            pos, pl.program_id(0), msgs, refs[2 * n], refs[2 * n + 1]
        )


def gather(pos, groups, msgs, pieces, places, after):
    rows, width = pieces[0].shape
    return call(
        "gather",
        functools.partial(gather_kernel, msgs),
        pos,
        [
            (piece, (rows, width), lambda r, pos, place=place: (place, 0))
            for piece, place in zip(pieces, places)
        ],
        [out_by_rel(groups, len(pieces) // 2 * msgs, width, BF)],
        grid=(groups,),
        after=after,
        limit=24,
    )[0]


def bases(pos, batch):
    half = batch // 2
    for core in (pos[3], 1 - pos[3]):
        for depth in LINE:
            owner = (pos[0] ^ depth) * SIDE * SIDE + pos[1] * SIDE + pos[2]
            yield owner * batch + core * half


def aggregate_part(scale, pos, batch, payloads, moved, side):
    rel = pl.program_id(0)
    half = batch // 2
    msgs = moved.shape[0] // len(payloads)
    dst = []
    for ref in payloads:
        owner, row, _, _ = fields(ref[ref.shape[0] - EXTRA :, :].astype(F32), rel, msgs)
        dst.append(owner * batch + row)
    dst = jnp.concatenate(dst, axis=1)
    rows = lax.broadcasted_iota(jnp.int32, (half, dst.shape[1]), 0)
    places = list(bases(pos, batch))[side * DEPTH : (side + 1) * DEPTH]
    hot = [one_hot(dst - base, rows) for base in places]
    return scale * dot(jnp.concatenate(hot, axis=0), moved)


def aggregate_near_kernel(scale, pos, own, near_a, near_b, one, two, mean, result):
    batch = mean.shape[1]
    half = batch // 2
    moved = jnp.concatenate([one[0], two[0]], axis=0)
    for side in range(2):
        total = aggregate_part(scale, pos, batch, [own, near_a, near_b], moved, side)
        core = pos[3] if side == 0 else 1 - pos[3]
        own_mean = mean[0, pl.ds(pl.multiple_of(core * half, half), half), :].astype(F32)
        at = side * DEPTH * half
        result[0, at : at + half, :] = total[:half] + own_mean
        result[0, at + half : at + DEPTH * half, :] = total[half:]


def aggregate_near(pos, mean, payloads, moved, scale, after):
    groups, batch, width = mean.shape
    return call(
        "aggregate_near",
        functools.partial(aggregate_near_kernel, scale),
        pos,
        [full(p) for p in payloads] + [by_rel(m) for m in moved] + [by_rel(mean)],
        [out_by_rel(groups, DEPTH * batch, width, F32)],
        grid=(groups,),
        after=after,
        limit=32,
    )[0]


def aggregate_kernel(scale, msgs, batch, pos, near_ab, far_ab, before, result):
    moved = gather_step(pos, pl.program_id(0), msgs, near_ab, far_ab)
    rows = DEPTH * batch // 2
    for side in range(2):
        span = slice(side * rows, (side + 1) * rows)
        total = aggregate_part(scale, pos, batch, [near_ab], moved, side)
        result[0, span, :] = (total + before[0, span, :]).astype(BF)


def aggregate(pos, msgs, batch, near_ab, far_ab, before, scale, after):
    groups, rows, width = before.shape
    return call(
        "aggregate",
        functools.partial(aggregate_kernel, scale, msgs, batch),
        pos,
        [full(near_ab), full(far_ab), by_rel(before)],
        [out_by_rel(groups, rows, width, BF)],
        grid=(groups,),
        after=after,
        limit=32,
    )[0]


def output_kernel(pos, sums, weight, result):
    total = dot(sums[0], weight[0])
    for rel in range(1, sums.shape[0]):
        total = total + dot(sums[rel], weight[rel])
    result[...] = total.astype(result.dtype)


def output_terms(pos, sums, weights, side, dtype, after):
    groups, rows, width = sums.shape
    return call(
        "output_terms",
        output_kernel,
        pos,
        [(sums, (groups, rows // 2, width), lambda s, pos: (0, side, 0)), full(weights)],
        [out((rows // 2, width), dtype)],
        after=after,
        limit=24,
    )[0]


def back_kernel(scale, batch, msgs, pos, payload, line, far, weight, kept, away, total):
    rel = pl.program_id(0)
    half = line.shape[0] // DEPTH
    owner, row, low, high = fields(
        payload[payload.shape[0] - EXTRA :, :].astype(F32), rel, msgs
    )
    column = jnp.transpose(jnp.broadcast_to(owner * batch + row, (128, msgs)))
    lanes = lax.broadcasted_iota(jnp.int32, (msgs, half), 1)
    hot = [one_hot(column, lanes + base) for base in bases(pos, batch)]
    picked = dot(jnp.concatenate(hot[:DEPTH], axis=1), line[...])
    picked = picked + dot(jnp.concatenate(hot[DEPTH:], axis=1), far[...])
    grads = (scale * dot(picked.astype(BF), weight[0], ((1,), (1,)))).astype(BF)
    rows = lax.broadcasted_iota(jnp.int32, (total.shape[0], msgs), 0)
    term = dot(one_hot(low + PART * high, rows), grads)

    @pl.when(rel == 0)
    def _():
        total[...] = term

    @pl.when(rel > 0)
    def _():
        total[...] += term

    @pl.when(rel == pl.num_programs(0) - 1)
    def _():
        size = kept.shape[0]
        kept[...] = total[pl.ds(pl.multiple_of(pos[3] * size, size), size), :]
        away[...] = total[pl.ds(pl.multiple_of((1 - pos[3]) * size, size), size), :].astype(BF)


def back_terms(pos, batch, msgs, payload, line, far, weights, scale, after):
    groups, width, _ = weights.shape
    half = payload.shape[0] - EXTRA
    return call(
        "feature_terms",
        functools.partial(back_kernel, scale, batch, msgs),
        pos,
        [full(payload), full(line), full(far), by_rel(weights)],
        [out((half, width), F32), out((half, width), BF)],
        grid=(groups,),
        after=after,
        scratch=[pltpu.VMEM((2 * half, width), F32)],
        limit=24,
    )


def sum_kernel(pos, *refs):
    total = refs[0][...].astype(F32)
    for ref in refs[1:-1]:
        total = total + ref[...].astype(F32)
    refs[-1][...] = total.astype(refs[-1].dtype)


def sum_rows_job(terms, dtype):
    shape = terms[0][0].shape
    ins = [(array, shape, lambda s, pos, place=place: (place, 0)) for array, place in terms]
    return (sum_kernel, ins, [out(shape, dtype)], {})


def sum_pair_kernel(pos, one, two, came, result):
    rows = one.shape[0]
    result[:rows, :] = (one[...] + came[:rows, :].astype(F32)).astype(BF)
    result[rows:, :] = (two[...] + came[rows:, :].astype(F32)).astype(BF)


def sum_pair_job(one, two, came):
    return (sum_pair_kernel, [full(one), full(two), full(came)], [out(came.shape, BF)], {})


def rows_fold_kernel(pos, kept, came, stay, away):
    rows = stay.shape[0]
    for ref, span in ((stay, slice(0, rows)), (away, slice(rows, 2 * rows))):
        ref[...] = (kept[span, :] + came[span, :].astype(F32)).astype(ref.dtype)


def rows_fold_job(kept, came):
    shape = (kept.shape[0] // 2, kept.shape[1])
    return (rows_fold_kernel, [full(kept), full(came)], [out(shape, F32), out(shape, BF)], {})


def line_sum_job(kept, came):
    return (sum_kernel, [full(kept), full(came)], [out(kept.shape, BF)], {})


def finish_kernel(pos, total, opposite, result):
    half = total.shape[0]
    result[pl.ds(pl.multiple_of(pos[3] * half, half), half), :] = total[...]
    result[pl.ds(pl.multiple_of((1 - pos[3]) * half, half), half), :] = opposite[...]


def finish_job(total, opposite):
    shape = (total.shape[0] * 2, total.shape[1])
    return (finish_kernel, [full(total), full(opposite)], [out(shape, BF)], {})


def weight_kernel(norm, pos, sums, line, far, away, kept):
    half = sums.shape[2] // 2
    rows = line.shape[0]
    place = jnp.where(pos[3] == 0, pos[1], pos[2])
    for ref, index in ((away, 1 - place), (kept, place)):
        columns = pl.ds(pl.multiple_of(index * half, 128), half)
        total = dot(sums[0, :rows, columns], line[...], ((0,), (0,)))
        total = total + dot(sums[0, rows:, columns], far[...], ((0,), (0,)))
        ref[0] = (norm * total).astype(ref.dtype)


def weight_terms(pos, sums, line, far, chunk, norm, after):
    groups, _, width = sums.shape
    span = width // CHUNKS
    shape = (groups, width // 2, span)
    flat = lambda array: (array, (array.shape[0], span), lambda s, pos: (0, chunk))
    block = ((1,) + shape[1:], lambda s, pos: (s, 0, 0))
    return call(
        "weight_terms",
        functools.partial(weight_kernel, norm),
        pos,
        [by_rel(sums), flat(line), flat(far)],
        [(shape, BF) + block, (shape, F32) + block],
        grid=(groups,),
        after=after,
        limit=24,
    )


PLACES = (
    lambda pos: jnp.where(pos[3] == 0, pos[2], pos[1]),
    lambda pos: pos[0] % 2,
    lambda pos: pos[0] // 2,
)


def weight_fold_kernel(place, pos, kept, came, stay, away):
    rows = stay.shape[1]
    for ref, index in ((stay, place(pos)), (away, 1 - place(pos))):
        span = pl.ds(pl.multiple_of(index * rows, 16), rows)
        ref[...] = (kept[:, span, :] + came[:, span, :].astype(F32)).astype(ref.dtype)


def weight_fold_job(kept, came, place):
    shape = (kept.shape[0], kept.shape[1] // 2, kept.shape[2])
    return (
        functools.partial(weight_fold_kernel, place),
        [full(kept), full(came)],
        [out(shape, F32), out(shape, BF)],
        {},
    )


def assemble_kernel(pos, *refs):
    result = refs[-1]
    z, y, x, core = pos[0], pos[1], pos[2], pos[3]
    first = jnp.where(core == 0, y, x)
    second = jnp.where(core == 0, x, y)
    count = pl.num_programs(0)
    rows = result.shape[1] // NODES_HERE
    for number, ref in enumerate(refs[:-1]):
        chunk, flip_a = number // 2, number % 2
        span = ref.shape[1]
        for index in range(2 * DEPTH):
            flip_b, k = index // DEPTH, LINE[index % DEPTH]
            block = ((first ^ flip_a) * 2 + (second ^ flip_b)) * DEPTH + z % 2 * 2 + z // 2
            place = block ^ (k % 2 * 2 + k // 2)
            start = (index * count + pl.program_id(0)) * rows
            result[
                0, pl.ds(pl.multiple_of(place * rows, 16), rows), chunk * span : (chunk + 1) * span
            ] = ref[pl.ds(pl.multiple_of(start, 16), rows), :].astype(F32)


def assemble(pos, pieces, groups, width):
    return call(
        "assemble",
        assemble_kernel,
        pos,
        [full(piece) for piece in pieces],
        [out_by_rel(groups, width, width, F32)],
        grid=(groups,),
        limit=24,
    )[0]


def body(
    features, history, history_mean, weights, source_rows, target_owner, target_rows, cotangent
):
    groups, width, _ = weights.shape
    batch = history_mean.shape[1]
    nodes = features.shape[0]
    msgs = source_rows.shape[1]
    owners = lax.axis_size("node")
    scale = 1.0 / (msgs // batch)
    dst = target_owner[:, :, 0] * batch + target_rows
    if owners != NODES_HERE:
        return anywhere(
            features, history, history_mean, weights, source_rows, dst, cotangent, scale
        )
    norm = (batch * owners) ** -0.5
    node = lax.axis_index("node")
    core = lax.axis_index("rel")
    z = node // 4
    pos = jnp.stack([z, node // 2 % 2, node % 2, core]).astype(jnp.int32)
    half = batch // 2
    swap = lambda array: hop(array, CORES)
    numbers = jnp.stack(
        [target_owner[:, :, 0], target_rows, source_rows % PART, source_rows // PART], axis=1
    )
    numbers = numbers.reshape(groups * FIELDS, msgs).astype(BF)
    numbers = jnp.concatenate([numbers, jnp.zeros((EXTRA - groups * FIELDS, msgs), BF)])

    own, theirs, mine = prepare(pos, features, history, numbers, cotangent)
    near_a, near_b = hop(own, FIRST), hop(own, SECOND)
    line_2 = hop(mine, ALONG[2])
    collect = functools.partial(gather, pos, groups, msgs)
    one = collect([own, theirs], [0, 0], [mine])
    (near,), (pair,), (near_b,) = together(
        pos, [join_job([near_a, near_b]), join_job([mine, line_2]), (copy_kernel, [full(near_b)], [out(near_b.shape, BF)], {})], [one]
    )
    near_ab, near_o, line_1 = hop(near_b, FIRST), swap(near), hop(pair, ALONG[1])
    two = collect([near_a, near_o, near_b, near_o], [0, 1, 0, 0], [near_b])
    ((near_ab,),) = together(pos, [gate_job([near_ab])], [two])
    far_ab = swap(near_ab)
    sums = aggregate_near(
        pos, history_mean, [own, near_a, near_b], [one, two], scale, [near_ab]
    )
    ((line,),) = together(pos, [join_job([pair, line_1])], [sums, far_ab])
    far = swap(line)
    sums = aggregate(pos, msgs, batch, near_ab, far_ab, sums, scale, [line])
    plane = [own, near_a, near_b, near_ab]

    chunks = [{"index": index} for index in range(CHUNKS)]
    last = sums
    for chunk in chunks:
        chunk["away"], chunk["kept"] = weight_terms(
            pos, sums, line, far, chunk["index"], norm, [last]
        )
        last = chunk["away"]
        chunk["came"] = hop(chunk["away"], FIRST)
        if chunk["index"] == 0:
            theirs = output_terms(pos, sums, weights, 1, BF, [last])
            last = output = output_terms(pos, sums, weights, 0, F32, [theirs])
    state, grown, given = {"away": theirs, "kept": output}, {}, {}
    ways = (SECOND, ALONG[1], ALONG[2])

    def weight_step(chunk, step):
        if step < 3:

            def sent(kept, away):
                chunk["kept"], chunk["came"] = kept, hop(away, ways[step])

            return weight_fold_job(chunk["kept"], chunk["came"], PLACES[step]), sent
        if step == 3:

            def summed(total):
                total = total.reshape(-1, total.shape[2])
                chunk["line"] = [total, hop(total, ALONG[2])]

            return line_sum_job(chunk["kept"], chunk["came"]), summed

        def joined(line):
            chunk["line"] = [line, hop(line, (ALONG[1], SECOND, FIRST)[step - 4])]

        return join_job(chunk["line"]), joined

    def rows_step(step):
        if step == 0:
            return gate_job([state["away"]]), lambda away: state.update(rows=swap(away))
        if step < 3:

            def sent(kept, away):
                state.update(kept=kept, rows=hop(away, ways[step]))

            return rows_fold_job(state["kept"], state["rows"]), sent
        if step == 3:
            job = line_sum_job(state["kept"], state["rows"])
            return job, lambda total: state.update(total=total, opposite=swap(total))
        job = finish_job(state["total"], state["opposite"])
        return job, lambda rows: state.update(out=rows)

    def back_step(step):
        if step == 0:
            job = join_job([given[2], given[3]])
            return job, lambda away: state.update(far=swap(away))
        if step == 1:
            return gate_job([given[1]]), lambda away: state.update(far_2=swap(away))
        if step == 2:
            job = sum_pair_job(grown[1], grown[3], state["far"])
            return job, lambda away: state.update(first=hop(away, FIRST))
        if step == 3:
            job = sum_rows_job([(grown[2], 0), (state["far_2"], 0), (state["first"], 1)], BF)
            return job, lambda away: state.update(second=hop(away, SECOND))
        if step == 4:
            return gate_job([given[0]]), lambda away: state.update(far_0=swap(away))
        if step == 5:
            terms = [(grown[0], 0), (state["far_0"], 0), (state["first"], 0), (state["second"], 0)]
            job = sum_rows_job(terms, BF)
            return job, lambda own: state.update(own=own, own_o=swap(own))
        job = finish_job(state["own"], state["own_o"])
        return job, lambda rows: state.update(back=rows)

    for steps, covers in ROUNDS:
        planned = []
        for what, step in steps:
            if what == "rows":
                planned.append(rows_step(step))
            elif what == "back":
                planned.append(back_step(step))
            else:
                planned.append(weight_step(chunks[what], step))
        results = together(pos, [job for job, _ in planned], [last])
        for (_, then), result in zip(planned, results):
            then(*result)
        last = results[0][0]
        for cover in covers:
            grown[cover], given[cover] = back_terms(
                pos, batch, msgs, plane[cover], line, far, weights, scale, [last]
            )
            last = grown[cover]
    pieces = [piece for chunk in chunks for piece in chunk["line"]]
    return state["out"], assemble(pos, pieces, groups, width), state["back"]


def anywhere(features, history, history_mean, weights, source_rows, dst, cotangent, scale):
    groups, width, _ = weights.shape
    batch, nodes = cotangent.shape[0], features.shape[0]
    total_batch = batch * lax.axis_size("node")
    deltas = (features.astype(F32) - history.astype(F32)).astype(BF)
    every = lax.all_gather(cotangent, "node", tiled=True)
    out = jnp.zeros((total_batch, width), F32)
    local = jnp.zeros((batch, width), F32)
    terms = jnp.zeros((nodes, width), F32)
    grads = []
    for rel in range(groups):
        rows = jnp.take(deltas, source_rows[rel], axis=0)
        picked = jnp.take(every, dst[rel], axis=0)
        out = out.at[dst[rel]].add(scale * dot(rows, weights[rel]))
        local = local + dot(history_mean[rel], weights[rel])
        edge = (scale * dot(picked, weights[rel], ((1,), (1,)))).astype(BF)
        terms = terms.at[source_rows[rel]].add(edge.astype(F32))
        grads.append(
            dot(history_mean[rel], cotangent, ((0,), (0,)))
            + scale * dot(rows, picked, ((0,), (0,)))
        )
    layer_out = lax.psum(lax.psum_scatter(out, "node", tiled=True) + local, "rel").astype(BF)
    weight_grads = lax.psum(jnp.stack(grads) * total_batch**-0.5, "node")
    return layer_out, weight_grads, lax.psum(terms, "rel").astype(BF)


def solution(mesh):
    in_specs = (
        P("node", None),
        P("node", None),
        P("rel", "node", None),
        P("rel", None, None),
        P("rel", "node"),
        P("rel", "node", None),
        P("rel", "node"),
        P("node", None),
    )
    out_specs = (P("node", None), P("rel", None, None), P("node", None))
    return jax.shard_map(body, mesh=mesh, in_specs=in_specs, out_specs=out_specs, check_vma=False)
```

time: 558 us -> 174 us (0.31)
  waiting for transfers between devices: 389 us -> 55.7 us
  Pallas kernels: 0 us -> 81.4 us
  local copies, waits for them, and re-layouts: 46.5 us -> 3.3 us
  matrix products: 32 us -> 0 us
  other arithmetic: 20.7 us -> 1.53 us
  between operations: 14.2 us -> 1.03 us
  starting transfers between devices: 42.6 us -> 30.4 us
  blocking collectives: 10.5 us -> 0 us
    all_to_all x3 -> x0, waiting for transfers between devices: 242 us -> none  [the longest x1 152 us: body(): lax.all_to_all(grad_rows.reshape(groups, owners, capacity, width), 'node'...]
    psum x1 -> x0, waiting for transfers between devices: 147 us -> none  [body(): weight_grads = lax.psum(local_grads, 'node')]
    pallas_call x0 -> x27, Pallas kernels: none -> 81.4 us  [call(): pl.pallas_call(run, grid_spec=pltpu.PrefetchScalarGridSpec(num_scalar_pre...]
    ppermute x0 -> x34, waiting for transfers between devices: none -> 55.7 us  [hop(): return lax.ppermute(array, AXES, table)]
    all_to_all x3 -> x0, starting transfers between devices: 42.4 us -> none  [the longest x1 27.1 us: body(): lax.all_to_all(grad_rows.reshape(groups, owners, capacity, width), 'node'...]
    dot_general x6 -> x0, matrix products: 32 us -> none  [the longest x1 9.09 us: body(): jnp.einsum('rmu,rmd->ud', source_hot, edge_grads, preferred_element_type=...]
    ppermute x0 -> x34, starting transfers between devices: none -> 30.4 us  [hop(): return lax.ppermute(array, AXES, table)]
    all_to_all x4 -> x0, local copies, waits for them, and re-layouts: 10.8 us -> none  [the longest x1 5.73 us: body(): lax.all_to_all(grad_rows.reshape(groups, owners, capacity, width), 'node'...]
  transfers between devices with their start and end apart: 4 -> 34, of which waited for: 3 -> 16; matrix products, arithmetic and copies ran while one was open for 13% -> 0% of each run, Pallas kernels for 0% -> 38%
where the time goes in v3:
time: 174 us; the launch traced here: 173 us
  Pallas kernels  81.4 us (47%)
  waiting for transfers between devices  55.7 us (32%)
  starting transfers between devices  30.4 us (17%)
  local copies, waits for them, and re-layouts  3.3 us (2%)
    pallas_call x27, Pallas kernels, call(): pl.pallas_call(run, grid_spec=pltpu.PrefetchScalarGridSpec(num_scalar_pre...  81.4 us
    ppermute x34, waiting for transfers between devices, hop(): return lax.ppermute(array, AXES, table)  55.7 us
    ppermute x34, starting transfers between devices, hop(): return lax.ppermute(array, AXES, table)  30.4 us
  transfers between devices with their start and end apart: 34, of which 16 were waited for; matrix products, arithmetic and copies ran while one was open for 0% of the time, Pallas kernels for 38%

profile of v3, /device:TPU:0, one launch (start us, length us, event | category | flops | bytes accessed | tf_op | source)
XLA Modules:
  0.0 173.4 jit_solution(16135042084550197310)
XLA Ops:
  2.3 1.1 copy-done.2
  3.4 1.1 copy-done.3
  4.6 1.0 copy-done.4
  6.3 3.0 %collective-permute-start = (bf16[272,768]{1,0:T(8,128)(2,1)S(1)}, bf16[272,768]{1,0:T(8,128)(2,1)S(1)}, u32[]{:S(2)}, u32[]{:S(2)}) collective-permute-start(bf16[272,768]{1,0:T(8,128)(2,1)S(1)} %get-tuple-element.53.refs_0_), channel_id=1, source_target_pairs={{0,4},{1,3},{2,6},{3,1},{4,0},{5,7},{6,2},{7,5},{8,12},{9,11},{10,... | collective-permute-start | bytes 1253384 | tf_op jit(solution)/shard_map/ppermute | solution.py:120
  9.3 1.5 collective-permute-start.1
  10.8 2.6 %collective-permute-start.2 = (bf16[128,768]{1,0:T(8,128)(2,1)S(1)}, bf16[128,768]{1,0:T(8,128)(2,1)S(1)}, u32[]{:S(2)}, u32[]{:S(2)}) collective-permute-start(bf16[128,768]{1,0:T(8,128)(2,1)S(1)} %get-tuple-element.54.refs_2_), channel_id=1, source_target_pairs={{0,16},{1,17},{2,18},{3,19},{4,20},{5,21},{6,22},{7,23},{8,24},{9,... | collective-permute-start | bytes 589832 | tf_op jit(solution)/shard_map/ppermute | solution.py:120
  13.4 2.5 %gather.2.refs_5_.refs_3_ = bf16[3,512,768]{2,1,0:T(8,128)(2,1)S(1)} custom-call(s32[4]{0:T(128)S(1)} %pad_add_fusion.pos_ref, bf16[272,768]{1,0:T(8,128)(2,1)S(1)} %get-tuple-element.53.refs_0_, bf16[272,768]{1,0:T(8,128)(2,1)S(1)} %get-tuple-element.55.refs_1_, bf16[128,768]{1,0:T(8,128)(2,1)S(1)} %get-tuple-element.54.refs_2_), custom_call_target="tpu_custom_call" | custom-call | flops 1000 | bytes 1000 | tf_op jit(solution)/shard_map/gather/pallas_call | solution.py:48
  15.9 6.1 %collective-permute-done.2.refs_3_ = bf16[128,768]{1,0:T(8,128)(2,1)S(1)} collective-permute-done((bf16[128,768]{1,0:T(8,128)(2,1)S(1)}, bf16[128,768]{1,0:T(8,128)(2,1)S(1)}, u32[]{:S(2)}, u32[]{:S(2)}) %collective-permute-start.2) | collective-permute-done | bytes 196640 | tf_op jit(solution)/shard_map/ppermute | solution.py:120
  23.3 1.8 %collective-permute-done.4.refs_1_.refs_3_ = bf16[544,768]{1,0:T(8,128)(2,1)S(1)} collective-permute-done((bf16[544,768]{1,0:T(8,128)(2,1)S(1)}, bf16[544,768]{1,0:T(8,128)(2,1)S(1)}, u32[]{:S(2)}, u32[]{:S(2)}) %collective-permute-start.4) | collective-permute-done | bytes 835616 | tf_op jit(solution)/shard_map/ppermute | solution.py:120
  25.1 3.7 %gather.3.refs_1_.refs_4_ = bf16[3,1024,768]{2,1,0:T(8,128)(2,1)S(1)} custom-call(s32[4]{0:T(128)S(1)} %pad_add_fusion.pos_ref, bf16[272,768]{1,0:T(8,128)(2,1)S(1)} %collective-permute-done.refs_0_.refs_1_, bf16[544,768]{1,0:T(8,128)(2,1)S(1)} %collective-permute-done.4.refs_1_.refs_3_, bf16[272,768]{1,0:T(8,128)(2,1)S(1)} %get-tuple-element.56.refs_2_.refs_4_.refs_0_, ...), custom_call_target="tpu_custom_call" | custom-call | flops 1000 | bytes 1000 | tf_op jit(solution)/shard_map/gather/pallas_call | solution.py:48
  28.8 2.0 %collective-permute-done.3.refs_0_ = bf16[272,768]{1,0:T(8,128)(2,1)S(1)} collective-permute-done((bf16[272,768]{1,0:T(8,128)(2,1)S(1)}, bf16[272,768]{1,0:T(8,128)(2,1)S(1)}, u32[]{:S(2)}, u32[]{:S(2)}) %collective-permute-start.3) | collective-permute-done | bytes 417824 | tf_op jit(solution)/shard_map/ppermute | solution.py:120
  32.2 8.5 %aggregate_near.1.refs_2_ = f32[3,1024,768]{2,1,0:T(8,128)S(1)} custom-call(s32[4]{0:T(128)S(1)} %pad_add_fusion.pos_ref, bf16[272,768]{1,0:T(8,128)(2,1)S(1)} %get-tuple-element.53.refs_0_, bf16[272,768]{1,0:T(8,128)(2,1)S(1)} %collective-permute-done.refs_0_.refs_1_, bf16[272,768]{1,0:T(8,128)(2,1)S(1)} %get-tuple-element.56.refs_2_.refs_4_.refs_0_, ...), custom_call_target="tpu_custom_call" | custom-call | flops 1000 | bytes 1000 | tf_op jit(solution)/shard_map/aggregate_near/pallas_call | solution.py:48
  40.7 2.3 %collective-permute-done.6.refs_1_ = bf16[256,768]{1,0:T(8,128)(2,1)S(1)} collective-permute-done((bf16[256,768]{1,0:T(8,128)(2,1)S(1)}, bf16[256,768]{1,0:T(8,128)(2,1)S(1)}, u32[]{:S(2)}, u32[]{:S(2)}) %collective-permute-start.6) | collective-permute-done | bytes 393248 | tf_op jit(solution)/shard_map/ppermute | solution.py:120
  43.7 5.1 %aggregate.1.refs_0_.refs_3_ = bf16[3,1024,768]{2,1,0:T(8,128)(2,1)S(1)} custom-call(s32[4]{0:T(128)S(1)} %pad_add_fusion.pos_ref, bf16[272,768]{1,0:T(8,128)(2,1)S(1)} %step.14.refs_6_.refs_0_, bf16[272,768]{1,0:T(8,128)(2,1)S(1)} %collective-permute-done.5.refs_3_.refs_1_, f32[3,1024,768]{2,1,0:T(8,128)S(1)} %aggregate_near.1.refs_2_, ...), custom_call_target="tpu_custom_call" | custom-call | flops 1000 | bytes 1000 | tf_op jit(solution)/shard_map/aggregate/pallas_call | solution.py:48
  48.9 3.7 %weight_terms.2 = (bf16[3,384,384]{2,1,0:T(8,128)(2,1)S(1)}, f32[3,384,384]{2,1,0:T(8,128)S(1)}) custom-call(s32[4]{0:T(128)S(1)} %pad_add_fusion.pos_ref, bf16[3,1024,768]{2,1,0:T(8,128)(2,1)S(1)} %aggregate.1.refs_0_.refs_3_, bf16[512,768]{1,0:T(8,128)(2,1)S(1)} %step.15.refs_3_.refs_1_, bf16[512,768]{1,0:T(8,128)(2,1)S(1)} %collective-permute-done.7.refs_2_, ...), custom_call_target="tpu_custom_call" | custom-call | flops 1000 | bytes 1000 | tf_op jit(solution)/shard_map/weight_terms/pallas_call | solution.py:48
  53.2 2.5 %output_terms.2.refs_2_.refs_8_ = bf16[512,768]{1,0:T(8,128)(2,1)S(1)} custom-call(s32[4]{0:T(128)S(1)} %pad_add_fusion.pos_ref, bf16[3,1024,768]{2,1,0:T(8,128)(2,1)S(1)} %aggregate.1.refs_0_.refs_3_, bf16[3,768,768]{2,1,0:T(8,128)(2,1)S(1)} %copy-done, bf16[3,384,384]{2,1,0:T(8,128)(2,1)S(1)} %get-tuple-element.59.refs_2_), custom_call_target="tpu_custom_call" | custom-call | flops 1000 | bytes 1000 | tf_op jit(solution)/shard_map/output_terms/pallas_call | solution.py:48
  55.7 2.5 %output_terms.3.refs_3_.refs_6_ = f32[512,768]{1,0:T(8,128)S(1)} custom-call(s32[4]{0:T(128)S(1)} %pad_add_fusion.pos_ref, bf16[3,1024,768]{2,1,0:T(8,128)(2,1)S(1)} %aggregate.1.refs_0_.refs_3_, bf16[3,768,768]{2,1,0:T(8,128)(2,1)S(1)} %copy-done, bf16[512,768]{1,0:T(8,128)(2,1)S(1)} %output_terms.2.refs_2_.refs_8_), custom_call_target="tpu_custom_call" | custom-call | flops 1000 | bytes 1000 | tf_op jit(solution)/shard_map/output_terms/pallas_call | solution.py:48
  58.3 3.7 %weight_terms.3 = (bf16[3,384,384]{2,1,0:T(8,128)(2,1)S(1)}, f32[3,384,384]{2,1,0:T(8,128)S(1)}) custom-call(s32[4]{0:T(128)S(1)} %pad_add_fusion.pos_ref, bf16[3,1024,768]{2,1,0:T(8,128)(2,1)S(1)} %aggregate.1.refs_0_.refs_3_, bf16[512,768]{1,0:T(8,128)(2,1)S(1)} %step.15.refs_3_.refs_1_, bf16[512,768]{1,0:T(8,128)(2,1)S(1)} %collective-permute-done.7.refs_2_, ...), custom_call_target="tpu_custom_call" | custom-call | flops 1000 | bytes 1000 | tf_op jit(solution)/shard_map/weight_terms/pallas_call | solution.py:48
  62.0 1.6 collective-permute-start.8
  63.6 2.1 %collective-permute-done.9.refs_1_ = bf16[3,384,384]{2,1,0:T(8,128)(2,1)S(1)} collective-permute-done((bf16[3,384,384]{2,1,0:T(8,128)(2,1)S(1)}, bf16[3,384,384]{2,1,0:T(8,128)(2,1)S(1)}, u32[]{:S(2)}, u32[]{:S(2)}) %collective-permute-start.9) | collective-permute-done | bytes 884768 | tf_op jit(solution)/shard_map/ppermute | solution.py:120
  67.0 8.6 %feature_terms.4 = (f32[256,768]{1,0:T(8,128)S(1)}, bf16[256,768]{1,0:T(8,128)(2,1)S(1)}) custom-call(s32[4]{0:T(128)S(1)} %pad_add_fusion.pos_ref, bf16[272,768]{1,0:T(8,128)(2,1)S(1)} %get-tuple-element.56.refs_2_.refs_4_.refs_0_, bf16[512,768]{1,0:T(8,128)(2,1)S(1)} %step.15.refs_3_.refs_1_, bf16[512,768]{1,0:T(8,128)(2,1)S(1)} %collective-permute-done.7.refs_2_, ...), custom_call_target="tpu_custom_call" | custom-call | flops 1000 | bytes 1000 | tf_op jit(solution)/shard_map/feature_terms/pallas_call | solution.py:48
  75.7 4.3 %collective-permute-done.8.refs_1_ = bf16[3,384,384]{2,1,0:T(8,128)(2,1)S(1)} collective-permute-done((bf16[3,384,384]{2,1,0:T(8,128)(2,1)S(1)}, bf16[3,384,384]{2,1,0:T(8,128)(2,1)S(1)}, u32[]{:S(2)}, u32[]{:S(2)}) %collective-permute-start.8) | collective-permute-done | bytes 884768 | tf_op jit(solution)/shard_map/ppermute | solution.py:120
  79.9 0.8 step.17
  81.4 0.9 collective-permute-start.11
  82.3 8.4 %feature_terms.5 = (f32[256,768]{1,0:T(8,128)S(1)}, bf16[256,768]{1,0:T(8,128)(2,1)S(1)}) custom-call(s32[4]{0:T(128)S(1)} %pad_add_fusion.pos_ref, bf16[272,768]{1,0:T(8,128)(2,1)S(1)} %step.14.refs_6_.refs_0_, bf16[512,768]{1,0:T(8,128)(2,1)S(1)} %step.15.refs_3_.refs_1_, bf16[512,768]{1,0:T(8,128)(2,1)S(1)} %collective-permute-done.7.refs_2_, ...), custom_call_target="tpu_custom_call" | custom-call | flops 1000 | bytes 1000 | tf_op jit(solution)/shard_map/feature_terms/pallas_call | solution.py:48
  91.6 1.2 collective-permute-start.14
  92.8 2.3 %collective-permute-start.13 = (bf16[3,48,384]{2,1,0:T(8,128)(2,1)S(1)}, bf16[3,48,384]{2,1,0:T(8,128)(2,1)S(1)}, u32[]{:S(2)}, u32[]{:S(2)}) collective-permute-start(bf16[3,48,384]{2,1,0:T(8,128)(2,1)S(1)} %get-tuple-element.74), channel_id=1, source_target_pairs={{0,16},{1,17},{2,18},{3,19},{4,20},{5,21},{6,22},{7,23},{8,24},{9,... | collective-permute-start | bytes 331784 | tf_op jit(solution)/shard_map/ppermute | solution.py:120
  95.1 8.4 %feature_terms.6 = (f32[256,768]{1,0:T(8,128)S(1)}, bf16[256,768]{1,0:T(8,128)(2,1)S(1)}) custom-call(s32[4]{0:T(128)S(1)} %pad_add_fusion.pos_ref, bf16[272,768]{1,0:T(8,128)(2,1)S(1)} %collective-permute-done.refs_0_.refs_1_, bf16[512,768]{1,0:T(8,128)(2,1)S(1)} %step.15.refs_3_.refs_1_, bf16[512,768]{1,0:T(8,128)(2,1)S(1)} %collective-permute-done.7.refs_2_, ...), custom_call_target="tpu_custom_call" | custom-call | flops 1000 | bytes 1000 | tf_op jit(solution)/shard_map/feature_terms/pallas_call | solution.py:48
  104.3 1.5 collective-permute-start.19
  106.5 2.3 %collective-permute-start.17 = (bf16[3,48,384]{2,1,0:T(8,128)(2,1)S(1)}, bf16[3,48,384]{2,1,0:T(8,128)(2,1)S(1)}, u32[]{:S(2)}, u32[]{:S(2)}) collective-permute-start(bf16[3,48,384]{2,1,0:T(8,128)(2,1)S(1)} %get-tuple-element.82), channel_id=1, source_target_pairs={{0,16},{1,17},{2,18},{3,19},{4,20},{5,21},{6,22},{7,23},{8,24},{9,... | collective-permute-start | bytes 331784 | tf_op jit(solution)/shard_map/ppermute | solution.py:120
  108.8 8.4 %feature_terms.7 = (f32[256,768]{1,0:T(8,128)S(1)}, bf16[256,768]{1,0:T(8,128)(2,1)S(1)}) custom-call(s32[4]{0:T(128)S(1)} %pad_add_fusion.pos_ref, bf16[272,768]{1,0:T(8,128)(2,1)S(1)} %get-tuple-element.53.refs_0_, bf16[512,768]{1,0:T(8,128)(2,1)S(1)} %step.15.refs_3_.refs_1_, bf16[512,768]{1,0:T(8,128)(2,1)S(1)} %collective-permute-done.7.refs_2_, ...), custom_call_target="tpu_custom_call" | custom-call | flops 1000 | bytes 1000 | tf_op jit(solution)/shard_map/feature_terms/pallas_call | solution.py:48
  117.3 2.0 %collective-permute-done.17.refs_3_ = bf16[3,48,384]{2,1,0:T(8,128)(2,1)S(1)} collective-permute-done((bf16[3,48,384]{2,1,0:T(8,128)(2,1)S(1)}, bf16[3,48,384]{2,1,0:T(8,128)(2,1)S(1)}, u32[]{:S(2)}, u32[]{:S(2)}) %collective-permute-start.17) | collective-permute-done | bytes 110624 | tf_op jit(solution)/shard_map/ppermute | solution.py:120
  120.1 1.6 collective-permute-start.23
  121.7 2.0 %collective-permute-start.21 = (bf16[144,384]{1,0:T(8,128)(2,1)S(1)}, bf16[144,384]{1,0:T(8,128)(2,1)S(1)}, u32[]{:S(2)}, u32[]{:S(2)}) collective-permute-start(bf16[144,384]{1,0:T(8,128)(2,1)S(1)} %bitcast.16), channel_id=1, source_target_pairs={{0,16},{1,17},{2,18},{3,19},{4,20},{5,21},{6,22},{7,23},{8,24},{9,... | collective-permute-start | bytes 331784 | tf_op jit(solution)/shard_map/ppermute | solution.py:120
  123.7 6.0 %collective-permute-done.21.refs_3_ = bf16[144,384]{1,0:T(8,128)(2,1)S(1)} collective-permute-done((bf16[144,384]{1,0:T(8,128)(2,1)S(1)}, bf16[144,384]{1,0:T(8,128)(2,1)S(1)}, u32[]{:S(2)}, u32[]{:S(2)}) %collective-permute-start.21) | collective-permute-done | bytes 110624 | tf_op jit(solution)/shard_map/ppermute | solution.py:120
  129.7 2.2 %collective-permute-done.20.refs_1_ = bf16[288,384]{1,0:T(8,128)(2,1)S(1)} collective-permute-done((bf16[288,384]{1,0:T(8,128)(2,1)S(1)}, bf16[288,384]{1,0:T(8,128)(2,1)S(1)}, u32[]{:S(2)}, u32[]{:S(2)}) %collective-permute-start.20) | collective-permute-done | bytes 221216 | tf_op jit(solution)/shard_map/ppermute | solution.py:120
  131.9 0.8 step.21
  133.6 7.5 %collective-permute-done.25.refs_3_ = bf16[288,384]{1,0:T(8,128)(2,1)S(1)} collective-permute-done((bf16[288,384]{1,0:T(8,128)(2,1)S(1)}, bf16[288,384]{1,0:T(8,128)(2,1)S(1)}, u32[]{:S(2)}, u32[]{:S(2)}) %collective-permute-start.25) | collective-permute-done | bytes 221216 | tf_op jit(solution)/shard_map/ppermute | solution.py:120
  141.1 1.7 step.22
  142.8 1.5 collective-permute-start.28
  145.2 9.2 %collective-permute-done.29.refs_3_ = bf16[256,768]{1,0:T(8,128)(2,1)S(1)} collective-permute-done((bf16[256,768]{1,0:T(8,128)(2,1)S(1)}, bf16[256,768]{1,0:T(8,128)(2,1)S(1)}, u32[]{:S(2)}, u32[]{:S(2)}) %collective-permute-start.29) | collective-permute-done | bytes 393248 | tf_op jit(solution)/shard_map/ppermute | solution.py:120
  154.4 1.3 collective-permute-done.28.refs_1_
  156.5 1.3 collective-permute-start.33
  157.7 1.2 collective-permute-start.30
  159.0 7.1 %collective-permute-done.30.refs_1_ = bf16[128,768]{1,0:T(8,128)(2,1)S(1)} collective-permute-done((bf16[128,768]{1,0:T(8,128)(2,1)S(1)}, bf16[128,768]{1,0:T(8,128)(2,1)S(1)}, u32[]{:S(2)}, u32[]{:S(2)}) %collective-permute-start.30) | collective-permute-done | bytes 196640 | tf_op jit(solution)/shard_map/ppermute | solution.py:120
  166.7 1.4 collective-permute-done.31.refs_1_
  168.2 1.3 step.25
  169.6 3.8 %assemble.1 = f32[3,768,768]{2,1,0:T(8,128)} custom-call(s32[4]{0:T(128)S(1)} %pad_add_fusion.pos_ref, bf16[1152,384]{1,0:T(8,128)(2,1)S(1)} %get-tuple-element.98.refs_4_.refs_0_, bf16[1152,384]{1,0:T(8,128)(2,1)S(1)} %collective-permute-done.32.refs_1_, bf16[1152,384]{1,0:T(8,128)(2,1)S(1)} %get-tuple-element.101.refs_2_, ...), custom_call_target="tpu_custom_call" | custom-call | flops 1000 | bytes 1000 | tf_op jit(solution)/shard_map/assemble/pallas_call | solution.py:48
  (64 shorter events, 14.5 us)
Async XLA Ops:
  2.3 1.1 copy-start.2
  3.4 1.1 copy-start.3
  4.5 1.0 copy-start.4
  6.3 15.7 %collective-permute-start = (bf16[272,768]{1,0:T(8,128)(2,1)S(1)}, bf16[272,768]{1,0:T(8,128)(2,1)S(1)}, u32[]{:S(2)}, u32[]{:S(2)}) collective-permute-start(bf16[272,768]{1,0:T(8,128)(2,1)S(1)} %get-tuple-element.53.refs_0_), channel_id=1, source_target_pairs={{0,4},{1,3},{2,6},{3,1},{4,0},{5,7},{6,2},{7,5},{8,12},{9,11},{10,... | collective-permute-start | bytes 1253384 | tf_op jit(solution)/shard_map/ppermute | solution.py:120
  9.3 12.7 %collective-permute-start.1 = (bf16[272,768]{1,0:T(8,128)(2,1)S(1)}, bf16[272,768]{1,0:T(8,128)(2,1)S(1)}, u32[]{:S(2)}, u32[]{:S(2)}) collective-permute-start(bf16[272,768]{1,0:T(8,128)(2,1)S(1)} %get-tuple-element.53.refs_0_), channel_id=1, source_target_pairs={{0,2},{1,5},{2,0},{3,7},{4,6},{5,1},{6,4},{7,3},{8,10},{9,13},{10,... | collective-permute-start | bytes 1253384 | tf_op jit(solution)/shard_map/ppermute | solution.py:120
  10.8 11.2 %collective-permute-start.2 = (bf16[128,768]{1,0:T(8,128)(2,1)S(1)}, bf16[128,768]{1,0:T(8,128)(2,1)S(1)}, u32[]{:S(2)}, u32[]{:S(2)}) collective-permute-start(bf16[128,768]{1,0:T(8,128)(2,1)S(1)} %get-tuple-element.54.refs_2_), channel_id=1, source_target_pairs={{0,16},{1,17},{2,18},{3,19},{4,20},{5,21},{6,22},{7,23},{8,24},{9,... | collective-permute-start | bytes 589832 | tf_op jit(solution)/shard_map/ppermute | solution.py:120
  22.7 2.4 %collective-permute-start.4 = (bf16[544,768]{1,0:T(8,128)(2,1)S(1)}, bf16[544,768]{1,0:T(8,128)(2,1)S(1)}, u32[]{:S(2)}, u32[]{:S(2)}) collective-permute-start(bf16[544,768]{1,0:T(8,128)(2,1)S(1)} %get-tuple-element.57), channel_id=1, source_target_pairs={{0,1},{1,0},{2,3},{3,2},{4,5},{5,4},{6,7},{7,6},{8,9},{9,8},{10,11... | collective-permute-start | bytes 2506760 | tf_op jit(solution)/shard_map/ppermute | solution.py:120
  22.7 8.1 %collective-permute-start.3 = (bf16[272,768]{1,0:T(8,128)(2,1)S(1)}, bf16[272,768]{1,0:T(8,128)(2,1)S(1)}, u32[]{:S(2)}, u32[]{:S(2)}) collective-permute-start(bf16[272,768]{1,0:T(8,128)(2,1)S(1)} %get-tuple-element.56.refs_2_.refs_4_.refs_0_), channel_id=1, source_target_pairs={{0,4},{1,3},{2,6},{3,1},{4,0},{5,7},{6,2},{7,5},{8,12},{9,11},{10,... | collective-permute-start | bytes 1253384 | tf_op jit(solution)/shard_map/ppermute | solution.py:120
  28.8 3.4 %copy-start.1 = (bf16[3,256,768]{2,1,0:T(8,128)(2,1)S(1)}, bf16[3,256,768]{2,1,0:T(8,128)(2,1)}, u32[]{:S(2)}) copy-start(bf16[3,256,768]{2,1,0:T(8,128)(2,1)} %refs_5_.1) | copy-start | bytes 3538948
  31.4 11.6 %collective-permute-start.5 = (bf16[272,768]{1,0:T(8,128)(2,1)S(1)}, bf16[272,768]{1,0:T(8,128)(2,1)S(1)}, u32[]{:S(2)}, u32[]{:S(2)}) collective-permute-start(bf16[272,768]{1,0:T(8,128)(2,1)S(1)} %step.14.refs_6_.refs_0_), channel_id=1, source_target_pairs={{0,1},{1,0},{2,3},{3,2},{4,5},{5,4},{6,7},{7,6},{8,9},{9,8},{10,11... | collective-permute-start | bytes 1253384 | tf_op jit(solution)/shard_map/ppermute | solution.py:120
  31.5 11.5 %collective-permute-start.6 = (bf16[256,768]{1,0:T(8,128)(2,1)S(1)}, bf16[256,768]{1,0:T(8,128)(2,1)S(1)}, u32[]{:S(2)}, u32[]{:S(2)}) collective-permute-start(bf16[256,768]{1,0:T(8,128)(2,1)S(1)} %get-tuple-element.58.refs_0_), channel_id=1, source_target_pairs={{0,8},{1,9},{2,10},{3,11},{4,12},{5,13},{6,14},{7,15},{8,0},{9,1},... | collective-permute-start | bytes 1179656 | tf_op jit(solution)/shard_map/ppermute | solution.py:120
  43.6 5.2 %collective-permute-start.7 = (bf16[512,768]{1,0:T(8,128)(2,1)S(1)}, bf16[512,768]{1,0:T(8,128)(2,1)S(1)}, u32[]{:S(2)}, u32[]{:S(2)}) collective-permute-start(bf16[512,768]{1,0:T(8,128)(2,1)S(1)} %step.15.refs_3_.refs_1_), channel_id=1, source_target_pairs={{0,1},{1,0},{2,3},{3,2},{4,5},{5,4},{6,7},{7,6},{8,9},{9,8},{10,11... | collective-permute-start | bytes 2359304 | tf_op jit(solution)/shard_map/ppermute | solution.py:120
  48.8 4.4 %copy-start = (bf16[3,768,768]{2,1,0:T(8,128)(2,1)S(1)}, bf16[3,768,768]{2,1,0:T(8,128)(2,1)}, u32[]{:S(2)}) copy-start(bf16[3,768,768]{2,1,0:T(8,128)(2,1)} %refs_3_.9) | copy-start | bytes 10616836
  52.6 13.1 %collective-permute-start.9 = (bf16[3,384,384]{2,1,0:T(8,128)(2,1)S(1)}, bf16[3,384,384]{2,1,0:T(8,128)(2,1)S(1)}, u32[]{:S(2)}, u32[]{:S(2)}) collective-permute-start(bf16[3,384,384]{2,1,0:T(8,128)(2,1)S(1)} %get-tuple-element.59.refs_2_), channel_id=1, source_target_pairs={{0,4},{1,3},{2,6},{3,1},{4,0},{5,7},{6,2},{7,5},{8,12},{9,11},{10,... | collective-permute-start | bytes 2654216 | tf_op jit(solution)/shard_map/ppermute | solution.py:120
  62.0 17.9 %collective-permute-start.8 = (bf16[3,384,384]{2,1,0:T(8,128)(2,1)S(1)}, bf16[3,384,384]{2,1,0:T(8,128)(2,1)S(1)}, u32[]{:S(2)}, u32[]{:S(2)}) collective-permute-start(bf16[3,384,384]{2,1,0:T(8,128)(2,1)S(1)} %get-tuple-element.61.refs_2_), channel_id=1, source_target_pairs={{0,4},{1,3},{2,6},{3,1},{4,0},{5,7},{6,2},{7,5},{8,12},{9,11},{10,... | collective-permute-start | bytes 2654216 | tf_op jit(solution)/shard_map/ppermute | solution.py:120
  66.4 13.5 %collective-permute-start.10 = (bf16[3,192,384]{2,1,0:T(8,128)(2,1)S(1)}, bf16[3,192,384]{2,1,0:T(8,128)(2,1)S(1)}, u32[]{:S(2)}, u32[]{:S(2)}) collective-permute-start(bf16[3,192,384]{2,1,0:T(8,128)(2,1)S(1)} %get-tuple-element.64), channel_id=1, source_target_pairs={{0,2},{1,5},{2,0},{3,7},{4,6},{5,1},{6,4},{7,3},{8,10},{9,13},{10,... | collective-permute-start | bytes 1327112 | tf_op jit(solution)/shard_map/ppermute | solution.py:120
  80.8 10.0 %collective-permute-start.12 = (bf16[3,192,384]{2,1,0:T(8,128)(2,1)S(1)}, bf16[3,192,384]{2,1,0:T(8,128)(2,1)S(1)}, u32[]{:S(2)}, u32[]{:S(2)}) collective-permute-start(bf16[3,192,384]{2,1,0:T(8,128)(2,1)S(1)} %get-tuple-element.69), channel_id=1, source_target_pairs={{0,2},{1,5},{2,0},{3,7},{4,6},{5,1},{6,4},{7,3},{8,10},{9,13},{10,... | collective-permute-start | bytes 1327112 | tf_op jit(solution)/shard_map/ppermute | solution.py:120
  81.4 9.4 %collective-permute-start.11 = (bf16[3,96,384]{2,1,0:T(8,128)(2,1)S(1)}, bf16[3,96,384]{2,1,0:T(8,128)(2,1)S(1)}, u32[]{:S(2)}, u32[]{:S(2)}) collective-permute-start(bf16[3,96,384]{2,1,0:T(8,128)(2,1)S(1)} %get-tuple-element.67), channel_id=1, source_target_pairs={{0,8},{1,9},{2,10},{3,11},{4,12},{5,13},{6,14},{7,15},{8,0},{9,1},... | collective-permute-start | bytes 663560 | tf_op jit(solution)/shard_map/ppermute | solution.py:120
  91.5 12.0 %collective-permute-start.15 = (bf16[512,768]{1,0:T(8,128)(2,1)S(1)}, bf16[512,768]{1,0:T(8,128)(2,1)S(1)}, u32[]{:S(2)}, u32[]{:S(2)}) collective-permute-start(bf16[512,768]{1,0:T(8,128)(2,1)S(1)} %get-tuple-element.78), channel_id=1, source_target_pairs={{0,1},{1,0},{2,3},{3,2},{4,5},{5,4},{6,7},{7,6},{8,9},{9,8},{10,11... | collective-permute-start | bytes 2359304 | tf_op jit(solution)/shard_map/ppermute | solution.py:120
  91.6 11.9 %collective-permute-start.14 = (bf16[3,96,384]{2,1,0:T(8,128)(2,1)S(1)}, bf16[3,96,384]{2,1,0:T(8,128)(2,1)S(1)}, u32[]{:S(2)}, u32[]{:S(2)}) collective-permute-start(bf16[3,96,384]{2,1,0:T(8,128)(2,1)S(1)} %get-tuple-element.76), channel_id=1, source_target_pairs={{0,8},{1,9},{2,10},{3,11},{4,12},{5,13},{6,14},{7,15},{8,0},{9,1},... | collective-permute-start | bytes 663560 | tf_op jit(solution)/shard_map/ppermute | solution.py:120
  92.8 10.8 %collective-permute-start.13 = (bf16[3,48,384]{2,1,0:T(8,128)(2,1)S(1)}, bf16[3,48,384]{2,1,0:T(8,128)(2,1)S(1)}, u32[]{:S(2)}, u32[]{:S(2)}) collective-permute-start(bf16[3,48,384]{2,1,0:T(8,128)(2,1)S(1)} %get-tuple-element.74), channel_id=1, source_target_pairs={{0,16},{1,17},{2,18},{3,19},{4,20},{5,21},{6,22},{7,23},{8,24},{9,... | collective-permute-start | bytes 331784 | tf_op jit(solution)/shard_map/ppermute | solution.py:120
  104.3 15.0 %collective-permute-start.19 = (bf16[512,768]{1,0:T(8,128)(2,1)S(1)}, bf16[512,768]{1,0:T(8,128)(2,1)S(1)}, u32[]{:S(2)}, u32[]{:S(2)}) collective-permute-start(bf16[512,768]{1,0:T(8,128)(2,1)S(1)} %get-tuple-element.84), channel_id=1, source_target_pairs={{0,4},{1,3},{2,6},{3,1},{4,0},{5,7},{6,2},{7,5},{8,12},{9,11},{10,... | collective-permute-start | bytes 2359304 | tf_op jit(solution)/shard_map/ppermute | solution.py:120
  105.8 13.5 %collective-permute-start.18 = (bf16[256,768]{1,0:T(8,128)(2,1)S(1)}, bf16[256,768]{1,0:T(8,128)(2,1)S(1)}, u32[]{:S(2)}, u32[]{:S(2)}) collective-permute-start(bf16[256,768]{1,0:T(8,128)(2,1)S(1)} %get-tuple-element.83), channel_id=1, source_target_pairs={{0,1},{1,0},{2,3},{3,2},{4,5},{5,4},{6,7},{7,6},{8,9},{9,8},{10,11... | collective-permute-start | bytes 1179656 | tf_op jit(solution)/shard_map/ppermute | solution.py:120
  105.8 11.5 %collective-permute-start.16 = (bf16[144,384]{1,0:T(8,128)(2,1)S(1)}, bf16[144,384]{1,0:T(8,128)(2,1)S(1)}, u32[]{:S(2)}, u32[]{:S(2)}) collective-permute-start(bf16[144,384]{1,0:T(8,128)(2,1)S(1)} %bitcast.14), channel_id=1, source_target_pairs={{0,16},{1,17},{2,18},{3,19},{4,20},{5,21},{6,22},{7,23},{8,24},{9,... | collective-permute-start | bytes 331784 | tf_op jit(solution)/shard_map/ppermute | solution.py:120
  106.5 12.8 %collective-permute-start.17 = (bf16[3,48,384]{2,1,0:T(8,128)(2,1)S(1)}, bf16[3,48,384]{2,1,0:T(8,128)(2,1)S(1)}, u32[]{:S(2)}, u32[]{:S(2)}) collective-permute-start(bf16[3,48,384]{2,1,0:T(8,128)(2,1)S(1)} %get-tuple-element.82), channel_id=1, source_target_pairs={{0,16},{1,17},{2,18},{3,19},{4,20},{5,21},{6,22},{7,23},{8,24},{9,... | collective-permute-start | bytes 331784 | tf_op jit(solution)/shard_map/ppermute | solution.py:120
  120.0 11.9 %collective-permute-start.22 = (bf16[256,768]{1,0:T(8,128)(2,1)S(1)}, bf16[256,768]{1,0:T(8,128)(2,1)S(1)}, u32[]{:S(2)}, u32[]{:S(2)}) collective-permute-start(bf16[256,768]{1,0:T(8,128)(2,1)S(1)} %get-tuple-element.89), channel_id=1, source_target_pairs={{0,1},{1,0},{2,3},{3,2},{4,5},{5,4},{6,7},{7,6},{8,9},{9,8},{10,11... | collective-permute-start | bytes 1179656 | tf_op jit(solution)/shard_map/ppermute | solution.py:120
  120.1 11.8 %collective-permute-start.23 = (bf16[256,768]{1,0:T(8,128)(2,1)S(1)}, bf16[256,768]{1,0:T(8,128)(2,1)S(1)}, u32[]{:S(2)}, u32[]{:S(2)}) collective-permute-start(bf16[256,768]{1,0:T(8,128)(2,1)S(1)} %get-tuple-element.90), channel_id=1, source_target_pairs={{0,2},{1,5},{2,0},{3,7},{4,6},{5,1},{6,4},{7,3},{8,10},{9,13},{10,... | collective-permute-start | bytes 1179656 | tf_op jit(solution)/shard_map/ppermute | solution.py:120
  121.7 19.5 %collective-permute-start.27 = (bf16[512,768]{1,0:T(8,128)(2,1)S(1)}, bf16[512,768]{1,0:T(8,128)(2,1)S(1)}, u32[]{:S(2)}, u32[]{:S(2)}) collective-permute-start(bf16[512,768]{1,0:T(8,128)(2,1)S(1)} %get-tuple-element.94), channel_id=1, source_target_pairs={{0,1},{1,0},{2,3},{3,2},{4,5},{5,4},{6,7},{7,6},{8,9},{9,8},{10,11... | collective-permute-start | bytes 2359304 | tf_op jit(solution)/shard_map/ppermute | solution.py:120
  121.7 10.2 %collective-permute-start.20 = (bf16[288,384]{1,0:T(8,128)(2,1)S(1)}, bf16[288,384]{1,0:T(8,128)(2,1)S(1)}, u32[]{:S(2)}, u32[]{:S(2)}) collective-permute-start(bf16[288,384]{1,0:T(8,128)(2,1)S(1)} %get-tuple-element.87.refs_0_.refs_8_), channel_id=1, source_target_pairs={{0,8},{1,9},{2,10},{3,11},{4,12},{5,13},{6,14},{7,15},{8,0},{9,1},... | collective-permute-start | bytes 663560 | tf_op jit(solution)/shard_map/ppermute | solution.py:120
  121.7 8.0 %collective-permute-start.21 = (bf16[144,384]{1,0:T(8,128)(2,1)S(1)}, bf16[144,384]{1,0:T(8,128)(2,1)S(1)}, u32[]{:S(2)}, u32[]{:S(2)}) collective-permute-start(bf16[144,384]{1,0:T(8,128)(2,1)S(1)} %bitcast.16), channel_id=1, source_target_pairs={{0,16},{1,17},{2,18},{3,19},{4,20},{5,21},{6,22},{7,23},{8,24},{9,... | collective-permute-start | bytes 331784 | tf_op jit(solution)/shard_map/ppermute | solution.py:120
  132.7 8.5 %collective-permute-start.24 = (bf16[576,384]{1,0:T(8,128)(2,1)S(1)}, bf16[576,384]{1,0:T(8,128)(2,1)S(1)}, u32[]{:S(2)}, u32[]{:S(2)}) collective-permute-start(bf16[576,384]{1,0:T(8,128)(2,1)S(1)} %get-tuple-element.91.refs_0_.refs_8_), channel_id=1, source_target_pairs={{0,2},{1,5},{2,0},{3,7},{4,6},{5,1},{6,4},{7,3},{8,10},{9,13},{10,... | collective-permute-start | bytes 1327112 | tf_op jit(solution)/shard_map/ppermute | solution.py:120
  133.3 7.8 %collective-permute-start.26 = (bf16[256,768]{1,0:T(8,128)(2,1)S(1)}, bf16[256,768]{1,0:T(8,128)(2,1)S(1)}, u32[]{:S(2)}, u32[]{:S(2)}) collective-permute-start(bf16[256,768]{1,0:T(8,128)(2,1)S(1)} %get-tuple-element.93.refs_4_), channel_id=1, source_target_pairs={{0,1},{1,0},{2,3},{3,2},{4,5},{5,4},{6,7},{7,6},{8,9},{9,8},{10,11... | collective-permute-start | bytes 1179656 | tf_op jit(solution)/shard_map/ppermute | solution.py:120
  133.3 7.8 %collective-permute-start.25 = (bf16[288,384]{1,0:T(8,128)(2,1)S(1)}, bf16[288,384]{1,0:T(8,128)(2,1)S(1)}, u32[]{:S(2)}, u32[]{:S(2)}) collective-permute-start(bf16[288,384]{1,0:T(8,128)(2,1)S(1)} %get-tuple-element.92.refs_2_), channel_id=1, source_target_pairs={{0,8},{1,9},{2,10},{3,11},{4,12},{5,13},{6,14},{7,15},{8,0},{9,1},... | collective-permute-start | bytes 663560 | tf_op jit(solution)/shard_map/ppermute | solution.py:120
  142.8 12.9 %collective-permute-start.28 = (bf16[576,384]{1,0:T(8,128)(2,1)S(1)}, bf16[576,384]{1,0:T(8,128)(2,1)S(1)}, u32[]{:S(2)}, u32[]{:S(2)}) collective-permute-start(bf16[576,384]{1,0:T(8,128)(2,1)S(1)} %get-tuple-element.95.refs_0_), channel_id=1, source_target_pairs={{0,2},{1,5},{2,0},{3,7},{4,6},{5,1},{6,4},{7,3},{8,10},{9,13},{10,... | collective-permute-start | bytes 1327112 | tf_op jit(solution)/shard_map/ppermute | solution.py:120
  144.3 10.1 %collective-permute-start.29 = (bf16[256,768]{1,0:T(8,128)(2,1)S(1)}, bf16[256,768]{1,0:T(8,128)(2,1)S(1)}, u32[]{:S(2)}, u32[]{:S(2)}) collective-permute-start(bf16[256,768]{1,0:T(8,128)(2,1)S(1)} %get-tuple-element.97), channel_id=1, source_target_pairs={{0,8},{1,9},{2,10},{3,11},{4,12},{5,13},{6,14},{7,15},{8,0},{9,1},... | collective-permute-start | bytes 1179656 | tf_op jit(solution)/shard_map/ppermute | solution.py:120
  144.7 24.8 %collective-permute-start.32 = (bf16[1152,384]{1,0:T(8,128)(2,1)S(1)}, bf16[1152,384]{1,0:T(8,128)(2,1)S(1)}, u32[]{:S(2)}, u32[]{:S(2)}) collective-permute-start(bf16[1152,384]{1,0:T(8,128)(2,1)S(1)} %get-tuple-element.98.refs_4_.refs_0_), channel_id=1, source_target_pairs={{0,4},{1,3},{2,6},{3,1},{4,0},{5,7},{6,2},{7,5},{8,12},{9,11},{10,... | collective-permute-start | bytes 2654216 | tf_op jit(solution)/shard_map/ppermute | solution.py:120
  156.5 13.1 %collective-permute-start.33 = (bf16[1152,384]{1,0:T(8,128)(2,1)S(1)}, bf16[1152,384]{1,0:T(8,128)(2,1)S(1)}, u32[]{:S(2)}, u32[]{:S(2)}) collective-permute-start(bf16[1152,384]{1,0:T(8,128)(2,1)S(1)} %get-tuple-element.101.refs_2_), channel_id=1, source_target_pairs={{0,4},{1,3},{2,6},{3,1},{4,0},{5,7},{6,2},{7,5},{8,12},{9,11},{10,... | collective-permute-start | bytes 2654216 | tf_op jit(solution)/shard_map/ppermute | solution.py:120
  157.7 8.3 %collective-permute-start.30 = (bf16[128,768]{1,0:T(8,128)(2,1)S(1)}, bf16[128,768]{1,0:T(8,128)(2,1)S(1)}, u32[]{:S(2)}, u32[]{:S(2)}) collective-permute-start(bf16[128,768]{1,0:T(8,128)(2,1)S(1)} %get-tuple-element.100), channel_id=1, source_target_pairs={{0,16},{1,17},{2,18},{3,19},{4,20},{5,21},{6,22},{7,23},{8,24},{9,... | collective-permute-start | bytes 589832 | tf_op jit(solution)/shard_map/ppermute | solution.py:120
  166.7 1.5 collective-permute-start.31

commit v4 on v3

--- a/solution.py
+++ b/solution.py
@@ -16,12 +16,11 @@
 ROUNDS = (
     (((0, 0),), (2,)),
     (((1, 0), (0, 1),), (3,)),
-    (((0, 2), (1, 1), ("back", 0),), (1,)),
+    (((0, 2), (1, 1), ("back", 0), ("rows", 0),), (1,)),
     (((0, 3), (1, 2), ("back", 2), ("back", 1),), (0,)),
-    (((0, 4), (1, 3), ("back", 3), ("back", 4), ("rows", 0),), ()),
+    (((0, 4), (1, 3), ("back", 3), ("back", 4), ("rows", 1),), ()),
     (((0, 5), (1, 4), ("back", 5),), ()),
-    (((0, 6), (1, 5), ("back", 6), ("rows", 1),), ()),
-    (((1, 6), ("rows", 2),), ()),
+    (((1, 5), ("back", 6), ("rows", 2),), ()),
     ((("rows", 3),), ()),
     ((("rows", 4),), ()),
 )
@@ -462,7 +461,6 @@
 PLACES = (
     lambda pos: jnp.where(pos[3] == 0, pos[2], pos[1]),
     lambda pos: pos[0] % 2,
-    lambda pos: pos[0] // 2,
 )
 
 
@@ -489,14 +487,13 @@
     first = jnp.where(core == 0, y, x)
     second = jnp.where(core == 0, x, y)
     count = pl.num_programs(0)
-    rows = result.shape[1] // NODES_HERE
+    rows = result.shape[1] // (2 * SIDE * SIDE)
     for number, ref in enumerate(refs[:-1]):
         chunk, flip_a = number // 2, number % 2
         span = ref.shape[1]
-        for index in range(2 * DEPTH):
-            flip_b, k = index // DEPTH, LINE[index % DEPTH]
-            block = ((first ^ flip_a) * 2 + (second ^ flip_b)) * DEPTH + z % 2 * 2 + z // 2
-            place = block ^ (k % 2 * 2 + k // 2)
+        for index in range(4):
+            flip_b, flip_z = index // 2, index % 2
+            place = ((first ^ flip_a) * 2 + (second ^ flip_b)) * 2 + (z % 2 ^ flip_z)
             start = (index * count + pl.program_id(0)) * rows
             result[
                 0, pl.ds(pl.multiple_of(place * rows, 16), rows), chunk * span : (chunk + 1) * span
@@ -577,22 +574,27 @@
     ways = (SECOND, ALONG[1], ALONG[2])
 
     def weight_step(chunk, step):
-        if step < 3:
+        if step < 2:
 
             def sent(kept, away):
                 chunk["kept"], chunk["came"] = kept, hop(away, ways[step])
 
             return weight_fold_job(chunk["kept"], chunk["came"], PLACES[step]), sent
+        if step == 2:
+            def exchanged(total):
+                chunk["kept"], chunk["came"] = total, hop(total, ALONG[2])
+
+            return line_sum_job(chunk["kept"], chunk["came"]), exchanged
         if step == 3:
 
             def summed(total):
                 total = total.reshape(-1, total.shape[2])
-                chunk["line"] = [total, hop(total, ALONG[2])]
+                chunk["line"] = [total, hop(total, ALONG[1])]
 
             return line_sum_job(chunk["kept"], chunk["came"]), summed
 
         def joined(line):
-            chunk["line"] = [line, hop(line, (ALONG[1], SECOND, FIRST)[step - 4])]
+            chunk["line"] = [line, hop(line, (SECOND, FIRST)[step - 4])]
 
         return join_job(chunk["line"]), joined
 

time: 174 us -> 168 us (0.966)
  starting transfers between devices: 30.4 us -> 24.5 us
    ppermute x34 -> x32, starting transfers between devices: 30.4 us -> 24.5 us  [hop(): return lax.ppermute(array, AXES, table)]
    ppermute x34 -> x32, waiting for transfers between devices: 55.7 us -> 56.5 us  [hop(): return lax.ppermute(array, AXES, table)]
    pallas_call x27 -> x26, Pallas kernels: 81.4 us -> 80.9 us  [call(): pl.pallas_call(run, grid_spec=pltpu.PrefetchScalarGridSpec(num_scalar_pre...]
  transfers between devices with their start and end apart: 34 -> 32, of which waited for: 16 -> 17; matrix products, arithmetic and copies ran while one was open for 0% -> 0% of each run, Pallas kernels for 38% -> 40%
where the time goes in v4:
time: 168 us
  Pallas kernels  80.9 us (48%)
  waiting for transfers between devices  56.5 us (34%)
  starting transfers between devices  24.5 us (15%)
  local copies, waits for them, and re-layouts  3.3 us (2%)
    pallas_call x26, Pallas kernels, call(): pl.pallas_call(run, grid_spec=pltpu.PrefetchScalarGridSpec(num_scalar_pre...  80.9 us
    ppermute x32, waiting for transfers between devices, hop(): return lax.ppermute(array, AXES, table)  56.5 us
    ppermute x32, starting transfers between devices, hop(): return lax.ppermute(array, AXES, table)  24.5 us
  transfers between devices with their start and end apart: 32, of which 17 were waited for; matrix products, arithmetic and copies ran while one was open for 0% of the time, Pallas kernels for 40%

profile of v4, /device:TPU:0, one launch (start us, length us, event | category | flops | bytes accessed | tf_op | source)
XLA Modules:
  0.0 167.8 jit_solution(7525106244674142338)
XLA Ops:
  2.3 1.1 copy-done.2
  3.4 1.1 copy-done.3
  4.6 1.0 copy-done.4
  6.3 3.0 %collective-permute-start = (bf16[272,768]{1,0:T(8,128)(2,1)S(1)}, bf16[272,768]{1,0:T(8,128)(2,1)S(1)}, u32[]{:S(2)}, u32[]{:S(2)}) collective-permute-start(bf16[272,768]{1,0:T(8,128)(2,1)S(1)} %get-tuple-element.49.refs_0_), channel_id=1, source_target_pairs={{0,4},{1,3},{2,6},{3,1},{4,0},{5,7},{6,2},{7,5},{8,12},{9,11},{10,... | collective-permute-start | bytes 1253384 | tf_op jit(solution)/shard_map/ppermute | solution.py:119
  9.3 1.5 collective-permute-start.1
  10.8 2.6 %collective-permute-start.2 = (bf16[128,768]{1,0:T(8,128)(2,1)S(1)}, bf16[128,768]{1,0:T(8,128)(2,1)S(1)}, u32[]{:S(2)}, u32[]{:S(2)}) collective-permute-start(bf16[128,768]{1,0:T(8,128)(2,1)S(1)} %get-tuple-element.50.refs_2_), channel_id=1, source_target_pairs={{0,16},{1,17},{2,18},{3,19},{4,20},{5,21},{6,22},{7,23},{8,24},{9,... | collective-permute-start | bytes 589832 | tf_op jit(solution)/shard_map/ppermute | solution.py:119
  13.4 2.5 %gather.2.refs_5_.refs_3_ = bf16[3,512,768]{2,1,0:T(8,128)(2,1)S(1)} custom-call(s32[4]{0:T(128)S(1)} %pad_add_fusion.pos_ref, bf16[272,768]{1,0:T(8,128)(2,1)S(1)} %get-tuple-element.49.refs_0_, bf16[272,768]{1,0:T(8,128)(2,1)S(1)} %get-tuple-element.51.refs_1_, bf16[128,768]{1,0:T(8,128)(2,1)S(1)} %get-tuple-element.50.refs_2_), custom_call_target="tpu_custom_call" | custom-call | flops 1000 | bytes 1000 | tf_op jit(solution)/shard_map/gather/pallas_call | solution.py:47
  15.9 6.1 %collective-permute-done.2.refs_3_ = bf16[128,768]{1,0:T(8,128)(2,1)S(1)} collective-permute-done((bf16[128,768]{1,0:T(8,128)(2,1)S(1)}, bf16[128,768]{1,0:T(8,128)(2,1)S(1)}, u32[]{:S(2)}, u32[]{:S(2)}) %collective-permute-start.2) | collective-permute-done | bytes 196640 | tf_op jit(solution)/shard_map/ppermute | solution.py:119
  23.3 1.8 %collective-permute-done.4.refs_1_.refs_3_ = bf16[544,768]{1,0:T(8,128)(2,1)S(1)} collective-permute-done((bf16[544,768]{1,0:T(8,128)(2,1)S(1)}, bf16[544,768]{1,0:T(8,128)(2,1)S(1)}, u32[]{:S(2)}, u32[]{:S(2)}) %collective-permute-start.4) | collective-permute-done | bytes 835616 | tf_op jit(solution)/shard_map/ppermute | solution.py:119
  25.1 3.7 %gather.3.refs_1_.refs_4_ = bf16[3,1024,768]{2,1,0:T(8,128)(2,1)S(1)} custom-call(s32[4]{0:T(128)S(1)} %pad_add_fusion.pos_ref, bf16[272,768]{1,0:T(8,128)(2,1)S(1)} %collective-permute-done.refs_0_.refs_1_, bf16[544,768]{1,0:T(8,128)(2,1)S(1)} %collective-permute-done.4.refs_1_.refs_3_, bf16[272,768]{1,0:T(8,128)(2,1)S(1)} %get-tuple-element.52.refs_2_.refs_4_.refs_0_, ...), custom_call_target="tpu_custom_call" | custom-call | flops 1000 | bytes 1000 | tf_op jit(solution)/shard_map/gather/pallas_call | solution.py:47
  28.8 2.0 %collective-permute-done.3.refs_0_ = bf16[272,768]{1,0:T(8,128)(2,1)S(1)} collective-permute-done((bf16[272,768]{1,0:T(8,128)(2,1)S(1)}, bf16[272,768]{1,0:T(8,128)(2,1)S(1)}, u32[]{:S(2)}, u32[]{:S(2)}) %collective-permute-start.3) | collective-permute-done | bytes 417824 | tf_op jit(solution)/shard_map/ppermute | solution.py:119
  32.2 8.5 %aggregate_near.1.refs_2_ = f32[3,1024,768]{2,1,0:T(8,128)S(1)} custom-call(s32[4]{0:T(128)S(1)} %pad_add_fusion.pos_ref, bf16[272,768]{1,0:T(8,128)(2,1)S(1)} %get-tuple-element.49.refs_0_, bf16[272,768]{1,0:T(8,128)(2,1)S(1)} %collective-permute-done.refs_0_.refs_1_, bf16[272,768]{1,0:T(8,128)(2,1)S(1)} %get-tuple-element.52.refs_2_.refs_4_.refs_0_, ...), custom_call_target="tpu_custom_call" | custom-call | flops 1000 | bytes 1000 | tf_op jit(solution)/shard_map/aggregate_near/pallas_call | solution.py:47
  40.7 2.3 %collective-permute-done.6.refs_1_ = bf16[256,768]{1,0:T(8,128)(2,1)S(1)} collective-permute-done((bf16[256,768]{1,0:T(8,128)(2,1)S(1)}, bf16[256,768]{1,0:T(8,128)(2,1)S(1)}, u32[]{:S(2)}, u32[]{:S(2)}) %collective-permute-start.6) | collective-permute-done | bytes 393248 | tf_op jit(solution)/shard_map/ppermute | solution.py:119
  43.7 5.1 %aggregate.1.refs_0_.refs_3_ = bf16[3,1024,768]{2,1,0:T(8,128)(2,1)S(1)} custom-call(s32[4]{0:T(128)S(1)} %pad_add_fusion.pos_ref, bf16[272,768]{1,0:T(8,128)(2,1)S(1)} %step.13.refs_6_.refs_0_, bf16[272,768]{1,0:T(8,128)(2,1)S(1)} %collective-permute-done.5.refs_3_.refs_1_, f32[3,1024,768]{2,1,0:T(8,128)S(1)} %aggregate_near.1.refs_2_, ...), custom_call_target="tpu_custom_call" | custom-call | flops 1000 | bytes 1000 | tf_op jit(solution)/shard_map/aggregate/pallas_call | solution.py:47
  48.9 3.7 %weight_terms.2 = (bf16[3,384,384]{2,1,0:T(8,128)(2,1)S(1)}, f32[3,384,384]{2,1,0:T(8,128)S(1)}) custom-call(s32[4]{0:T(128)S(1)} %pad_add_fusion.pos_ref, bf16[3,1024,768]{2,1,0:T(8,128)(2,1)S(1)} %aggregate.1.refs_0_.refs_3_, bf16[512,768]{1,0:T(8,128)(2,1)S(1)} %step.14.refs_3_.refs_1_, bf16[512,768]{1,0:T(8,128)(2,1)S(1)} %collective-permute-done.7.refs_2_, ...), custom_call_target="tpu_custom_call" | custom-call | flops 1000 | bytes 1000 | tf_op jit(solution)/shard_map/weight_terms/pallas_call | solution.py:47
  53.2 2.5 %output_terms.2.refs_2_.refs_6_ = bf16[512,768]{1,0:T(8,128)(2,1)S(1)} custom-call(s32[4]{0:T(128)S(1)} %pad_add_fusion.pos_ref, bf16[3,1024,768]{2,1,0:T(8,128)(2,1)S(1)} %aggregate.1.refs_0_.refs_3_, bf16[3,768,768]{2,1,0:T(8,128)(2,1)S(1)} %copy-done, bf16[3,384,384]{2,1,0:T(8,128)(2,1)S(1)} %get-tuple-element.55.refs_2_), custom_call_target="tpu_custom_call" | custom-call | flops 1000 | bytes 1000 | tf_op jit(solution)/shard_map/output_terms/pallas_call | solution.py:47
  55.7 2.5 %output_terms.3.refs_3_.refs_8_ = f32[512,768]{1,0:T(8,128)S(1)} custom-call(s32[4]{0:T(128)S(1)} %pad_add_fusion.pos_ref, bf16[3,1024,768]{2,1,0:T(8,128)(2,1)S(1)} %aggregate.1.refs_0_.refs_3_, bf16[3,768,768]{2,1,0:T(8,128)(2,1)S(1)} %copy-done, bf16[512,768]{1,0:T(8,128)(2,1)S(1)} %output_terms.2.refs_2_.refs_6_), custom_call_target="tpu_custom_call" | custom-call | flops 1000 | bytes 1000 | tf_op jit(solution)/shard_map/output_terms/pallas_call | solution.py:47
  58.3 3.7 %weight_terms.3 = (bf16[3,384,384]{2,1,0:T(8,128)(2,1)S(1)}, f32[3,384,384]{2,1,0:T(8,128)S(1)}) custom-call(s32[4]{0:T(128)S(1)} %pad_add_fusion.pos_ref, bf16[3,1024,768]{2,1,0:T(8,128)(2,1)S(1)} %aggregate.1.refs_0_.refs_3_, bf16[512,768]{1,0:T(8,128)(2,1)S(1)} %step.14.refs_3_.refs_1_, bf16[512,768]{1,0:T(8,128)(2,1)S(1)} %collective-permute-done.7.refs_2_, ...), custom_call_target="tpu_custom_call" | custom-call | flops 1000 | bytes 1000 | tf_op jit(solution)/shard_map/weight_terms/pallas_call | solution.py:47
  62.0 1.6 collective-permute-start.8
  63.6 2.1 %collective-permute-done.9.refs_1_ = bf16[3,384,384]{2,1,0:T(8,128)(2,1)S(1)} collective-permute-done((bf16[3,384,384]{2,1,0:T(8,128)(2,1)S(1)}, bf16[3,384,384]{2,1,0:T(8,128)(2,1)S(1)}, u32[]{:S(2)}, u32[]{:S(2)}) %collective-permute-start.9) | collective-permute-done | bytes 884768 | tf_op jit(solution)/shard_map/ppermute | solution.py:119
  67.0 8.6 %feature_terms.4 = (f32[256,768]{1,0:T(8,128)S(1)}, bf16[256,768]{1,0:T(8,128)(2,1)S(1)}) custom-call(s32[4]{0:T(128)S(1)} %pad_add_fusion.pos_ref, bf16[272,768]{1,0:T(8,128)(2,1)S(1)} %get-tuple-element.52.refs_2_.refs_4_.refs_0_, bf16[512,768]{1,0:T(8,128)(2,1)S(1)} %step.14.refs_3_.refs_1_, bf16[512,768]{1,0:T(8,128)(2,1)S(1)} %collective-permute-done.7.refs_2_, ...), custom_call_target="tpu_custom_call" | custom-call | flops 1000 | bytes 1000 | tf_op jit(solution)/shard_map/feature_terms/pallas_call | solution.py:47
  75.7 4.3 %collective-permute-done.8.refs_1_ = bf16[3,384,384]{2,1,0:T(8,128)(2,1)S(1)} collective-permute-done((bf16[3,384,384]{2,1,0:T(8,128)(2,1)S(1)}, bf16[3,384,384]{2,1,0:T(8,128)(2,1)S(1)}, u32[]{:S(2)}, u32[]{:S(2)}) %collective-permute-start.8) | collective-permute-done | bytes 884768 | tf_op jit(solution)/shard_map/ppermute | solution.py:119
  79.9 0.8 step.16
  81.4 0.9 collective-permute-start.11
  82.3 8.4 %feature_terms.5 = (f32[256,768]{1,0:T(8,128)S(1)}, bf16[256,768]{1,0:T(8,128)(2,1)S(1)}) custom-call(s32[4]{0:T(128)S(1)} %pad_add_fusion.pos_ref, bf16[272,768]{1,0:T(8,128)(2,1)S(1)} %step.13.refs_6_.refs_0_, bf16[512,768]{1,0:T(8,128)(2,1)S(1)} %step.14.refs_3_.refs_1_, bf16[512,768]{1,0:T(8,128)(2,1)S(1)} %collective-permute-done.7.refs_2_, ...), custom_call_target="tpu_custom_call" | custom-call | flops 1000 | bytes 1000 | tf_op jit(solution)/shard_map/feature_terms/pallas_call | solution.py:47
  91.6 3.2 %collective-permute-start.13 = (bf16[3,96,384]{2,1,0:T(8,128)(2,1)S(1)}, bf16[3,96,384]{2,1,0:T(8,128)(2,1)S(1)}, u32[]{:S(2)}, u32[]{:S(2)}) collective-permute-start(bf16[3,96,384]{2,1,0:T(8,128)(2,1)S(1)} %get-tuple-element.69.refs_4_.refs_0_), channel_id=1, source_target_pairs={{0,16},{1,17},{2,18},{3,19},{4,20},{5,21},{6,22},{7,23},{8,24},{9,... | collective-permute-start | bytes 663560 | tf_op jit(solution)/shard_map/ppermute | solution.py:119
  95.1 8.5 %feature_terms.6 = (f32[256,768]{1,0:T(8,128)S(1)}, bf16[256,768]{1,0:T(8,128)(2,1)S(1)}) custom-call(s32[4]{0:T(128)S(1)} %pad_add_fusion.pos_ref, bf16[272,768]{1,0:T(8,128)(2,1)S(1)} %collective-permute-done.refs_0_.refs_1_, bf16[512,768]{1,0:T(8,128)(2,1)S(1)} %step.14.refs_3_.refs_1_, bf16[512,768]{1,0:T(8,128)(2,1)S(1)} %collective-permute-done.7.refs_2_, ...), custom_call_target="tpu_custom_call" | custom-call | flops 1000 | bytes 1000 | tf_op jit(solution)/shard_map/feature_terms/pallas_call | solution.py:47
  103.5 2.1 %collective-permute-done.13.refs_1_ = bf16[3,96,384]{2,1,0:T(8,128)(2,1)S(1)} collective-permute-done((bf16[3,96,384]{2,1,0:T(8,128)(2,1)S(1)}, bf16[3,96,384]{2,1,0:T(8,128)(2,1)S(1)}, u32[]{:S(2)}, u32[]{:S(2)}) %collective-permute-start.13) | collective-permute-done | bytes 221216 | tf_op jit(solution)/shard_map/ppermute | solution.py:119
  105.7 1.2 collective-permute-done.14.refs_3_
  106.8 0.8 step.18
  107.6 1.5 collective-permute-start.19
  109.7 1.2 collective-permute-start.17
  110.8 8.4 %feature_terms.7 = (f32[256,768]{1,0:T(8,128)S(1)}, bf16[256,768]{1,0:T(8,128)(2,1)S(1)}) custom-call(s32[4]{0:T(128)S(1)} %pad_add_fusion.pos_ref, bf16[272,768]{1,0:T(8,128)(2,1)S(1)} %get-tuple-element.49.refs_0_, bf16[512,768]{1,0:T(8,128)(2,1)S(1)} %step.14.refs_3_.refs_1_, bf16[512,768]{1,0:T(8,128)(2,1)S(1)} %collective-permute-done.7.refs_2_, ...), custom_call_target="tpu_custom_call" | custom-call | flops 1000 | bytes 1000 | tf_op jit(solution)/shard_map/feature_terms/pallas_call | solution.py:47
  120.0 2.9 %collective-permute-done.17.refs_3_ = bf16[3,96,384]{2,1,0:T(8,128)(2,1)S(1)} collective-permute-done((bf16[3,96,384]{2,1,0:T(8,128)(2,1)S(1)}, bf16[3,96,384]{2,1,0:T(8,128)(2,1)S(1)}, u32[]{:S(2)}, u32[]{:S(2)}) %collective-permute-start.17) | collective-permute-done | bytes 221216 | tf_op jit(solution)/shard_map/ppermute | solution.py:119
  122.9 0.9 step.19
  123.9 1.6 collective-permute-start.21
  126.0 7.6 %collective-permute-done.22.refs_3_ = bf16[288,384]{1,0:T(8,128)(2,1)S(1)} collective-permute-done((bf16[288,384]{1,0:T(8,128)(2,1)S(1)}, bf16[288,384]{1,0:T(8,128)(2,1)S(1)}, u32[]{:S(2)}, u32[]{:S(2)}) %collective-permute-start.22) | collective-permute-done | bytes 221216 | tf_op jit(solution)/shard_map/ppermute | solution.py:119
  133.5 2.9 %collective-permute-done.24.refs_7_ = bf16[256,768]{1,0:T(8,128)(2,1)S(1)} collective-permute-done((bf16[256,768]{1,0:T(8,128)(2,1)S(1)}, bf16[256,768]{1,0:T(8,128)(2,1)S(1)}, u32[]{:S(2)}, u32[]{:S(2)}) %collective-permute-start.24) | collective-permute-done | bytes 393248 | tf_op jit(solution)/shard_map/ppermute | solution.py:119
  136.4 0.8 step.20
  137.3 1.6 collective-permute-start.25
  139.4 7.6 %collective-permute-done.27.refs_5_ = bf16[256,768]{1,0:T(8,128)(2,1)S(1)} collective-permute-done((bf16[256,768]{1,0:T(8,128)(2,1)S(1)}, bf16[256,768]{1,0:T(8,128)(2,1)S(1)}, u32[]{:S(2)}, u32[]{:S(2)}) %collective-permute-start.27) | collective-permute-done | bytes 393248 | tf_op jit(solution)/shard_map/ppermute | solution.py:119
  147.0 2.3 %collective-permute-done.25.refs_1_ = bf16[576,384]{1,0:T(8,128)(2,1)S(1)} collective-permute-done((bf16[576,384]{1,0:T(8,128)(2,1)S(1)}, bf16[576,384]{1,0:T(8,128)(2,1)S(1)}, u32[]{:S(2)}, u32[]{:S(2)}) %collective-permute-start.25) | collective-permute-done | bytes 442400 | tf_op jit(solution)/shard_map/ppermute | solution.py:119
  149.3 1.6 step.21
  151.5 7.8 %collective-permute-done.28.refs_1_ = bf16[128,768]{1,0:T(8,128)(2,1)S(1)} collective-permute-done((bf16[128,768]{1,0:T(8,128)(2,1)S(1)}, bf16[128,768]{1,0:T(8,128)(2,1)S(1)}, u32[]{:S(2)}, u32[]{:S(2)}) %collective-permute-start.28) | collective-permute-done | bytes 196640 | tf_op jit(solution)/shard_map/ppermute | solution.py:119
  160.0 1.4 collective-permute-done.29.refs_1_
  161.4 1.3 step.23
  162.7 1.2 collective-permute-done.31.refs_3_
  164.0 3.8 %assemble.1 = f32[3,768,768]{2,1,0:T(8,128)} custom-call(s32[4]{0:T(128)S(1)} %pad_add_fusion.pos_ref, bf16[1152,384]{1,0:T(8,128)(2,1)S(1)} %get-tuple-element.90.refs_6_.refs_0_, bf16[1152,384]{1,0:T(8,128)(2,1)S(1)} %collective-permute-done.30.refs_1_, bf16[1152,384]{1,0:T(8,128)(2,1)S(1)} %get-tuple-element.93.refs_2_, ...), custom_call_target="tpu_custom_call" | custom-call | flops 1000 | bytes 1000 | tf_op jit(solution)/shard_map/assemble/pallas_call | solution.py:47
  (59 shorter events, 12.8 us)
Async XLA Ops:
  2.3 1.1 copy-start.2
  3.4 1.1 copy-start.3
  4.5 1.0 copy-start.4
  6.3 15.7 %collective-permute-start = (bf16[272,768]{1,0:T(8,128)(2,1)S(1)}, bf16[272,768]{1,0:T(8,128)(2,1)S(1)}, u32[]{:S(2)}, u32[]{:S(2)}) collective-permute-start(bf16[272,768]{1,0:T(8,128)(2,1)S(1)} %get-tuple-element.49.refs_0_), channel_id=1, source_target_pairs={{0,4},{1,3},{2,6},{3,1},{4,0},{5,7},{6,2},{7,5},{8,12},{9,11},{10,... | collective-permute-start | bytes 1253384 | tf_op jit(solution)/shard_map/ppermute | solution.py:119
  9.3 12.7 %collective-permute-start.1 = (bf16[272,768]{1,0:T(8,128)(2,1)S(1)}, bf16[272,768]{1,0:T(8,128)(2,1)S(1)}, u32[]{:S(2)}, u32[]{:S(2)}) collective-permute-start(bf16[272,768]{1,0:T(8,128)(2,1)S(1)} %get-tuple-element.49.refs_0_), channel_id=1, source_target_pairs={{0,2},{1,5},{2,0},{3,7},{4,6},{5,1},{6,4},{7,3},{8,10},{9,13},{10,... | collective-permute-start | bytes 1253384 | tf_op jit(solution)/shard_map/ppermute | solution.py:119
  10.8 11.2 %collective-permute-start.2 = (bf16[128,768]{1,0:T(8,128)(2,1)S(1)}, bf16[128,768]{1,0:T(8,128)(2,1)S(1)}, u32[]{:S(2)}, u32[]{:S(2)}) collective-permute-start(bf16[128,768]{1,0:T(8,128)(2,1)S(1)} %get-tuple-element.50.refs_2_), channel_id=1, source_target_pairs={{0,16},{1,17},{2,18},{3,19},{4,20},{5,21},{6,22},{7,23},{8,24},{9,... | collective-permute-start | bytes 589832 | tf_op jit(solution)/shard_map/ppermute | solution.py:119
  22.7 2.4 %collective-permute-start.4 = (bf16[544,768]{1,0:T(8,128)(2,1)S(1)}, bf16[544,768]{1,0:T(8,128)(2,1)S(1)}, u32[]{:S(2)}, u32[]{:S(2)}) collective-permute-start(bf16[544,768]{1,0:T(8,128)(2,1)S(1)} %get-tuple-element.53), channel_id=1, source_target_pairs={{0,1},{1,0},{2,3},{3,2},{4,5},{5,4},{6,7},{7,6},{8,9},{9,8},{10,11... | collective-permute-start | bytes 2506760 | tf_op jit(solution)/shard_map/ppermute | solution.py:119
  22.7 8.1 %collective-permute-start.3 = (bf16[272,768]{1,0:T(8,128)(2,1)S(1)}, bf16[272,768]{1,0:T(8,128)(2,1)S(1)}, u32[]{:S(2)}, u32[]{:S(2)}) collective-permute-start(bf16[272,768]{1,0:T(8,128)(2,1)S(1)} %get-tuple-element.52.refs_2_.refs_4_.refs_0_), channel_id=1, source_target_pairs={{0,4},{1,3},{2,6},{3,1},{4,0},{5,7},{6,2},{7,5},{8,12},{9,11},{10,... | collective-permute-start | bytes 1253384 | tf_op jit(solution)/shard_map/ppermute | solution.py:119
  28.8 3.4 %copy-start.1 = (bf16[3,256,768]{2,1,0:T(8,128)(2,1)S(1)}, bf16[3,256,768]{2,1,0:T(8,128)(2,1)}, u32[]{:S(2)}) copy-start(bf16[3,256,768]{2,1,0:T(8,128)(2,1)} %refs_5_.1) | copy-start | bytes 3538948
  31.4 11.6 %collective-permute-start.5 = (bf16[272,768]{1,0:T(8,128)(2,1)S(1)}, bf16[272,768]{1,0:T(8,128)(2,1)S(1)}, u32[]{:S(2)}, u32[]{:S(2)}) collective-permute-start(bf16[272,768]{1,0:T(8,128)(2,1)S(1)} %step.13.refs_6_.refs_0_), channel_id=1, source_target_pairs={{0,1},{1,0},{2,3},{3,2},{4,5},{5,4},{6,7},{7,6},{8,9},{9,8},{10,11... | collective-permute-start | bytes 1253384 | tf_op jit(solution)/shard_map/ppermute | solution.py:119
  31.5 11.5 %collective-permute-start.6 = (bf16[256,768]{1,0:T(8,128)(2,1)S(1)}, bf16[256,768]{1,0:T(8,128)(2,1)S(1)}, u32[]{:S(2)}, u32[]{:S(2)}) collective-permute-start(bf16[256,768]{1,0:T(8,128)(2,1)S(1)} %get-tuple-element.54.refs_0_), channel_id=1, source_target_pairs={{0,8},{1,9},{2,10},{3,11},{4,12},{5,13},{6,14},{7,15},{8,0},{9,1},... | collective-permute-start | bytes 1179656 | tf_op jit(solution)/shard_map/ppermute | solution.py:119
  43.6 5.2 %collective-permute-start.7 = (bf16[512,768]{1,0:T(8,128)(2,1)S(1)}, bf16[512,768]{1,0:T(8,128)(2,1)S(1)}, u32[]{:S(2)}, u32[]{:S(2)}) collective-permute-start(bf16[512,768]{1,0:T(8,128)(2,1)S(1)} %step.14.refs_3_.refs_1_), channel_id=1, source_target_pairs={{0,1},{1,0},{2,3},{3,2},{4,5},{5,4},{6,7},{7,6},{8,9},{9,8},{10,11... | collective-permute-start | bytes 2359304 | tf_op jit(solution)/shard_map/ppermute | solution.py:119
  48.8 4.4 %copy-start = (bf16[3,768,768]{2,1,0:T(8,128)(2,1)S(1)}, bf16[3,768,768]{2,1,0:T(8,128)(2,1)}, u32[]{:S(2)}) copy-start(bf16[3,768,768]{2,1,0:T(8,128)(2,1)} %refs_3_.9) | copy-start | bytes 10616836
  52.6 13.1 %collective-permute-start.9 = (bf16[3,384,384]{2,1,0:T(8,128)(2,1)S(1)}, bf16[3,384,384]{2,1,0:T(8,128)(2,1)S(1)}, u32[]{:S(2)}, u32[]{:S(2)}) collective-permute-start(bf16[3,384,384]{2,1,0:T(8,128)(2,1)S(1)} %get-tuple-element.55.refs_2_), channel_id=1, source_target_pairs={{0,4},{1,3},{2,6},{3,1},{4,0},{5,7},{6,2},{7,5},{8,12},{9,11},{10,... | collective-permute-start | bytes 2654216 | tf_op jit(solution)/shard_map/ppermute | solution.py:119
  62.0 17.9 %collective-permute-start.8 = (bf16[3,384,384]{2,1,0:T(8,128)(2,1)S(1)}, bf16[3,384,384]{2,1,0:T(8,128)(2,1)S(1)}, u32[]{:S(2)}, u32[]{:S(2)}) collective-permute-start(bf16[3,384,384]{2,1,0:T(8,128)(2,1)S(1)} %get-tuple-element.57.refs_2_), channel_id=1, source_target_pairs={{0,4},{1,3},{2,6},{3,1},{4,0},{5,7},{6,2},{7,5},{8,12},{9,11},{10,... | collective-permute-start | bytes 2654216 | tf_op jit(solution)/shard_map/ppermute | solution.py:119
  66.4 13.5 %collective-permute-start.10 = (bf16[3,192,384]{2,1,0:T(8,128)(2,1)S(1)}, bf16[3,192,384]{2,1,0:T(8,128)(2,1)S(1)}, u32[]{:S(2)}, u32[]{:S(2)}) collective-permute-start(bf16[3,192,384]{2,1,0:T(8,128)(2,1)S(1)} %get-tuple-element.60), channel_id=1, source_target_pairs={{0,2},{1,5},{2,0},{3,7},{4,6},{5,1},{6,4},{7,3},{8,10},{9,13},{10,... | collective-permute-start | bytes 1327112 | tf_op jit(solution)/shard_map/ppermute | solution.py:119
  80.8 10.0 %collective-permute-start.12 = (bf16[3,192,384]{2,1,0:T(8,128)(2,1)S(1)}, bf16[3,192,384]{2,1,0:T(8,128)(2,1)S(1)}, u32[]{:S(2)}, u32[]{:S(2)}) collective-permute-start(bf16[3,192,384]{2,1,0:T(8,128)(2,1)S(1)} %get-tuple-element.65), channel_id=1, source_target_pairs={{0,2},{1,5},{2,0},{3,7},{4,6},{5,1},{6,4},{7,3},{8,10},{9,13},{10,... | collective-permute-start | bytes 1327112 | tf_op jit(solution)/shard_map/ppermute | solution.py:119
  81.4 9.4 %collective-permute-start.11 = (bf16[3,96,384]{2,1,0:T(8,128)(2,1)S(1)}, bf16[3,96,384]{2,1,0:T(8,128)(2,1)S(1)}, u32[]{:S(2)}, u32[]{:S(2)}) collective-permute-start(bf16[3,96,384]{2,1,0:T(8,128)(2,1)S(1)} %get-tuple-element.63), channel_id=1, source_target_pairs={{0,8},{1,9},{2,10},{3,11},{4,12},{5,13},{6,14},{7,15},{8,0},{9,1},... | collective-permute-start | bytes 663560 | tf_op jit(solution)/shard_map/ppermute | solution.py:119
  91.5 15.3 %collective-permute-start.15 = (bf16[512,768]{1,0:T(8,128)(2,1)S(1)}, bf16[512,768]{1,0:T(8,128)(2,1)S(1)}, u32[]{:S(2)}, u32[]{:S(2)}) collective-permute-start(bf16[512,768]{1,0:T(8,128)(2,1)S(1)} %get-tuple-element.73), channel_id=1, source_target_pairs={{0,1},{1,0},{2,3},{3,2},{4,5},{5,4},{6,7},{7,6},{8,9},{9,8},{10,11... | collective-permute-start | bytes 2359304 | tf_op jit(solution)/shard_map/ppermute | solution.py:119
  91.6 14.1 %collective-permute-start.13 = (bf16[3,96,384]{2,1,0:T(8,128)(2,1)S(1)}, bf16[3,96,384]{2,1,0:T(8,128)(2,1)S(1)}, u32[]{:S(2)}, u32[]{:S(2)}) collective-permute-start(bf16[3,96,384]{2,1,0:T(8,128)(2,1)S(1)} %get-tuple-element.69.refs_4_.refs_0_), channel_id=1, source_target_pairs={{0,16},{1,17},{2,18},{3,19},{4,20},{5,21},{6,22},{7,23},{8,24},{9,... | collective-permute-start | bytes 663560 | tf_op jit(solution)/shard_map/ppermute | solution.py:119
  94.8 12.1 %collective-permute-start.14 = (bf16[3,96,384]{2,1,0:T(8,128)(2,1)S(1)}, bf16[3,96,384]{2,1,0:T(8,128)(2,1)S(1)}, u32[]{:S(2)}, u32[]{:S(2)}) collective-permute-start(bf16[3,96,384]{2,1,0:T(8,128)(2,1)S(1)} %get-tuple-element.71), channel_id=1, source_target_pairs={{0,8},{1,9},{2,10},{3,11},{4,12},{5,13},{6,14},{7,15},{8,0},{9,1},... | collective-permute-start | bytes 663560 | tf_op jit(solution)/shard_map/ppermute | solution.py:119
  95.1 24.2 %collective-permute-start.20 = (bf16[512,768]{1,0:T(8,128)(2,1)S(1)}, bf16[512,768]{1,0:T(8,128)(2,1)S(1)}, u32[]{:S(2)}, u32[]{:S(2)}) collective-permute-start(bf16[512,768]{1,0:T(8,128)(2,1)S(1)} %get-tuple-element.80), channel_id=1, source_target_pairs={{0,1},{1,0},{2,3},{3,2},{4,5},{5,4},{6,7},{7,6},{8,9},{9,8},{10,11... | collective-permute-start | bytes 2359304 | tf_op jit(solution)/shard_map/ppermute | solution.py:119
  107.6 15.3 %collective-permute-start.19 = (bf16[512,768]{1,0:T(8,128)(2,1)S(1)}, bf16[512,768]{1,0:T(8,128)(2,1)S(1)}, u32[]{:S(2)}, u32[]{:S(2)}) collective-permute-start(bf16[512,768]{1,0:T(8,128)(2,1)S(1)} %get-tuple-element.78), channel_id=1, source_target_pairs={{0,4},{1,3},{2,6},{3,1},{4,0},{5,7},{6,2},{7,5},{8,12},{9,11},{10,... | collective-permute-start | bytes 2359304 | tf_op jit(solution)/shard_map/ppermute | solution.py:119
  109.2 13.8 %collective-permute-start.18 = (bf16[256,768]{1,0:T(8,128)(2,1)S(1)}, bf16[256,768]{1,0:T(8,128)(2,1)S(1)}, u32[]{:S(2)}, u32[]{:S(2)}) collective-permute-start(bf16[256,768]{1,0:T(8,128)(2,1)S(1)} %get-tuple-element.77), channel_id=1, source_target_pairs={{0,1},{1,0},{2,3},{3,2},{4,5},{5,4},{6,7},{7,6},{8,9},{9,8},{10,11... | collective-permute-start | bytes 1179656 | tf_op jit(solution)/shard_map/ppermute | solution.py:119
  109.2 10.9 %collective-permute-start.16 = (bf16[288,384]{1,0:T(8,128)(2,1)S(1)}, bf16[288,384]{1,0:T(8,128)(2,1)S(1)}, u32[]{:S(2)}, u32[]{:S(2)}) collective-permute-start(bf16[288,384]{1,0:T(8,128)(2,1)S(1)} %bitcast.14), channel_id=1, source_target_pairs={{0,8},{1,9},{2,10},{3,11},{4,12},{5,13},{6,14},{7,15},{8,0},{9,1},... | collective-permute-start | bytes 663560 | tf_op jit(solution)/shard_map/ppermute | solution.py:119
  109.7 13.2 %collective-permute-start.17 = (bf16[3,96,384]{2,1,0:T(8,128)(2,1)S(1)}, bf16[3,96,384]{2,1,0:T(8,128)(2,1)S(1)}, u32[]{:S(2)}, u32[]{:S(2)}) collective-permute-start(bf16[3,96,384]{2,1,0:T(8,128)(2,1)S(1)} %get-tuple-element.76.refs_2_), channel_id=1, source_target_pairs={{0,16},{1,17},{2,18},{3,19},{4,20},{5,21},{6,22},{7,23},{8,24},{9,... | collective-permute-start | bytes 663560 | tf_op jit(solution)/shard_map/ppermute | solution.py:119
  123.9 12.6 %collective-permute-start.21 = (bf16[576,384]{1,0:T(8,128)(2,1)S(1)}, bf16[576,384]{1,0:T(8,128)(2,1)S(1)}, u32[]{:S(2)}, u32[]{:S(2)}) collective-permute-start(bf16[576,384]{1,0:T(8,128)(2,1)S(1)} %get-tuple-element.82.refs_0_.refs_8_), channel_id=1, source_target_pairs={{0,2},{1,5},{2,0},{3,7},{4,6},{5,1},{6,4},{7,3},{8,10},{9,13},{10,... | collective-permute-start | bytes 1327112 | tf_op jit(solution)/shard_map/ppermute | solution.py:119
  125.4 8.1 %collective-permute-start.23 = (bf16[256,768]{1,0:T(8,128)(2,1)S(1)}, bf16[256,768]{1,0:T(8,128)(2,1)S(1)}, u32[]{:S(2)}, u32[]{:S(2)}) collective-permute-start(bf16[256,768]{1,0:T(8,128)(2,1)S(1)} %get-tuple-element.84), channel_id=1, source_target_pairs={{0,1},{1,0},{2,3},{3,2},{4,5},{5,4},{6,7},{7,6},{8,9},{9,8},{10,11... | collective-permute-start | bytes 1179656 | tf_op jit(solution)/shard_map/ppermute | solution.py:119
  125.4 11.0 %collective-permute-start.24 = (bf16[256,768]{1,0:T(8,128)(2,1)S(1)}, bf16[256,768]{1,0:T(8,128)(2,1)S(1)}, u32[]{:S(2)}, u32[]{:S(2)}) collective-permute-start(bf16[256,768]{1,0:T(8,128)(2,1)S(1)} %get-tuple-element.85), channel_id=1, source_target_pairs={{0,2},{1,5},{2,0},{3,7},{4,6},{5,1},{6,4},{7,3},{8,10},{9,13},{10,... | collective-permute-start | bytes 1179656 | tf_op jit(solution)/shard_map/ppermute | solution.py:119
  125.9 7.6 %collective-permute-start.22 = (bf16[288,384]{1,0:T(8,128)(2,1)S(1)}, bf16[288,384]{1,0:T(8,128)(2,1)S(1)}, u32[]{:S(2)}, u32[]{:S(2)}) collective-permute-start(bf16[288,384]{1,0:T(8,128)(2,1)S(1)} %bitcast.16), channel_id=1, source_target_pairs={{0,8},{1,9},{2,10},{3,11},{4,12},{5,13},{6,14},{7,15},{8,0},{9,1},... | collective-permute-start | bytes 663560 | tf_op jit(solution)/shard_map/ppermute | solution.py:119
  137.3 12.1 %collective-permute-start.25 = (bf16[576,384]{1,0:T(8,128)(2,1)S(1)}, bf16[576,384]{1,0:T(8,128)(2,1)S(1)}, u32[]{:S(2)}, u32[]{:S(2)}) collective-permute-start(bf16[576,384]{1,0:T(8,128)(2,1)S(1)} %get-tuple-element.86.refs_0_), channel_id=1, source_target_pairs={{0,2},{1,5},{2,0},{3,7},{4,6},{5,1},{6,4},{7,3},{8,10},{9,13},{10,... | collective-permute-start | bytes 1327112 | tf_op jit(solution)/shard_map/ppermute | solution.py:119
  138.8 8.2 %collective-permute-start.27 = (bf16[256,768]{1,0:T(8,128)(2,1)S(1)}, bf16[256,768]{1,0:T(8,128)(2,1)S(1)}, u32[]{:S(2)}, u32[]{:S(2)}) collective-permute-start(bf16[256,768]{1,0:T(8,128)(2,1)S(1)} %get-tuple-element.89), channel_id=1, source_target_pairs={{0,8},{1,9},{2,10},{3,11},{4,12},{5,13},{6,14},{7,15},{8,0},{9,1},... | collective-permute-start | bytes 1179656 | tf_op jit(solution)/shard_map/ppermute | solution.py:119
  138.8 8.2 %collective-permute-start.26 = (bf16[256,768]{1,0:T(8,128)(2,1)S(1)}, bf16[256,768]{1,0:T(8,128)(2,1)S(1)}, u32[]{:S(2)}, u32[]{:S(2)}) collective-permute-start(bf16[256,768]{1,0:T(8,128)(2,1)S(1)} %get-tuple-element.87.refs_2_), channel_id=1, source_target_pairs={{0,1},{1,0},{2,3},{3,2},{4,5},{5,4},{6,7},{7,6},{8,9},{9,8},{10,11... | collective-permute-start | bytes 1179656 | tf_op jit(solution)/shard_map/ppermute | solution.py:119
  138.8 23.9 %collective-permute-start.30 = (bf16[1152,384]{1,0:T(8,128)(2,1)S(1)}, bf16[1152,384]{1,0:T(8,128)(2,1)S(1)}, u32[]{:S(2)}, u32[]{:S(2)}) collective-permute-start(bf16[1152,384]{1,0:T(8,128)(2,1)S(1)} %get-tuple-element.90.refs_6_.refs_0_), channel_id=1, source_target_pairs={{0,4},{1,3},{2,6},{3,1},{4,0},{5,7},{6,2},{7,5},{8,12},{9,11},{10,... | collective-permute-start | bytes 2654216 | tf_op jit(solution)/shard_map/ppermute | solution.py:119
  150.9 13.0 %collective-permute-start.31 = (bf16[1152,384]{1,0:T(8,128)(2,1)S(1)}, bf16[1152,384]{1,0:T(8,128)(2,1)S(1)}, u32[]{:S(2)}, u32[]{:S(2)}) collective-permute-start(bf16[1152,384]{1,0:T(8,128)(2,1)S(1)} %get-tuple-element.93.refs_2_), channel_id=1, source_target_pairs={{0,4},{1,3},{2,6},{3,1},{4,0},{5,7},{6,2},{7,5},{8,12},{9,11},{10,... | collective-permute-start | bytes 2654216 | tf_op jit(solution)/shard_map/ppermute | solution.py:119
  151.5 7.8 %collective-permute-start.28 = (bf16[128,768]{1,0:T(8,128)(2,1)S(1)}, bf16[128,768]{1,0:T(8,128)(2,1)S(1)}, u32[]{:S(2)}, u32[]{:S(2)}) collective-permute-start(bf16[128,768]{1,0:T(8,128)(2,1)S(1)} %get-tuple-element.92), channel_id=1, source_target_pairs={{0,16},{1,17},{2,18},{3,19},{4,20},{5,21},{6,22},{7,23},{8,24},{9,... | collective-permute-start | bytes 589832 | tf_op jit(solution)/shard_map/ppermute | solution.py:119
  159.9 1.5 collective-permute-start.29

commit v5 on v4

--- a/solution.py
+++ b/solution.py
@@ -429,33 +429,31 @@
     return (finish_kernel, [full(total), full(opposite)], [out(shape, BF)], {})
 
 
-def weight_kernel(norm, pos, sums, line, far, away, kept):
+def weight_kernel(norm, sent, pos, sums, line, far, result):
     half = sums.shape[2] // 2
     rows = line.shape[0]
     place = jnp.where(pos[3] == 0, pos[1], pos[2])
-    for ref, index in ((away, 1 - place), (kept, place)):
-        columns = pl.ds(pl.multiple_of(index * half, 128), half)
-        total = dot(sums[0, :rows, columns], line[...], ((0,), (0,)))
-        total = total + dot(sums[0, rows:, columns], far[...], ((0,), (0,)))
-        ref[0] = (norm * total).astype(ref.dtype)
-
-
-def weight_terms(pos, sums, line, far, chunk, norm, after):
+    columns = pl.ds(pl.multiple_of((1 - place if sent else place) * half, 128), half)
+    total = dot(sums[0, :rows, columns], line[...], ((0,), (0,)))
+    total = total + dot(sums[0, rows:, columns], far[...], ((0,), (0,)))
+    result[0] = (norm * total).astype(result.dtype)
+
+
+def weight_terms(pos, sums, line, far, chunk, norm, sent, after):
     groups, _, width = sums.shape
     span = width // CHUNKS
     shape = (groups, width // 2, span)
     flat = lambda array: (array, (array.shape[0], span), lambda s, pos: (0, chunk))
-    block = ((1,) + shape[1:], lambda s, pos: (s, 0, 0))
     return call(
         "weight_terms",
-        functools.partial(weight_kernel, norm),
+        functools.partial(weight_kernel, norm, sent),
         pos,
         [by_rel(sums), flat(line), flat(far)],
-        [(shape, BF) + block, (shape, F32) + block],
+        [(shape, BF if sent else F32, (1,) + shape[1:], lambda s, pos: (s, 0, 0))],
         grid=(groups,),
         after=after,
         limit=24,
-    )
+    )[0]
 
 
 PLACES = (
@@ -562,14 +560,14 @@
     chunks = [{"index": index} for index in range(CHUNKS)]
     last = sums
     for chunk in chunks:
-        chunk["away"], chunk["kept"] = weight_terms(
-            pos, sums, line, far, chunk["index"], norm, [last]
-        )
-        last = chunk["away"]
-        chunk["came"] = hop(chunk["away"], FIRST)
+        last = weight_terms(pos, sums, line, far, chunk["index"], norm, True, [last])
+        chunk["came"] = hop(last, FIRST)
         if chunk["index"] == 0:
             theirs = output_terms(pos, sums, weights, 1, BF, [last])
             last = output = output_terms(pos, sums, weights, 0, F32, [theirs])
+    for chunk in chunks:
+        last = weight_terms(pos, sums, line, far, chunk["index"], norm, False, [last])
+        chunk["kept"] = last
     state, grown, given = {"away": theirs, "kept": output}, {}, {}
     ways = (SECOND, ALONG[1], ALONG[2])
 

time: 168 us -> 166 us (0.988)
  waiting for transfers between devices: 56.5 us -> 51.1 us
  Pallas kernels: 80.9 us -> 83.5 us
    ppermute x32, waiting for transfers between devices: 56.5 us -> 51.1 us  [hop(): return lax.ppermute(array, AXES, table)]
    pallas_call x26 -> x28, Pallas kernels: 80.9 us -> 83.5 us  [call(): pl.pallas_call(run, grid_spec=pltpu.PrefetchScalarGridSpec(num_scalar_pre...]
  transfers between devices with their start and end apart: 32 -> 32, of which waited for: 17 -> 16; matrix products, arithmetic and copies ran while one was open for 0% -> 0% of each run, Pallas kernels for 40% -> 43%
where the time goes in v5:
time: 166 us
  Pallas kernels  83.5 us (50%)
  waiting for transfers between devices  51.1 us (31%)
  starting transfers between devices  25.2 us (15%)
  local copies, waits for them, and re-layouts  3.3 us (2%)
    pallas_call x28, Pallas kernels, call(): pl.pallas_call(run, grid_spec=pltpu.PrefetchScalarGridSpec(num_scalar_pre...  83.5 us
    ppermute x32, waiting for transfers between devices, hop(): return lax.ppermute(array, AXES, table)  51.1 us
    ppermute x32, starting transfers between devices, hop(): return lax.ppermute(array, AXES, table)  25.2 us
  transfers between devices with their start and end apart: 32, of which 16 were waited for; matrix products, arithmetic and copies ran while one was open for 0% of the time, Pallas kernels for 43%

profile of v5, /device:TPU:0, one launch (start us, length us, event | category | flops | bytes accessed | tf_op | source)
XLA Modules:
  0.0 165.6 jit_solution(1987837016696827304)
XLA Ops:
  2.3 1.1 copy-done.2
  3.4 1.1 copy-done.3
  4.6 1.0 copy-done.4
  6.3 3.0 %collective-permute-start = (bf16[272,768]{1,0:T(8,128)(2,1)S(1)}, bf16[272,768]{1,0:T(8,128)(2,1)S(1)}, u32[]{:S(2)}, u32[]{:S(2)}) collective-permute-start(bf16[272,768]{1,0:T(8,128)(2,1)S(1)} %get-tuple-element.45.refs_0_), channel_id=1, source_target_pairs={{0,4},{1,3},{2,6},{3,1},{4,0},{5,7},{6,2},{7,5},{8,12},{9,11},{10,... | collective-permute-start | bytes 1253384 | tf_op jit(solution)/shard_map/ppermute | solution.py:119
  9.3 1.5 collective-permute-start.1
  10.8 2.6 %collective-permute-start.2 = (bf16[128,768]{1,0:T(8,128)(2,1)S(1)}, bf16[128,768]{1,0:T(8,128)(2,1)S(1)}, u32[]{:S(2)}, u32[]{:S(2)}) collective-permute-start(bf16[128,768]{1,0:T(8,128)(2,1)S(1)} %get-tuple-element.46.refs_2_), channel_id=1, source_target_pairs={{0,16},{1,17},{2,18},{3,19},{4,20},{5,21},{6,22},{7,23},{8,24},{9,... | collective-permute-start | bytes 589832 | tf_op jit(solution)/shard_map/ppermute | solution.py:119
  13.4 2.5 %gather.2.refs_5_.refs_3_ = bf16[3,512,768]{2,1,0:T(8,128)(2,1)S(1)} custom-call(s32[4]{0:T(128)S(1)} %pad_add_fusion.pos_ref, bf16[272,768]{1,0:T(8,128)(2,1)S(1)} %get-tuple-element.45.refs_0_, bf16[272,768]{1,0:T(8,128)(2,1)S(1)} %get-tuple-element.47.refs_1_, bf16[128,768]{1,0:T(8,128)(2,1)S(1)} %get-tuple-element.46.refs_2_), custom_call_target="tpu_custom_call" | custom-call | flops 1000 | bytes 1000 | tf_op jit(solution)/shard_map/gather/pallas_call | solution.py:47
  15.9 6.1 %collective-permute-done.2.refs_3_ = bf16[128,768]{1,0:T(8,128)(2,1)S(1)} collective-permute-done((bf16[128,768]{1,0:T(8,128)(2,1)S(1)}, bf16[128,768]{1,0:T(8,128)(2,1)S(1)}, u32[]{:S(2)}, u32[]{:S(2)}) %collective-permute-start.2) | collective-permute-done | bytes 196640 | tf_op jit(solution)/shard_map/ppermute | solution.py:119
  23.3 1.8 %collective-permute-done.4.refs_1_.refs_3_ = bf16[544,768]{1,0:T(8,128)(2,1)S(1)} collective-permute-done((bf16[544,768]{1,0:T(8,128)(2,1)S(1)}, bf16[544,768]{1,0:T(8,128)(2,1)S(1)}, u32[]{:S(2)}, u32[]{:S(2)}) %collective-permute-start.4) | collective-permute-done | bytes 835616 | tf_op jit(solution)/shard_map/ppermute | solution.py:119
  25.1 3.7 %gather.3.refs_1_.refs_4_ = bf16[3,1024,768]{2,1,0:T(8,128)(2,1)S(1)} custom-call(s32[4]{0:T(128)S(1)} %pad_add_fusion.pos_ref, bf16[272,768]{1,0:T(8,128)(2,1)S(1)} %collective-permute-done.refs_0_.refs_1_, bf16[544,768]{1,0:T(8,128)(2,1)S(1)} %collective-permute-done.4.refs_1_.refs_3_, bf16[272,768]{1,0:T(8,128)(2,1)S(1)} %get-tuple-element.48.refs_2_.refs_4_.refs_0_, ...), custom_call_target="tpu_custom_call" | custom-call | flops 1000 | bytes 1000 | tf_op jit(solution)/shard_map/gather/pallas_call | solution.py:47
  28.8 2.0 %collective-permute-done.3.refs_0_ = bf16[272,768]{1,0:T(8,128)(2,1)S(1)} collective-permute-done((bf16[272,768]{1,0:T(8,128)(2,1)S(1)}, bf16[272,768]{1,0:T(8,128)(2,1)S(1)}, u32[]{:S(2)}, u32[]{:S(2)}) %collective-permute-start.3) | collective-permute-done | bytes 417824 | tf_op jit(solution)/shard_map/ppermute | solution.py:119
  32.2 8.4 %aggregate_near.1.refs_2_ = f32[3,1024,768]{2,1,0:T(8,128)S(1)} custom-call(s32[4]{0:T(128)S(1)} %pad_add_fusion.pos_ref, bf16[272,768]{1,0:T(8,128)(2,1)S(1)} %get-tuple-element.45.refs_0_, bf16[272,768]{1,0:T(8,128)(2,1)S(1)} %collective-permute-done.refs_0_.refs_1_, bf16[272,768]{1,0:T(8,128)(2,1)S(1)} %get-tuple-element.48.refs_2_.refs_4_.refs_0_, ...), custom_call_target="tpu_custom_call" | custom-call | flops 1000 | bytes 1000 | tf_op jit(solution)/shard_map/aggregate_near/pallas_call | solution.py:47
  40.7 2.3 %collective-permute-done.6.refs_1_ = bf16[256,768]{1,0:T(8,128)(2,1)S(1)} collective-permute-done((bf16[256,768]{1,0:T(8,128)(2,1)S(1)}, bf16[256,768]{1,0:T(8,128)(2,1)S(1)}, u32[]{:S(2)}, u32[]{:S(2)}) %collective-permute-start.6) | collective-permute-done | bytes 393248 | tf_op jit(solution)/shard_map/ppermute | solution.py:119
  43.7 5.1 %aggregate.1.refs_0_.refs_3_ = bf16[3,1024,768]{2,1,0:T(8,128)(2,1)S(1)} custom-call(s32[4]{0:T(128)S(1)} %pad_add_fusion.pos_ref, bf16[272,768]{1,0:T(8,128)(2,1)S(1)} %step.13.refs_6_.refs_0_, bf16[272,768]{1,0:T(8,128)(2,1)S(1)} %collective-permute-done.5.refs_3_.refs_1_, f32[3,1024,768]{2,1,0:T(8,128)S(1)} %aggregate_near.1.refs_2_, ...), custom_call_target="tpu_custom_call" | custom-call | flops 1000 | bytes 1000 | tf_op jit(solution)/shard_map/aggregate/pallas_call | solution.py:47
  48.9 2.5 %weight_terms.4.refs_2_ = bf16[3,384,384]{2,1,0:T(8,128)(2,1)S(1)} custom-call(s32[4]{0:T(128)S(1)} %pad_add_fusion.pos_ref, bf16[3,1024,768]{2,1,0:T(8,128)(2,1)S(1)} %aggregate.1.refs_0_.refs_3_, bf16[512,768]{1,0:T(8,128)(2,1)S(1)} %step.14.refs_3_.refs_1_, bf16[512,768]{1,0:T(8,128)(2,1)S(1)} %collective-permute-done.7.refs_2_, ...), custom_call_target="tpu_custom_call" | custom-call | flops 1000 | bytes 1000 | tf_op jit(solution)/shard_map/weight_terms/pallas_call | solution.py:47
  52.0 2.5 %output_terms.2.refs_2_.refs_6_ = bf16[512,768]{1,0:T(8,128)(2,1)S(1)} custom-call(s32[4]{0:T(128)S(1)} %pad_add_fusion.pos_ref, bf16[3,1024,768]{2,1,0:T(8,128)(2,1)S(1)} %aggregate.1.refs_0_.refs_3_, bf16[3,768,768]{2,1,0:T(8,128)(2,1)S(1)} %copy-done, bf16[3,384,384]{2,1,0:T(8,128)(2,1)S(1)} %weight_terms.4.refs_2_), custom_call_target="tpu_custom_call" | custom-call | flops 1000 | bytes 1000 | tf_op jit(solution)/shard_map/output_terms/pallas_call | solution.py:47
  54.5 2.5 %output_terms.3.refs_3_.refs_8_ = f32[512,768]{1,0:T(8,128)S(1)} custom-call(s32[4]{0:T(128)S(1)} %pad_add_fusion.pos_ref, bf16[3,1024,768]{2,1,0:T(8,128)(2,1)S(1)} %aggregate.1.refs_0_.refs_3_, bf16[3,768,768]{2,1,0:T(8,128)(2,1)S(1)} %copy-done, bf16[512,768]{1,0:T(8,128)(2,1)S(1)} %output_terms.2.refs_2_.refs_6_), custom_call_target="tpu_custom_call" | custom-call | flops 1000 | bytes 1000 | tf_op jit(solution)/shard_map/output_terms/pallas_call | solution.py:47
  57.1 2.5 %weight_terms.5.refs_3_ = bf16[3,384,384]{2,1,0:T(8,128)(2,1)S(1)} custom-call(s32[4]{0:T(128)S(1)} %pad_add_fusion.pos_ref, bf16[3,1024,768]{2,1,0:T(8,128)(2,1)S(1)} %aggregate.1.refs_0_.refs_3_, bf16[512,768]{1,0:T(8,128)(2,1)S(1)} %step.14.refs_3_.refs_1_, bf16[512,768]{1,0:T(8,128)(2,1)S(1)} %collective-permute-done.7.refs_2_, ...), custom_call_target="tpu_custom_call" | custom-call | flops 1000 | bytes 1000 | tf_op jit(solution)/shard_map/weight_terms/pallas_call | solution.py:47
  59.6 1.6 collective-permute-start.8
  61.2 2.5 %weight_terms.6.refs_3_.refs_0_ = f32[3,384,384]{2,1,0:T(8,128)S(1)} custom-call(s32[4]{0:T(128)S(1)} %pad_add_fusion.pos_ref, bf16[3,1024,768]{2,1,0:T(8,128)(2,1)S(1)} %aggregate.1.refs_0_.refs_3_, bf16[512,768]{1,0:T(8,128)(2,1)S(1)} %step.14.refs_3_.refs_1_, bf16[512,768]{1,0:T(8,128)(2,1)S(1)} %collective-permute-done.7.refs_2_, ...), custom_call_target="tpu_custom_call" | custom-call | flops 1000 | bytes 1000 | tf_op jit(solution)/shard_map/weight_terms/pallas_call | solution.py:47
  63.7 2.5 %weight_terms.7.refs_2_.refs_0_ = f32[3,384,384]{2,1,0:T(8,128)S(1)} custom-call(s32[4]{0:T(128)S(1)} %pad_add_fusion.pos_ref, bf16[3,1024,768]{2,1,0:T(8,128)(2,1)S(1)} %aggregate.1.refs_0_.refs_3_, bf16[512,768]{1,0:T(8,128)(2,1)S(1)} %step.14.refs_3_.refs_1_, bf16[512,768]{1,0:T(8,128)(2,1)S(1)} %collective-permute-done.7.refs_2_, ...), custom_call_target="tpu_custom_call" | custom-call | flops 1000 | bytes 1000 | tf_op jit(solution)/shard_map/weight_terms/pallas_call | solution.py:47
  67.6 8.6 %feature_terms.4 = (f32[256,768]{1,0:T(8,128)S(1)}, bf16[256,768]{1,0:T(8,128)(2,1)S(1)}) custom-call(s32[4]{0:T(128)S(1)} %pad_add_fusion.pos_ref, bf16[272,768]{1,0:T(8,128)(2,1)S(1)} %get-tuple-element.48.refs_2_.refs_4_.refs_0_, bf16[512,768]{1,0:T(8,128)(2,1)S(1)} %step.14.refs_3_.refs_1_, bf16[512,768]{1,0:T(8,128)(2,1)S(1)} %collective-permute-done.7.refs_2_, ...), custom_call_target="tpu_custom_call" | custom-call | flops 1000 | bytes 1000 | tf_op jit(solution)/shard_map/feature_terms/pallas_call | solution.py:47
  76.2 2.1 %collective-permute-done.8.refs_1_ = bf16[3,384,384]{2,1,0:T(8,128)(2,1)S(1)} collective-permute-done((bf16[3,384,384]{2,1,0:T(8,128)(2,1)S(1)}, bf16[3,384,384]{2,1,0:T(8,128)(2,1)S(1)}, u32[]{:S(2)}, u32[]{:S(2)}) %collective-permute-start.8) | collective-permute-done | bytes 884768 | tf_op jit(solution)/shard_map/ppermute | solution.py:119
  80.4 8.5 %feature_terms.5 = (f32[256,768]{1,0:T(8,128)S(1)}, bf16[256,768]{1,0:T(8,128)(2,1)S(1)}) custom-call(s32[4]{0:T(128)S(1)} %pad_add_fusion.pos_ref, bf16[272,768]{1,0:T(8,128)(2,1)S(1)} %step.13.refs_6_.refs_0_, bf16[512,768]{1,0:T(8,128)(2,1)S(1)} %step.14.refs_3_.refs_1_, bf16[512,768]{1,0:T(8,128)(2,1)S(1)} %collective-permute-done.7.refs_2_, ...), custom_call_target="tpu_custom_call" | custom-call | flops 1000 | bytes 1000 | tf_op jit(solution)/shard_map/feature_terms/pallas_call | solution.py:47
  89.7 3.4 %collective-permute-start.13 = (bf16[3,96,384]{2,1,0:T(8,128)(2,1)S(1)}, bf16[3,96,384]{2,1,0:T(8,128)(2,1)S(1)}, u32[]{:S(2)}, u32[]{:S(2)}) collective-permute-start(bf16[3,96,384]{2,1,0:T(8,128)(2,1)S(1)} %get-tuple-element.61.refs_4_.refs_0_), channel_id=1, source_target_pairs={{0,16},{1,17},{2,18},{3,19},{4,20},{5,21},{6,22},{7,23},{8,24},{9,... | collective-permute-start | bytes 663560 | tf_op jit(solution)/shard_map/ppermute | solution.py:119
  93.4 8.5 %feature_terms.6 = (f32[256,768]{1,0:T(8,128)S(1)}, bf16[256,768]{1,0:T(8,128)(2,1)S(1)}) custom-call(s32[4]{0:T(128)S(1)} %pad_add_fusion.pos_ref, bf16[272,768]{1,0:T(8,128)(2,1)S(1)} %collective-permute-done.refs_0_.refs_1_, bf16[512,768]{1,0:T(8,128)(2,1)S(1)} %step.14.refs_3_.refs_1_, bf16[512,768]{1,0:T(8,128)(2,1)S(1)} %collective-permute-done.7.refs_2_, ...), custom_call_target="tpu_custom_call" | custom-call | flops 1000 | bytes 1000 | tf_op jit(solution)/shard_map/feature_terms/pallas_call | solution.py:47
  101.9 2.1 %collective-permute-done.13.refs_1_ = bf16[3,96,384]{2,1,0:T(8,128)(2,1)S(1)} collective-permute-done((bf16[3,96,384]{2,1,0:T(8,128)(2,1)S(1)}, bf16[3,96,384]{2,1,0:T(8,128)(2,1)S(1)}, u32[]{:S(2)}, u32[]{:S(2)}) %collective-permute-start.13) | collective-permute-done | bytes 221216 | tf_op jit(solution)/shard_map/ppermute | solution.py:119
  104.0 1.2 collective-permute-done.14.refs_3_
  105.2 0.8 step.18
  106.0 0.8 collective-permute-start.19
  107.4 1.1 collective-permute-start.17
  108.5 8.5 %feature_terms.7 = (f32[256,768]{1,0:T(8,128)S(1)}, bf16[256,768]{1,0:T(8,128)(2,1)S(1)}) custom-call(s32[4]{0:T(128)S(1)} %pad_add_fusion.pos_ref, bf16[272,768]{1,0:T(8,128)(2,1)S(1)} %get-tuple-element.45.refs_0_, bf16[512,768]{1,0:T(8,128)(2,1)S(1)} %step.14.refs_3_.refs_1_, bf16[512,768]{1,0:T(8,128)(2,1)S(1)} %collective-permute-done.7.refs_2_, ...), custom_call_target="tpu_custom_call" | custom-call | flops 1000 | bytes 1000 | tf_op jit(solution)/shard_map/feature_terms/pallas_call | solution.py:47
  117.7 2.8 %collective-permute-done.17.refs_3_ = bf16[3,96,384]{2,1,0:T(8,128)(2,1)S(1)} collective-permute-done((bf16[3,96,384]{2,1,0:T(8,128)(2,1)S(1)}, bf16[3,96,384]{2,1,0:T(8,128)(2,1)S(1)}, u32[]{:S(2)}, u32[]{:S(2)}) %collective-permute-start.17) | collective-permute-done | bytes 221216 | tf_op jit(solution)/shard_map/ppermute | solution.py:119
  120.5 0.9 step.19
  121.5 1.3 collective-permute-start.21
  123.5 8.3 %collective-permute-done.22.refs_3_ = bf16[288,384]{1,0:T(8,128)(2,1)S(1)} collective-permute-done((bf16[288,384]{1,0:T(8,128)(2,1)S(1)}, bf16[288,384]{1,0:T(8,128)(2,1)S(1)}, u32[]{:S(2)}, u32[]{:S(2)}) %collective-permute-start.22) | collective-permute-done | bytes 221216 | tf_op jit(solution)/shard_map/ppermute | solution.py:119
  131.8 2.2 %collective-permute-done.24.refs_7_ = bf16[256,768]{1,0:T(8,128)(2,1)S(1)} collective-permute-done((bf16[256,768]{1,0:T(8,128)(2,1)S(1)}, bf16[256,768]{1,0:T(8,128)(2,1)S(1)}, u32[]{:S(2)}, u32[]{:S(2)}) %collective-permute-start.24) | collective-permute-done | bytes 393248 | tf_op jit(solution)/shard_map/ppermute | solution.py:119
  134.0 0.8 step.20
  134.9 1.3 collective-permute-start.25
  136.2 1.5 collective-permute-start.30
  137.7 7.8 %collective-permute-done.27.refs_5_ = bf16[256,768]{1,0:T(8,128)(2,1)S(1)} collective-permute-done((bf16[256,768]{1,0:T(8,128)(2,1)S(1)}, bf16[256,768]{1,0:T(8,128)(2,1)S(1)}, u32[]{:S(2)}, u32[]{:S(2)}) %collective-permute-start.27) | collective-permute-done | bytes 393248 | tf_op jit(solution)/shard_map/ppermute | solution.py:119
  145.5 1.7 %collective-permute-done.25.refs_1_ = bf16[576,384]{1,0:T(8,128)(2,1)S(1)} collective-permute-done((bf16[576,384]{1,0:T(8,128)(2,1)S(1)}, bf16[576,384]{1,0:T(8,128)(2,1)S(1)}, u32[]{:S(2)}, u32[]{:S(2)}) %collective-permute-start.25) | collective-permute-done | bytes 442400 | tf_op jit(solution)/shard_map/ppermute | solution.py:119
  147.2 1.6 step.21
  148.8 1.0 collective-permute-start.31
  149.8 8.5 %collective-permute-done.28.refs_1_ = bf16[128,768]{1,0:T(8,128)(2,1)S(1)} collective-permute-done((bf16[128,768]{1,0:T(8,128)(2,1)S(1)}, bf16[128,768]{1,0:T(8,128)(2,1)S(1)}, u32[]{:S(2)}, u32[]{:S(2)}) %collective-permute-start.28) | collective-permute-done | bytes 196640 | tf_op jit(solution)/shard_map/ppermute | solution.py:119
  159.0 1.4 collective-permute-done.29.refs_1_
  160.5 1.3 step.23
  161.9 3.8 %assemble.1 = f32[3,768,768]{2,1,0:T(8,128)} custom-call(s32[4]{0:T(128)S(1)} %pad_add_fusion.pos_ref, bf16[1152,384]{1,0:T(8,128)(2,1)S(1)} %get-tuple-element.82.refs_6_.refs_0_, bf16[1152,384]{1,0:T(8,128)(2,1)S(1)} %collective-permute-done.30.refs_1_, bf16[1152,384]{1,0:T(8,128)(2,1)S(1)} %get-tuple-element.85.refs_2_, ...), custom_call_target="tpu_custom_call" | custom-call | flops 1000 | bytes 1000 | tf_op jit(solution)/shard_map/assemble/pallas_call | solution.py:47
  (61 shorter events, 13.6 us)
Async XLA Ops:
  2.3 1.1 copy-start.2
  3.4 1.1 copy-start.3
  4.5 1.0 copy-start.4
  6.3 15.7 %collective-permute-start = (bf16[272,768]{1,0:T(8,128)(2,1)S(1)}, bf16[272,768]{1,0:T(8,128)(2,1)S(1)}, u32[]{:S(2)}, u32[]{:S(2)}) collective-permute-start(bf16[272,768]{1,0:T(8,128)(2,1)S(1)} %get-tuple-element.45.refs_0_), channel_id=1, source_target_pairs={{0,4},{1,3},{2,6},{3,1},{4,0},{5,7},{6,2},{7,5},{8,12},{9,11},{10,... | collective-permute-start | bytes 1253384 | tf_op jit(solution)/shard_map/ppermute | solution.py:119
  9.3 12.7 %collective-permute-start.1 = (bf16[272,768]{1,0:T(8,128)(2,1)S(1)}, bf16[272,768]{1,0:T(8,128)(2,1)S(1)}, u32[]{:S(2)}, u32[]{:S(2)}) collective-permute-start(bf16[272,768]{1,0:T(8,128)(2,1)S(1)} %get-tuple-element.45.refs_0_), channel_id=1, source_target_pairs={{0,2},{1,5},{2,0},{3,7},{4,6},{5,1},{6,4},{7,3},{8,10},{9,13},{10,... | collective-permute-start | bytes 1253384 | tf_op jit(solution)/shard_map/ppermute | solution.py:119
  10.8 11.2 %collective-permute-start.2 = (bf16[128,768]{1,0:T(8,128)(2,1)S(1)}, bf16[128,768]{1,0:T(8,128)(2,1)S(1)}, u32[]{:S(2)}, u32[]{:S(2)}) collective-permute-start(bf16[128,768]{1,0:T(8,128)(2,1)S(1)} %get-tuple-element.46.refs_2_), channel_id=1, source_target_pairs={{0,16},{1,17},{2,18},{3,19},{4,20},{5,21},{6,22},{7,23},{8,24},{9,... | collective-permute-start | bytes 589832 | tf_op jit(solution)/shard_map/ppermute | solution.py:119
  22.7 2.4 %collective-permute-start.4 = (bf16[544,768]{1,0:T(8,128)(2,1)S(1)}, bf16[544,768]{1,0:T(8,128)(2,1)S(1)}, u32[]{:S(2)}, u32[]{:S(2)}) collective-permute-start(bf16[544,768]{1,0:T(8,128)(2,1)S(1)} %get-tuple-element.49), channel_id=1, source_target_pairs={{0,1},{1,0},{2,3},{3,2},{4,5},{5,4},{6,7},{7,6},{8,9},{9,8},{10,11... | collective-permute-start | bytes 2506760 | tf_op jit(solution)/shard_map/ppermute | solution.py:119
  22.7 8.1 %collective-permute-start.3 = (bf16[272,768]{1,0:T(8,128)(2,1)S(1)}, bf16[272,768]{1,0:T(8,128)(2,1)S(1)}, u32[]{:S(2)}, u32[]{:S(2)}) collective-permute-start(bf16[272,768]{1,0:T(8,128)(2,1)S(1)} %get-tuple-element.48.refs_2_.refs_4_.refs_0_), channel_id=1, source_target_pairs={{0,4},{1,3},{2,6},{3,1},{4,0},{5,7},{6,2},{7,5},{8,12},{9,11},{10,... | collective-permute-start | bytes 1253384 | tf_op jit(solution)/shard_map/ppermute | solution.py:119
  28.8 3.4 %copy-start.1 = (bf16[3,256,768]{2,1,0:T(8,128)(2,1)S(1)}, bf16[3,256,768]{2,1,0:T(8,128)(2,1)}, u32[]{:S(2)}) copy-start(bf16[3,256,768]{2,1,0:T(8,128)(2,1)} %refs_5_.1) | copy-start | bytes 3538948
  31.4 11.6 %collective-permute-start.5 = (bf16[272,768]{1,0:T(8,128)(2,1)S(1)}, bf16[272,768]{1,0:T(8,128)(2,1)S(1)}, u32[]{:S(2)}, u32[]{:S(2)}) collective-permute-start(bf16[272,768]{1,0:T(8,128)(2,1)S(1)} %step.13.refs_6_.refs_0_), channel_id=1, source_target_pairs={{0,1},{1,0},{2,3},{3,2},{4,5},{5,4},{6,7},{7,6},{8,9},{9,8},{10,11... | collective-permute-start | bytes 1253384 | tf_op jit(solution)/shard_map/ppermute | solution.py:119
  31.5 11.5 %collective-permute-start.6 = (bf16[256,768]{1,0:T(8,128)(2,1)S(1)}, bf16[256,768]{1,0:T(8,128)(2,1)S(1)}, u32[]{:S(2)}, u32[]{:S(2)}) collective-permute-start(bf16[256,768]{1,0:T(8,128)(2,1)S(1)} %get-tuple-element.50.refs_0_), channel_id=1, source_target_pairs={{0,8},{1,9},{2,10},{3,11},{4,12},{5,13},{6,14},{7,15},{8,0},{9,1},... | collective-permute-start | bytes 1179656 | tf_op jit(solution)/shard_map/ppermute | solution.py:119
  43.6 5.2 %collective-permute-start.7 = (bf16[512,768]{1,0:T(8,128)(2,1)S(1)}, bf16[512,768]{1,0:T(8,128)(2,1)S(1)}, u32[]{:S(2)}, u32[]{:S(2)}) collective-permute-start(bf16[512,768]{1,0:T(8,128)(2,1)S(1)} %step.14.refs_3_.refs_1_), channel_id=1, source_target_pairs={{0,1},{1,0},{2,3},{3,2},{4,5},{5,4},{6,7},{7,6},{8,9},{9,8},{10,11... | collective-permute-start | bytes 2359304 | tf_op jit(solution)/shard_map/ppermute | solution.py:119
  48.8 3.1 %copy-start = (bf16[3,768,768]{2,1,0:T(8,128)(2,1)S(1)}, bf16[3,768,768]{2,1,0:T(8,128)(2,1)}, u32[]{:S(2)}) copy-start(bf16[3,768,768]{2,1,0:T(8,128)(2,1)} %refs_3_.9) | copy-start | bytes 10616836
  51.4 14.9 %collective-permute-start.9 = (bf16[3,384,384]{2,1,0:T(8,128)(2,1)S(1)}, bf16[3,384,384]{2,1,0:T(8,128)(2,1)S(1)}, u32[]{:S(2)}, u32[]{:S(2)}) collective-permute-start(bf16[3,384,384]{2,1,0:T(8,128)(2,1)S(1)} %weight_terms.4.refs_2_), channel_id=1, source_target_pairs={{0,4},{1,3},{2,6},{3,1},{4,0},{5,7},{6,2},{7,5},{8,12},{9,11},{10,... | collective-permute-start | bytes 2654216 | tf_op jit(solution)/shard_map/ppermute | solution.py:119
  59.6 18.7 %collective-permute-start.8 = (bf16[3,384,384]{2,1,0:T(8,128)(2,1)S(1)}, bf16[3,384,384]{2,1,0:T(8,128)(2,1)S(1)}, u32[]{:S(2)}, u32[]{:S(2)}) collective-permute-start(bf16[3,384,384]{2,1,0:T(8,128)(2,1)S(1)} %weight_terms.5.refs_3_), channel_id=1, source_target_pairs={{0,4},{1,3},{2,6},{3,1},{4,0},{5,7},{6,2},{7,5},{8,12},{9,11},{10,... | collective-permute-start | bytes 2654216 | tf_op jit(solution)/shard_map/ppermute | solution.py:119
  67.0 11.3 %collective-permute-start.10 = (bf16[3,192,384]{2,1,0:T(8,128)(2,1)S(1)}, bf16[3,192,384]{2,1,0:T(8,128)(2,1)S(1)}, u32[]{:S(2)}, u32[]{:S(2)}) collective-permute-start(bf16[3,192,384]{2,1,0:T(8,128)(2,1)S(1)} %get-tuple-element.52), channel_id=1, source_target_pairs={{0,2},{1,5},{2,0},{3,7},{4,6},{5,1},{6,4},{7,3},{8,10},{9,13},{10,... | collective-permute-start | bytes 1327112 | tf_op jit(solution)/shard_map/ppermute | solution.py:119
  79.0 9.8 %collective-permute-start.12 = (bf16[3,192,384]{2,1,0:T(8,128)(2,1)S(1)}, bf16[3,192,384]{2,1,0:T(8,128)(2,1)S(1)}, u32[]{:S(2)}, u32[]{:S(2)}) collective-permute-start(bf16[3,192,384]{2,1,0:T(8,128)(2,1)S(1)} %get-tuple-element.57), channel_id=1, source_target_pairs={{0,2},{1,5},{2,0},{3,7},{4,6},{5,1},{6,4},{7,3},{8,10},{9,13},{10,... | collective-permute-start | bytes 1327112 | tf_op jit(solution)/shard_map/ppermute | solution.py:119
  79.7 9.2 %collective-permute-start.11 = (bf16[3,96,384]{2,1,0:T(8,128)(2,1)S(1)}, bf16[3,96,384]{2,1,0:T(8,128)(2,1)S(1)}, u32[]{:S(2)}, u32[]{:S(2)}) collective-permute-start(bf16[3,96,384]{2,1,0:T(8,128)(2,1)S(1)} %get-tuple-element.55), channel_id=1, source_target_pairs={{0,8},{1,9},{2,10},{3,11},{4,12},{5,13},{6,14},{7,15},{8,0},{9,1},... | collective-permute-start | bytes 663560 | tf_op jit(solution)/shard_map/ppermute | solution.py:119
  89.6 15.6 %collective-permute-start.15 = (bf16[512,768]{1,0:T(8,128)(2,1)S(1)}, bf16[512,768]{1,0:T(8,128)(2,1)S(1)}, u32[]{:S(2)}, u32[]{:S(2)}) collective-permute-start(bf16[512,768]{1,0:T(8,128)(2,1)S(1)} %get-tuple-element.65), channel_id=1, source_target_pairs={{0,1},{1,0},{2,3},{3,2},{4,5},{5,4},{6,7},{7,6},{8,9},{9,8},{10,11... | collective-permute-start | bytes 2359304 | tf_op jit(solution)/shard_map/ppermute | solution.py:119
  89.7 14.3 %collective-permute-start.13 = (bf16[3,96,384]{2,1,0:T(8,128)(2,1)S(1)}, bf16[3,96,384]{2,1,0:T(8,128)(2,1)S(1)}, u32[]{:S(2)}, u32[]{:S(2)}) collective-permute-start(bf16[3,96,384]{2,1,0:T(8,128)(2,1)S(1)} %get-tuple-element.61.refs_4_.refs_0_), channel_id=1, source_target_pairs={{0,16},{1,17},{2,18},{3,19},{4,20},{5,21},{6,22},{7,23},{8,24},{9,... | collective-permute-start | bytes 663560 | tf_op jit(solution)/shard_map/ppermute | solution.py:119
  93.1 12.1 %collective-permute-start.14 = (bf16[3,96,384]{2,1,0:T(8,128)(2,1)S(1)}, bf16[3,96,384]{2,1,0:T(8,128)(2,1)S(1)}, u32[]{:S(2)}, u32[]{:S(2)}) collective-permute-start(bf16[3,96,384]{2,1,0:T(8,128)(2,1)S(1)} %get-tuple-element.63), channel_id=1, source_target_pairs={{0,8},{1,9},{2,10},{3,11},{4,12},{5,13},{6,14},{7,15},{8,0},{9,1},... | collective-permute-start | bytes 663560 | tf_op jit(solution)/shard_map/ppermute | solution.py:119
  93.4 23.6 %collective-permute-start.20 = (bf16[512,768]{1,0:T(8,128)(2,1)S(1)}, bf16[512,768]{1,0:T(8,128)(2,1)S(1)}, u32[]{:S(2)}, u32[]{:S(2)}) collective-permute-start(bf16[512,768]{1,0:T(8,128)(2,1)S(1)} %get-tuple-element.72), channel_id=1, source_target_pairs={{0,1},{1,0},{2,3},{3,2},{4,5},{5,4},{6,7},{7,6},{8,9},{9,8},{10,11... | collective-permute-start | bytes 2359304 | tf_op jit(solution)/shard_map/ppermute | solution.py:119
  106.0 14.5 %collective-permute-start.19 = (bf16[512,768]{1,0:T(8,128)(2,1)S(1)}, bf16[512,768]{1,0:T(8,128)(2,1)S(1)}, u32[]{:S(2)}, u32[]{:S(2)}) collective-permute-start(bf16[512,768]{1,0:T(8,128)(2,1)S(1)} %get-tuple-element.70), channel_id=1, source_target_pairs={{0,4},{1,3},{2,6},{3,1},{4,0},{5,7},{6,2},{7,5},{8,12},{9,11},{10,... | collective-permute-start | bytes 2359304 | tf_op jit(solution)/shard_map/ppermute | solution.py:119
  106.8 13.7 %collective-permute-start.18 = (bf16[256,768]{1,0:T(8,128)(2,1)S(1)}, bf16[256,768]{1,0:T(8,128)(2,1)S(1)}, u32[]{:S(2)}, u32[]{:S(2)}) collective-permute-start(bf16[256,768]{1,0:T(8,128)(2,1)S(1)} %get-tuple-element.69), channel_id=1, source_target_pairs={{0,1},{1,0},{2,3},{3,2},{4,5},{5,4},{6,7},{7,6},{8,9},{9,8},{10,11... | collective-permute-start | bytes 1179656 | tf_op jit(solution)/shard_map/ppermute | solution.py:119
  106.8 10.9 %collective-permute-start.16 = (bf16[288,384]{1,0:T(8,128)(2,1)S(1)}, bf16[288,384]{1,0:T(8,128)(2,1)S(1)}, u32[]{:S(2)}, u32[]{:S(2)}) collective-permute-start(bf16[288,384]{1,0:T(8,128)(2,1)S(1)} %bitcast.14), channel_id=1, source_target_pairs={{0,8},{1,9},{2,10},{3,11},{4,12},{5,13},{6,14},{7,15},{8,0},{9,1},... | collective-permute-start | bytes 663560 | tf_op jit(solution)/shard_map/ppermute | solution.py:119
  107.4 13.1 %collective-permute-start.17 = (bf16[3,96,384]{2,1,0:T(8,128)(2,1)S(1)}, bf16[3,96,384]{2,1,0:T(8,128)(2,1)S(1)}, u32[]{:S(2)}, u32[]{:S(2)}) collective-permute-start(bf16[3,96,384]{2,1,0:T(8,128)(2,1)S(1)} %get-tuple-element.68.refs_2_), channel_id=1, source_target_pairs={{0,16},{1,17},{2,18},{3,19},{4,20},{5,21},{6,22},{7,23},{8,24},{9,... | collective-permute-start | bytes 663560 | tf_op jit(solution)/shard_map/ppermute | solution.py:119
  121.5 12.6 %collective-permute-start.21 = (bf16[576,384]{1,0:T(8,128)(2,1)S(1)}, bf16[576,384]{1,0:T(8,128)(2,1)S(1)}, u32[]{:S(2)}, u32[]{:S(2)}) collective-permute-start(bf16[576,384]{1,0:T(8,128)(2,1)S(1)} %get-tuple-element.74.refs_0_.refs_8_), channel_id=1, source_target_pairs={{0,2},{1,5},{2,0},{3,7},{4,6},{5,1},{6,4},{7,3},{8,10},{9,13},{10,... | collective-permute-start | bytes 1327112 | tf_op jit(solution)/shard_map/ppermute | solution.py:119
  122.8 9.1 %collective-permute-start.23 = (bf16[256,768]{1,0:T(8,128)(2,1)S(1)}, bf16[256,768]{1,0:T(8,128)(2,1)S(1)}, u32[]{:S(2)}, u32[]{:S(2)}) collective-permute-start(bf16[256,768]{1,0:T(8,128)(2,1)S(1)} %get-tuple-element.76), channel_id=1, source_target_pairs={{0,1},{1,0},{2,3},{3,2},{4,5},{5,4},{6,7},{7,6},{8,9},{9,8},{10,11... | collective-permute-start | bytes 1179656 | tf_op jit(solution)/shard_map/ppermute | solution.py:119
  122.8 11.3 %collective-permute-start.24 = (bf16[256,768]{1,0:T(8,128)(2,1)S(1)}, bf16[256,768]{1,0:T(8,128)(2,1)S(1)}, u32[]{:S(2)}, u32[]{:S(2)}) collective-permute-start(bf16[256,768]{1,0:T(8,128)(2,1)S(1)} %get-tuple-element.77), channel_id=1, source_target_pairs={{0,2},{1,5},{2,0},{3,7},{4,6},{5,1},{6,4},{7,3},{8,10},{9,13},{10,... | collective-permute-start | bytes 1179656 | tf_op jit(solution)/shard_map/ppermute | solution.py:119
  123.5 8.3 %collective-permute-start.22 = (bf16[288,384]{1,0:T(8,128)(2,1)S(1)}, bf16[288,384]{1,0:T(8,128)(2,1)S(1)}, u32[]{:S(2)}, u32[]{:S(2)}) collective-permute-start(bf16[288,384]{1,0:T(8,128)(2,1)S(1)} %bitcast.16), channel_id=1, source_target_pairs={{0,8},{1,9},{2,10},{3,11},{4,12},{5,13},{6,14},{7,15},{8,0},{9,1},... | collective-permute-start | bytes 663560 | tf_op jit(solution)/shard_map/ppermute | solution.py:119
  134.9 12.3 %collective-permute-start.25 = (bf16[576,384]{1,0:T(8,128)(2,1)S(1)}, bf16[576,384]{1,0:T(8,128)(2,1)S(1)}, u32[]{:S(2)}, u32[]{:S(2)}) collective-permute-start(bf16[576,384]{1,0:T(8,128)(2,1)S(1)} %get-tuple-element.78.refs_0_), channel_id=1, source_target_pairs={{0,2},{1,5},{2,0},{3,7},{4,6},{5,1},{6,4},{7,3},{8,10},{9,13},{10,... | collective-permute-start | bytes 1327112 | tf_op jit(solution)/shard_map/ppermute | solution.py:119
  136.2 9.3 %collective-permute-start.27 = (bf16[256,768]{1,0:T(8,128)(2,1)S(1)}, bf16[256,768]{1,0:T(8,128)(2,1)S(1)}, u32[]{:S(2)}, u32[]{:S(2)}) collective-permute-start(bf16[256,768]{1,0:T(8,128)(2,1)S(1)} %get-tuple-element.81), channel_id=1, source_target_pairs={{0,8},{1,9},{2,10},{3,11},{4,12},{5,13},{6,14},{7,15},{8,0},{9,1},... | collective-permute-start | bytes 1179656 | tf_op jit(solution)/shard_map/ppermute | solution.py:119
  136.2 9.3 %collective-permute-start.26 = (bf16[256,768]{1,0:T(8,128)(2,1)S(1)}, bf16[256,768]{1,0:T(8,128)(2,1)S(1)}, u32[]{:S(2)}, u32[]{:S(2)}) collective-permute-start(bf16[256,768]{1,0:T(8,128)(2,1)S(1)} %get-tuple-element.79.refs_2_), channel_id=1, source_target_pairs={{0,1},{1,0},{2,3},{3,2},{4,5},{5,4},{6,7},{7,6},{8,9},{9,8},{10,11... | collective-permute-start | bytes 1179656 | tf_op jit(solution)/shard_map/ppermute | solution.py:119
  136.2 25.6 %collective-permute-start.30 = (bf16[1152,384]{1,0:T(8,128)(2,1)S(1)}, bf16[1152,384]{1,0:T(8,128)(2,1)S(1)}, u32[]{:S(2)}, u32[]{:S(2)}) collective-permute-start(bf16[1152,384]{1,0:T(8,128)(2,1)S(1)} %get-tuple-element.82.refs_6_.refs_0_), channel_id=1, source_target_pairs={{0,4},{1,3},{2,6},{3,1},{4,0},{5,7},{6,2},{7,5},{8,12},{9,11},{10,... | collective-permute-start | bytes 2654216 | tf_op jit(solution)/shard_map/ppermute | solution.py:119
  148.8 13.0 %collective-permute-start.31 = (bf16[1152,384]{1,0:T(8,128)(2,1)S(1)}, bf16[1152,384]{1,0:T(8,128)(2,1)S(1)}, u32[]{:S(2)}, u32[]{:S(2)}) collective-permute-start(bf16[1152,384]{1,0:T(8,128)(2,1)S(1)} %get-tuple-element.85.refs_2_), channel_id=1, source_target_pairs={{0,4},{1,3},{2,6},{3,1},{4,0},{5,7},{6,2},{7,5},{8,12},{9,11},{10,... | collective-permute-start | bytes 2654216 | tf_op jit(solution)/shard_map/ppermute | solution.py:119
  149.8 8.5 %collective-permute-start.28 = (bf16[128,768]{1,0:T(8,128)(2,1)S(1)}, bf16[128,768]{1,0:T(8,128)(2,1)S(1)}, u32[]{:S(2)}, u32[]{:S(2)}) collective-permute-start(bf16[128,768]{1,0:T(8,128)(2,1)S(1)} %get-tuple-element.84), channel_id=1, source_target_pairs={{0,16},{1,17},{2,18},{3,19},{4,20},{5,21},{6,22},{7,23},{8,24},{9,... | collective-permute-start | bytes 589832 | tf_op jit(solution)/shard_map/ppermute | solution.py:119
  159.0 1.5 collective-permute-start.29

commit v6 on v5

--- a/solution.py
+++ b/solution.py
@@ -12,7 +12,7 @@
 AXES = ("node", "rel")
 DEPTH, SIDE = 4, 2
 CHUNKS = 2
-LIMIT = 24
+LIMIT = 12
 ROUNDS = (
     (((0, 0),), (2,)),
     (((1, 0), (0, 1),), (3,)),
@@ -481,31 +481,35 @@
 
 def assemble_kernel(pos, *refs):
     result = refs[-1]
-    z, y, x, core = pos[0], pos[1], pos[2], pos[3]
-    first = jnp.where(core == 0, y, x)
-    second = jnp.where(core == 0, x, y)
+    second = jnp.where(pos[3] == 0, pos[2], pos[1])
     count = pl.num_programs(0)
-    rows = result.shape[1] // (2 * SIDE * SIDE)
-    for number, ref in enumerate(refs[:-1]):
-        chunk, flip_a = number // 2, number % 2
-        span = ref.shape[1]
-        for index in range(4):
-            flip_b, flip_z = index // 2, index % 2
-            place = ((first ^ flip_a) * 2 + (second ^ flip_b)) * 2 + (z % 2 ^ flip_z)
-            start = (index * count + pl.program_id(0)) * rows
-            result[
-                0, pl.ds(pl.multiple_of(place * rows, 16), rows), chunk * span : (chunk + 1) * span
-            ] = ref[pl.ds(pl.multiple_of(start, 16), rows), :].astype(F32)
+    rows = result.shape[1] // (2 * SIDE)
+    for flip_a in range(2):
+
+        @pl.when(pl.program_id(1) == flip_a)
+        def _():
+            for chunk, ref in enumerate(refs[flip_a:-1:2]):
+                span = ref.shape[1]
+                for index in range(4):
+                    flip_b, flip_z = index // 2, index % 2
+                    place = (second ^ flip_b) * 2 + (pos[0] % 2 ^ flip_z)
+                    start = (index * count + pl.program_id(0)) * rows
+                    result[
+                        0,
+                        pl.ds(pl.multiple_of(place * rows, 16), rows),
+                        chunk * span : (chunk + 1) * span,
+                    ] = ref[pl.ds(pl.multiple_of(start, 16), rows), :].astype(F32)
 
 
 def assemble(pos, pieces, groups, width):
+    half = lambda r, f, pos: (r, jnp.where(pos[3] == 0, pos[1], pos[2]) ^ f, 0)
     return call(
         "assemble",
         assemble_kernel,
         pos,
         [full(piece) for piece in pieces],
-        [out_by_rel(groups, width, width, F32)],
-        grid=(groups,),
+        [((groups, width, width), F32, (1, width // 2, width), half)],
+        grid=(groups, 2),
         limit=24,
     )[0]
 

time: 166 us -> 166 us (level)
  no operation moved by 1% of the time
where the time goes in v6:
time: 166 us
  Pallas kernels  84.1 us (51%)
  waiting for transfers between devices  51 us (31%)
  starting transfers between devices  25.2 us (15%)
  local copies, waits for them, and re-layouts  3.3 us (2%)
    pallas_call x28, Pallas kernels, call(): pl.pallas_call(run, grid_spec=pltpu.PrefetchScalarGridSpec(num_scalar_pre...  84.1 us
    ppermute x32, waiting for transfers between devices, hop(): return lax.ppermute(array, AXES, table)  51 us
    ppermute x32, starting transfers between devices, hop(): return lax.ppermute(array, AXES, table)  25.2 us
  transfers between devices with their start and end apart: 32, of which 16 were waited for; matrix products, arithmetic and copies ran while one was open for 0% of the time, Pallas kernels for 43%

profile of v6, /device:TPU:0, one launch (start us, length us, event | category | flops | bytes accessed | tf_op | source)
XLA Modules:
  0.0 166.1 jit_solution(14682803841950202204)
XLA Ops:
  2.3 1.1 copy-done.2
  3.4 1.1 copy-done.3
  4.6 1.0 copy-done.4
  6.3 3.0 %collective-permute-start = (bf16[272,768]{1,0:T(8,128)(2,1)S(1)}, bf16[272,768]{1,0:T(8,128)(2,1)S(1)}, u32[]{:S(2)}, u32[]{:S(2)}) collective-permute-start(bf16[272,768]{1,0:T(8,128)(2,1)S(1)} %get-tuple-element.45.refs_0_), channel_id=1, source_target_pairs={{0,4},{1,3},{2,6},{3,1},{4,0},{5,7},{6,2},{7,5},{8,12},{9,11},{10,... | collective-permute-start | bytes 1253384 | tf_op jit(solution)/shard_map/ppermute | solution.py:119
  9.3 1.5 collective-permute-start.1
  10.8 2.6 %collective-permute-start.2 = (bf16[128,768]{1,0:T(8,128)(2,1)S(1)}, bf16[128,768]{1,0:T(8,128)(2,1)S(1)}, u32[]{:S(2)}, u32[]{:S(2)}) collective-permute-start(bf16[128,768]{1,0:T(8,128)(2,1)S(1)} %get-tuple-element.46.refs_2_), channel_id=1, source_target_pairs={{0,16},{1,17},{2,18},{3,19},{4,20},{5,21},{6,22},{7,23},{8,24},{9,... | collective-permute-start | bytes 589832 | tf_op jit(solution)/shard_map/ppermute | solution.py:119
  13.4 2.5 %gather.2.refs_5_.refs_3_ = bf16[3,512,768]{2,1,0:T(8,128)(2,1)S(1)} custom-call(s32[4]{0:T(128)S(1)} %pad_add_fusion.pos_ref, bf16[272,768]{1,0:T(8,128)(2,1)S(1)} %get-tuple-element.45.refs_0_, bf16[272,768]{1,0:T(8,128)(2,1)S(1)} %get-tuple-element.47.refs_1_, bf16[128,768]{1,0:T(8,128)(2,1)S(1)} %get-tuple-element.46.refs_2_), custom_call_target="tpu_custom_call" | custom-call | flops 1000 | bytes 1000 | tf_op jit(solution)/shard_map/gather/pallas_call | solution.py:47
  15.9 6.1 %collective-permute-done.2.refs_3_ = bf16[128,768]{1,0:T(8,128)(2,1)S(1)} collective-permute-done((bf16[128,768]{1,0:T(8,128)(2,1)S(1)}, bf16[128,768]{1,0:T(8,128)(2,1)S(1)}, u32[]{:S(2)}, u32[]{:S(2)}) %collective-permute-start.2) | collective-permute-done | bytes 196640 | tf_op jit(solution)/shard_map/ppermute | solution.py:119
  23.3 1.8 %collective-permute-done.4.refs_1_.refs_3_ = bf16[544,768]{1,0:T(8,128)(2,1)S(1)} collective-permute-done((bf16[544,768]{1,0:T(8,128)(2,1)S(1)}, bf16[544,768]{1,0:T(8,128)(2,1)S(1)}, u32[]{:S(2)}, u32[]{:S(2)}) %collective-permute-start.4) | collective-permute-done | bytes 835616 | tf_op jit(solution)/shard_map/ppermute | solution.py:119
  25.1 3.7 %gather.3.refs_1_.refs_4_ = bf16[3,1024,768]{2,1,0:T(8,128)(2,1)S(1)} custom-call(s32[4]{0:T(128)S(1)} %pad_add_fusion.pos_ref, bf16[272,768]{1,0:T(8,128)(2,1)S(1)} %collective-permute-done.refs_0_.refs_1_, bf16[544,768]{1,0:T(8,128)(2,1)S(1)} %collective-permute-done.4.refs_1_.refs_3_, bf16[272,768]{1,0:T(8,128)(2,1)S(1)} %get-tuple-element.48.refs_2_.refs_4_.refs_0_, ...), custom_call_target="tpu_custom_call" | custom-call | flops 1000 | bytes 1000 | tf_op jit(solution)/shard_map/gather/pallas_call | solution.py:47
  28.8 2.0 %collective-permute-done.3.refs_0_ = bf16[272,768]{1,0:T(8,128)(2,1)S(1)} collective-permute-done((bf16[272,768]{1,0:T(8,128)(2,1)S(1)}, bf16[272,768]{1,0:T(8,128)(2,1)S(1)}, u32[]{:S(2)}, u32[]{:S(2)}) %collective-permute-start.3) | collective-permute-done | bytes 417824 | tf_op jit(solution)/shard_map/ppermute | solution.py:119
  32.2 8.4 %aggregate_near.1.refs_2_ = f32[3,1024,768]{2,1,0:T(8,128)S(1)} custom-call(s32[4]{0:T(128)S(1)} %pad_add_fusion.pos_ref, bf16[272,768]{1,0:T(8,128)(2,1)S(1)} %get-tuple-element.45.refs_0_, bf16[272,768]{1,0:T(8,128)(2,1)S(1)} %collective-permute-done.refs_0_.refs_1_, bf16[272,768]{1,0:T(8,128)(2,1)S(1)} %get-tuple-element.48.refs_2_.refs_4_.refs_0_, ...), custom_call_target="tpu_custom_call" | custom-call | flops 1000 | bytes 1000 | tf_op jit(solution)/shard_map/aggregate_near/pallas_call | solution.py:47
  40.7 2.3 %collective-permute-done.6.refs_1_ = bf16[256,768]{1,0:T(8,128)(2,1)S(1)} collective-permute-done((bf16[256,768]{1,0:T(8,128)(2,1)S(1)}, bf16[256,768]{1,0:T(8,128)(2,1)S(1)}, u32[]{:S(2)}, u32[]{:S(2)}) %collective-permute-start.6) | collective-permute-done | bytes 393248 | tf_op jit(solution)/shard_map/ppermute | solution.py:119
  43.7 5.1 %aggregate.1.refs_0_.refs_3_ = bf16[3,1024,768]{2,1,0:T(8,128)(2,1)S(1)} custom-call(s32[4]{0:T(128)S(1)} %pad_add_fusion.pos_ref, bf16[272,768]{1,0:T(8,128)(2,1)S(1)} %step.13.refs_6_.refs_0_, bf16[272,768]{1,0:T(8,128)(2,1)S(1)} %collective-permute-done.5.refs_3_.refs_1_, f32[3,1024,768]{2,1,0:T(8,128)S(1)} %aggregate_near.1.refs_2_, ...), custom_call_target="tpu_custom_call" | custom-call | flops 1000 | bytes 1000 | tf_op jit(solution)/shard_map/aggregate/pallas_call | solution.py:47
  48.9 2.6 %weight_terms.4.refs_2_ = bf16[3,384,384]{2,1,0:T(8,128)(2,1)S(1)} custom-call(s32[4]{0:T(128)S(1)} %pad_add_fusion.pos_ref, bf16[3,1024,768]{2,1,0:T(8,128)(2,1)S(1)} %aggregate.1.refs_0_.refs_3_, bf16[512,768]{1,0:T(8,128)(2,1)S(1)} %step.14.refs_3_.refs_1_, bf16[512,768]{1,0:T(8,128)(2,1)S(1)} %collective-permute-done.7.refs_2_, ...), custom_call_target="tpu_custom_call" | custom-call | flops 1000 | bytes 1000 | tf_op jit(solution)/shard_map/weight_terms/pallas_call | solution.py:47
  52.0 2.5 %output_terms.2.refs_2_.refs_6_ = bf16[512,768]{1,0:T(8,128)(2,1)S(1)} custom-call(s32[4]{0:T(128)S(1)} %pad_add_fusion.pos_ref, bf16[3,1024,768]{2,1,0:T(8,128)(2,1)S(1)} %aggregate.1.refs_0_.refs_3_, bf16[3,768,768]{2,1,0:T(8,128)(2,1)S(1)} %copy-done, bf16[3,384,384]{2,1,0:T(8,128)(2,1)S(1)} %weight_terms.4.refs_2_), custom_call_target="tpu_custom_call" | custom-call | flops 1000 | bytes 1000 | tf_op jit(solution)/shard_map/output_terms/pallas_call | solution.py:47
  54.5 2.5 %output_terms.3.refs_3_.refs_8_ = f32[512,768]{1,0:T(8,128)S(1)} custom-call(s32[4]{0:T(128)S(1)} %pad_add_fusion.pos_ref, bf16[3,1024,768]{2,1,0:T(8,128)(2,1)S(1)} %aggregate.1.refs_0_.refs_3_, bf16[3,768,768]{2,1,0:T(8,128)(2,1)S(1)} %copy-done, bf16[512,768]{1,0:T(8,128)(2,1)S(1)} %output_terms.2.refs_2_.refs_6_), custom_call_target="tpu_custom_call" | custom-call | flops 1000 | bytes 1000 | tf_op jit(solution)/shard_map/output_terms/pallas_call | solution.py:47
  57.1 2.6 %weight_terms.5.refs_3_ = bf16[3,384,384]{2,1,0:T(8,128)(2,1)S(1)} custom-call(s32[4]{0:T(128)S(1)} %pad_add_fusion.pos_ref, bf16[3,1024,768]{2,1,0:T(8,128)(2,1)S(1)} %aggregate.1.refs_0_.refs_3_, bf16[512,768]{1,0:T(8,128)(2,1)S(1)} %step.14.refs_3_.refs_1_, bf16[512,768]{1,0:T(8,128)(2,1)S(1)} %collective-permute-done.7.refs_2_, ...), custom_call_target="tpu_custom_call" | custom-call | flops 1000 | bytes 1000 | tf_op jit(solution)/shard_map/weight_terms/pallas_call | solution.py:47
  59.6 1.6 collective-permute-start.8
  61.2 2.5 %weight_terms.6.refs_3_.refs_0_ = f32[3,384,384]{2,1,0:T(8,128)S(1)} custom-call(s32[4]{0:T(128)S(1)} %pad_add_fusion.pos_ref, bf16[3,1024,768]{2,1,0:T(8,128)(2,1)S(1)} %aggregate.1.refs_0_.refs_3_, bf16[512,768]{1,0:T(8,128)(2,1)S(1)} %step.14.refs_3_.refs_1_, bf16[512,768]{1,0:T(8,128)(2,1)S(1)} %collective-permute-done.7.refs_2_, ...), custom_call_target="tpu_custom_call" | custom-call | flops 1000 | bytes 1000 | tf_op jit(solution)/shard_map/weight_terms/pallas_call | solution.py:47
  63.8 2.5 %weight_terms.7.refs_2_.refs_0_ = f32[3,384,384]{2,1,0:T(8,128)S(1)} custom-call(s32[4]{0:T(128)S(1)} %pad_add_fusion.pos_ref, bf16[3,1024,768]{2,1,0:T(8,128)(2,1)S(1)} %aggregate.1.refs_0_.refs_3_, bf16[512,768]{1,0:T(8,128)(2,1)S(1)} %step.14.refs_3_.refs_1_, bf16[512,768]{1,0:T(8,128)(2,1)S(1)} %collective-permute-done.7.refs_2_, ...), custom_call_target="tpu_custom_call" | custom-call | flops 1000 | bytes 1000 | tf_op jit(solution)/shard_map/weight_terms/pallas_call | solution.py:47
  67.6 8.6 %feature_terms.4 = (f32[256,768]{1,0:T(8,128)S(1)}, bf16[256,768]{1,0:T(8,128)(2,1)S(1)}) custom-call(s32[4]{0:T(128)S(1)} %pad_add_fusion.pos_ref, bf16[272,768]{1,0:T(8,128)(2,1)S(1)} %get-tuple-element.48.refs_2_.refs_4_.refs_0_, bf16[512,768]{1,0:T(8,128)(2,1)S(1)} %step.14.refs_3_.refs_1_, bf16[512,768]{1,0:T(8,128)(2,1)S(1)} %collective-permute-done.7.refs_2_, ...), custom_call_target="tpu_custom_call" | custom-call | flops 1000 | bytes 1000 | tf_op jit(solution)/shard_map/feature_terms/pallas_call | solution.py:47
  76.2 2.1 %collective-permute-done.8.refs_1_ = bf16[3,384,384]{2,1,0:T(8,128)(2,1)S(1)} collective-permute-done((bf16[3,384,384]{2,1,0:T(8,128)(2,1)S(1)}, bf16[3,384,384]{2,1,0:T(8,128)(2,1)S(1)}, u32[]{:S(2)}, u32[]{:S(2)}) %collective-permute-start.8) | collective-permute-done | bytes 884768 | tf_op jit(solution)/shard_map/ppermute | solution.py:119
  80.4 8.5 %feature_terms.5 = (f32[256,768]{1,0:T(8,128)S(1)}, bf16[256,768]{1,0:T(8,128)(2,1)S(1)}) custom-call(s32[4]{0:T(128)S(1)} %pad_add_fusion.pos_ref, bf16[272,768]{1,0:T(8,128)(2,1)S(1)} %step.13.refs_6_.refs_0_, bf16[512,768]{1,0:T(8,128)(2,1)S(1)} %step.14.refs_3_.refs_1_, bf16[512,768]{1,0:T(8,128)(2,1)S(1)} %collective-permute-done.7.refs_2_, ...), custom_call_target="tpu_custom_call" | custom-call | flops 1000 | bytes 1000 | tf_op jit(solution)/shard_map/feature_terms/pallas_call | solution.py:47
  89.7 3.4 %collective-permute-start.13 = (bf16[3,96,384]{2,1,0:T(8,128)(2,1)S(1)}, bf16[3,96,384]{2,1,0:T(8,128)(2,1)S(1)}, u32[]{:S(2)}, u32[]{:S(2)}) collective-permute-start(bf16[3,96,384]{2,1,0:T(8,128)(2,1)S(1)} %get-tuple-element.61.refs_4_.refs_0_), channel_id=1, source_target_pairs={{0,16},{1,17},{2,18},{3,19},{4,20},{5,21},{6,22},{7,23},{8,24},{9,... | collective-permute-start | bytes 663560 | tf_op jit(solution)/shard_map/ppermute | solution.py:119
  93.4 8.5 %feature_terms.6 = (f32[256,768]{1,0:T(8,128)S(1)}, bf16[256,768]{1,0:T(8,128)(2,1)S(1)}) custom-call(s32[4]{0:T(128)S(1)} %pad_add_fusion.pos_ref, bf16[272,768]{1,0:T(8,128)(2,1)S(1)} %collective-permute-done.refs_0_.refs_1_, bf16[512,768]{1,0:T(8,128)(2,1)S(1)} %step.14.refs_3_.refs_1_, bf16[512,768]{1,0:T(8,128)(2,1)S(1)} %collective-permute-done.7.refs_2_, ...), custom_call_target="tpu_custom_call" | custom-call | flops 1000 | bytes 1000 | tf_op jit(solution)/shard_map/feature_terms/pallas_call | solution.py:47
  101.8 2.2 %collective-permute-done.13.refs_1_ = bf16[3,96,384]{2,1,0:T(8,128)(2,1)S(1)} collective-permute-done((bf16[3,96,384]{2,1,0:T(8,128)(2,1)S(1)}, bf16[3,96,384]{2,1,0:T(8,128)(2,1)S(1)}, u32[]{:S(2)}, u32[]{:S(2)}) %collective-permute-start.13) | collective-permute-done | bytes 221216 | tf_op jit(solution)/shard_map/ppermute | solution.py:119
  104.0 1.2 collective-permute-done.14.refs_3_
  105.1 0.8 step.18
  105.9 0.8 collective-permute-start.19
  107.4 1.2 collective-permute-start.17
  108.6 8.4 %feature_terms.7 = (f32[256,768]{1,0:T(8,128)S(1)}, bf16[256,768]{1,0:T(8,128)(2,1)S(1)}) custom-call(s32[4]{0:T(128)S(1)} %pad_add_fusion.pos_ref, bf16[272,768]{1,0:T(8,128)(2,1)S(1)} %get-tuple-element.45.refs_0_, bf16[512,768]{1,0:T(8,128)(2,1)S(1)} %step.14.refs_3_.refs_1_, bf16[512,768]{1,0:T(8,128)(2,1)S(1)} %collective-permute-done.7.refs_2_, ...), custom_call_target="tpu_custom_call" | custom-call | flops 1000 | bytes 1000 | tf_op jit(solution)/shard_map/feature_terms/pallas_call | solution.py:47
  117.6 2.8 %collective-permute-done.17.refs_3_ = bf16[3,96,384]{2,1,0:T(8,128)(2,1)S(1)} collective-permute-done((bf16[3,96,384]{2,1,0:T(8,128)(2,1)S(1)}, bf16[3,96,384]{2,1,0:T(8,128)(2,1)S(1)}, u32[]{:S(2)}, u32[]{:S(2)}) %collective-permute-start.17) | collective-permute-done | bytes 221216 | tf_op jit(solution)/shard_map/ppermute | solution.py:119
  120.5 0.9 step.19
  121.4 1.3 collective-permute-start.21
  123.5 8.3 %collective-permute-done.22.refs_3_ = bf16[288,384]{1,0:T(8,128)(2,1)S(1)} collective-permute-done((bf16[288,384]{1,0:T(8,128)(2,1)S(1)}, bf16[288,384]{1,0:T(8,128)(2,1)S(1)}, u32[]{:S(2)}, u32[]{:S(2)}) %collective-permute-start.22) | collective-permute-done | bytes 221216 | tf_op jit(solution)/shard_map/ppermute | solution.py:119
  131.8 2.2 %collective-permute-done.24.refs_7_ = bf16[256,768]{1,0:T(8,128)(2,1)S(1)} collective-permute-done((bf16[256,768]{1,0:T(8,128)(2,1)S(1)}, bf16[256,768]{1,0:T(8,128)(2,1)S(1)}, u32[]{:S(2)}, u32[]{:S(2)}) %collective-permute-start.24) | collective-permute-done | bytes 393248 | tf_op jit(solution)/shard_map/ppermute | solution.py:119
  134.0 0.8 step.20
  134.8 1.3 collective-permute-start.25
  136.1 1.5 collective-permute-start.30
  137.7 7.8 %collective-permute-done.27.refs_5_ = bf16[256,768]{1,0:T(8,128)(2,1)S(1)} collective-permute-done((bf16[256,768]{1,0:T(8,128)(2,1)S(1)}, bf16[256,768]{1,0:T(8,128)(2,1)S(1)}, u32[]{:S(2)}, u32[]{:S(2)}) %collective-permute-start.27) | collective-permute-done | bytes 393248 | tf_op jit(solution)/shard_map/ppermute | solution.py:119
  145.5 1.7 %collective-permute-done.25.refs_1_ = bf16[576,384]{1,0:T(8,128)(2,1)S(1)} collective-permute-done((bf16[576,384]{1,0:T(8,128)(2,1)S(1)}, bf16[576,384]{1,0:T(8,128)(2,1)S(1)}, u32[]{:S(2)}, u32[]{:S(2)}) %collective-permute-start.25) | collective-permute-done | bytes 442400 | tf_op jit(solution)/shard_map/ppermute | solution.py:119
  147.2 1.6 step.21
  148.8 1.1 collective-permute-start.31
  149.9 8.4 %collective-permute-done.28.refs_1_ = bf16[128,768]{1,0:T(8,128)(2,1)S(1)} collective-permute-done((bf16[128,768]{1,0:T(8,128)(2,1)S(1)}, bf16[128,768]{1,0:T(8,128)(2,1)S(1)}, u32[]{:S(2)}, u32[]{:S(2)}) %collective-permute-start.28) | collective-permute-done | bytes 196640 | tf_op jit(solution)/shard_map/ppermute | solution.py:119
  159.0 1.4 collective-permute-done.29.refs_1_
  160.4 1.3 step.23
  161.8 4.3 %assemble.1 = f32[3,768,768]{2,1,0:T(8,128)} custom-call(s32[4]{0:T(128)S(1)} %pad_add_fusion.pos_ref, bf16[1152,384]{1,0:T(8,128)(2,1)S(1)} %get-tuple-element.82.refs_6_.refs_0_, bf16[1152,384]{1,0:T(8,128)(2,1)S(1)} %collective-permute-done.30.refs_1_, bf16[1152,384]{1,0:T(8,128)(2,1)S(1)} %get-tuple-element.85.refs_2_, ...), custom_call_target="tpu_custom_call" | custom-call | flops 1000 | bytes 1000 | tf_op jit(solution)/shard_map/assemble/pallas_call | solution.py:47
  (61 shorter events, 13.4 us)
Async XLA Ops:
  2.3 1.1 copy-start.2
  3.4 1.1 copy-start.3
  4.5 1.0 copy-start.4
  6.3 15.7 %collective-permute-start = (bf16[272,768]{1,0:T(8,128)(2,1)S(1)}, bf16[272,768]{1,0:T(8,128)(2,1)S(1)}, u32[]{:S(2)}, u32[]{:S(2)}) collective-permute-start(bf16[272,768]{1,0:T(8,128)(2,1)S(1)} %get-tuple-element.45.refs_0_), channel_id=1, source_target_pairs={{0,4},{1,3},{2,6},{3,1},{4,0},{5,7},{6,2},{7,5},{8,12},{9,11},{10,... | collective-permute-start | bytes 1253384 | tf_op jit(solution)/shard_map/ppermute | solution.py:119
  9.3 12.7 %collective-permute-start.1 = (bf16[272,768]{1,0:T(8,128)(2,1)S(1)}, bf16[272,768]{1,0:T(8,128)(2,1)S(1)}, u32[]{:S(2)}, u32[]{:S(2)}) collective-permute-start(bf16[272,768]{1,0:T(8,128)(2,1)S(1)} %get-tuple-element.45.refs_0_), channel_id=1, source_target_pairs={{0,2},{1,5},{2,0},{3,7},{4,6},{5,1},{6,4},{7,3},{8,10},{9,13},{10,... | collective-permute-start | bytes 1253384 | tf_op jit(solution)/shard_map/ppermute | solution.py:119
  10.8 11.2 %collective-permute-start.2 = (bf16[128,768]{1,0:T(8,128)(2,1)S(1)}, bf16[128,768]{1,0:T(8,128)(2,1)S(1)}, u32[]{:S(2)}, u32[]{:S(2)}) collective-permute-start(bf16[128,768]{1,0:T(8,128)(2,1)S(1)} %get-tuple-element.46.refs_2_), channel_id=1, source_target_pairs={{0,16},{1,17},{2,18},{3,19},{4,20},{5,21},{6,22},{7,23},{8,24},{9,... | collective-permute-start | bytes 589832 | tf_op jit(solution)/shard_map/ppermute | solution.py:119
  22.7 2.4 %collective-permute-start.4 = (bf16[544,768]{1,0:T(8,128)(2,1)S(1)}, bf16[544,768]{1,0:T(8,128)(2,1)S(1)}, u32[]{:S(2)}, u32[]{:S(2)}) collective-permute-start(bf16[544,768]{1,0:T(8,128)(2,1)S(1)} %get-tuple-element.49), channel_id=1, source_target_pairs={{0,1},{1,0},{2,3},{3,2},{4,5},{5,4},{6,7},{7,6},{8,9},{9,8},{10,11... | collective-permute-start | bytes 2506760 | tf_op jit(solution)/shard_map/ppermute | solution.py:119
  22.7 8.1 %collective-permute-start.3 = (bf16[272,768]{1,0:T(8,128)(2,1)S(1)}, bf16[272,768]{1,0:T(8,128)(2,1)S(1)}, u32[]{:S(2)}, u32[]{:S(2)}) collective-permute-start(bf16[272,768]{1,0:T(8,128)(2,1)S(1)} %get-tuple-element.48.refs_2_.refs_4_.refs_0_), channel_id=1, source_target_pairs={{0,4},{1,3},{2,6},{3,1},{4,0},{5,7},{6,2},{7,5},{8,12},{9,11},{10,... | collective-permute-start | bytes 1253384 | tf_op jit(solution)/shard_map/ppermute | solution.py:119
  28.8 3.4 %copy-start.1 = (bf16[3,256,768]{2,1,0:T(8,128)(2,1)S(1)}, bf16[3,256,768]{2,1,0:T(8,128)(2,1)}, u32[]{:S(2)}) copy-start(bf16[3,256,768]{2,1,0:T(8,128)(2,1)} %refs_5_.1) | copy-start | bytes 3538948
  31.4 11.6 %collective-permute-start.5 = (bf16[272,768]{1,0:T(8,128)(2,1)S(1)}, bf16[272,768]{1,0:T(8,128)(2,1)S(1)}, u32[]{:S(2)}, u32[]{:S(2)}) collective-permute-start(bf16[272,768]{1,0:T(8,128)(2,1)S(1)} %step.13.refs_6_.refs_0_), channel_id=1, source_target_pairs={{0,1},{1,0},{2,3},{3,2},{4,5},{5,4},{6,7},{7,6},{8,9},{9,8},{10,11... | collective-permute-start | bytes 1253384 | tf_op jit(solution)/shard_map/ppermute | solution.py:119
  31.5 11.5 %collective-permute-start.6 = (bf16[256,768]{1,0:T(8,128)(2,1)S(1)}, bf16[256,768]{1,0:T(8,128)(2,1)S(1)}, u32[]{:S(2)}, u32[]{:S(2)}) collective-permute-start(bf16[256,768]{1,0:T(8,128)(2,1)S(1)} %get-tuple-element.50.refs_0_), channel_id=1, source_target_pairs={{0,8},{1,9},{2,10},{3,11},{4,12},{5,13},{6,14},{7,15},{8,0},{9,1},... | collective-permute-start | bytes 1179656 | tf_op jit(solution)/shard_map/ppermute | solution.py:119
  43.6 5.2 %collective-permute-start.7 = (bf16[512,768]{1,0:T(8,128)(2,1)S(1)}, bf16[512,768]{1,0:T(8,128)(2,1)S(1)}, u32[]{:S(2)}, u32[]{:S(2)}) collective-permute-start(bf16[512,768]{1,0:T(8,128)(2,1)S(1)} %step.14.refs_3_.refs_1_), channel_id=1, source_target_pairs={{0,1},{1,0},{2,3},{3,2},{4,5},{5,4},{6,7},{7,6},{8,9},{9,8},{10,11... | collective-permute-start | bytes 2359304 | tf_op jit(solution)/shard_map/ppermute | solution.py:119
  48.8 3.1 %copy-start = (bf16[3,768,768]{2,1,0:T(8,128)(2,1)S(1)}, bf16[3,768,768]{2,1,0:T(8,128)(2,1)}, u32[]{:S(2)}) copy-start(bf16[3,768,768]{2,1,0:T(8,128)(2,1)} %refs_3_.9) | copy-start | bytes 10616836
  51.4 14.9 %collective-permute-start.9 = (bf16[3,384,384]{2,1,0:T(8,128)(2,1)S(1)}, bf16[3,384,384]{2,1,0:T(8,128)(2,1)S(1)}, u32[]{:S(2)}, u32[]{:S(2)}) collective-permute-start(bf16[3,384,384]{2,1,0:T(8,128)(2,1)S(1)} %weight_terms.4.refs_2_), channel_id=1, source_target_pairs={{0,4},{1,3},{2,6},{3,1},{4,0},{5,7},{6,2},{7,5},{8,12},{9,11},{10,... | collective-permute-start | bytes 2654216 | tf_op jit(solution)/shard_map/ppermute | solution.py:119
  59.6 18.7 %collective-permute-start.8 = (bf16[3,384,384]{2,1,0:T(8,128)(2,1)S(1)}, bf16[3,384,384]{2,1,0:T(8,128)(2,1)S(1)}, u32[]{:S(2)}, u32[]{:S(2)}) collective-permute-start(bf16[3,384,384]{2,1,0:T(8,128)(2,1)S(1)} %weight_terms.5.refs_3_), channel_id=1, source_target_pairs={{0,4},{1,3},{2,6},{3,1},{4,0},{5,7},{6,2},{7,5},{8,12},{9,11},{10,... | collective-permute-start | bytes 2654216 | tf_op jit(solution)/shard_map/ppermute | solution.py:119
  67.0 11.3 %collective-permute-start.10 = (bf16[3,192,384]{2,1,0:T(8,128)(2,1)S(1)}, bf16[3,192,384]{2,1,0:T(8,128)(2,1)S(1)}, u32[]{:S(2)}, u32[]{:S(2)}) collective-permute-start(bf16[3,192,384]{2,1,0:T(8,128)(2,1)S(1)} %get-tuple-element.52), channel_id=1, source_target_pairs={{0,2},{1,5},{2,0},{3,7},{4,6},{5,1},{6,4},{7,3},{8,10},{9,13},{10,... | collective-permute-start | bytes 1327112 | tf_op jit(solution)/shard_map/ppermute | solution.py:119
  79.1 9.8 %collective-permute-start.12 = (bf16[3,192,384]{2,1,0:T(8,128)(2,1)S(1)}, bf16[3,192,384]{2,1,0:T(8,128)(2,1)S(1)}, u32[]{:S(2)}, u32[]{:S(2)}) collective-permute-start(bf16[3,192,384]{2,1,0:T(8,128)(2,1)S(1)} %get-tuple-element.57), channel_id=1, source_target_pairs={{0,2},{1,5},{2,0},{3,7},{4,6},{5,1},{6,4},{7,3},{8,10},{9,13},{10,... | collective-permute-start | bytes 1327112 | tf_op jit(solution)/shard_map/ppermute | solution.py:119
  79.7 9.1 %collective-permute-start.11 = (bf16[3,96,384]{2,1,0:T(8,128)(2,1)S(1)}, bf16[3,96,384]{2,1,0:T(8,128)(2,1)S(1)}, u32[]{:S(2)}, u32[]{:S(2)}) collective-permute-start(bf16[3,96,384]{2,1,0:T(8,128)(2,1)S(1)} %get-tuple-element.55), channel_id=1, source_target_pairs={{0,8},{1,9},{2,10},{3,11},{4,12},{5,13},{6,14},{7,15},{8,0},{9,1},... | collective-permute-start | bytes 663560 | tf_op jit(solution)/shard_map/ppermute | solution.py:119
  89.6 15.5 %collective-permute-start.15 = (bf16[512,768]{1,0:T(8,128)(2,1)S(1)}, bf16[512,768]{1,0:T(8,128)(2,1)S(1)}, u32[]{:S(2)}, u32[]{:S(2)}) collective-permute-start(bf16[512,768]{1,0:T(8,128)(2,1)S(1)} %get-tuple-element.65), channel_id=1, source_target_pairs={{0,1},{1,0},{2,3},{3,2},{4,5},{5,4},{6,7},{7,6},{8,9},{9,8},{10,11... | collective-permute-start | bytes 2359304 | tf_op jit(solution)/shard_map/ppermute | solution.py:119
  89.7 14.3 %collective-permute-start.13 = (bf16[3,96,384]{2,1,0:T(8,128)(2,1)S(1)}, bf16[3,96,384]{2,1,0:T(8,128)(2,1)S(1)}, u32[]{:S(2)}, u32[]{:S(2)}) collective-permute-start(bf16[3,96,384]{2,1,0:T(8,128)(2,1)S(1)} %get-tuple-element.61.refs_4_.refs_0_), channel_id=1, source_target_pairs={{0,16},{1,17},{2,18},{3,19},{4,20},{5,21},{6,22},{7,23},{8,24},{9,... | collective-permute-start | bytes 663560 | tf_op jit(solution)/shard_map/ppermute | solution.py:119
  93.1 12.0 %collective-permute-start.14 = (bf16[3,96,384]{2,1,0:T(8,128)(2,1)S(1)}, bf16[3,96,384]{2,1,0:T(8,128)(2,1)S(1)}, u32[]{:S(2)}, u32[]{:S(2)}) collective-permute-start(bf16[3,96,384]{2,1,0:T(8,128)(2,1)S(1)} %get-tuple-element.63), channel_id=1, source_target_pairs={{0,8},{1,9},{2,10},{3,11},{4,12},{5,13},{6,14},{7,15},{8,0},{9,1},... | collective-permute-start | bytes 663560 | tf_op jit(solution)/shard_map/ppermute | solution.py:119
  93.4 23.7 %collective-permute-start.20 = (bf16[512,768]{1,0:T(8,128)(2,1)S(1)}, bf16[512,768]{1,0:T(8,128)(2,1)S(1)}, u32[]{:S(2)}, u32[]{:S(2)}) collective-permute-start(bf16[512,768]{1,0:T(8,128)(2,1)S(1)} %get-tuple-element.72), channel_id=1, source_target_pairs={{0,1},{1,0},{2,3},{3,2},{4,5},{5,4},{6,7},{7,6},{8,9},{9,8},{10,11... | collective-permute-start | bytes 2359304 | tf_op jit(solution)/shard_map/ppermute | solution.py:119
  105.9 14.6 %collective-permute-start.19 = (bf16[512,768]{1,0:T(8,128)(2,1)S(1)}, bf16[512,768]{1,0:T(8,128)(2,1)S(1)}, u32[]{:S(2)}, u32[]{:S(2)}) collective-permute-start(bf16[512,768]{1,0:T(8,128)(2,1)S(1)} %get-tuple-element.70), channel_id=1, source_target_pairs={{0,4},{1,3},{2,6},{3,1},{4,0},{5,7},{6,2},{7,5},{8,12},{9,11},{10,... | collective-permute-start | bytes 2359304 | tf_op jit(solution)/shard_map/ppermute | solution.py:119
  106.7 13.7 %collective-permute-start.18 = (bf16[256,768]{1,0:T(8,128)(2,1)S(1)}, bf16[256,768]{1,0:T(8,128)(2,1)S(1)}, u32[]{:S(2)}, u32[]{:S(2)}) collective-permute-start(bf16[256,768]{1,0:T(8,128)(2,1)S(1)} %get-tuple-element.69), channel_id=1, source_target_pairs={{0,1},{1,0},{2,3},{3,2},{4,5},{5,4},{6,7},{7,6},{8,9},{9,8},{10,11... | collective-permute-start | bytes 1179656 | tf_op jit(solution)/shard_map/ppermute | solution.py:119
  106.7 10.9 %collective-permute-start.16 = (bf16[288,384]{1,0:T(8,128)(2,1)S(1)}, bf16[288,384]{1,0:T(8,128)(2,1)S(1)}, u32[]{:S(2)}, u32[]{:S(2)}) collective-permute-start(bf16[288,384]{1,0:T(8,128)(2,1)S(1)} %bitcast.14), channel_id=1, source_target_pairs={{0,8},{1,9},{2,10},{3,11},{4,12},{5,13},{6,14},{7,15},{8,0},{9,1},... | collective-permute-start | bytes 663560 | tf_op jit(solution)/shard_map/ppermute | solution.py:119
  107.4 13.1 %collective-permute-start.17 = (bf16[3,96,384]{2,1,0:T(8,128)(2,1)S(1)}, bf16[3,96,384]{2,1,0:T(8,128)(2,1)S(1)}, u32[]{:S(2)}, u32[]{:S(2)}) collective-permute-start(bf16[3,96,384]{2,1,0:T(8,128)(2,1)S(1)} %get-tuple-element.68.refs_2_), channel_id=1, source_target_pairs={{0,16},{1,17},{2,18},{3,19},{4,20},{5,21},{6,22},{7,23},{8,24},{9,... | collective-permute-start | bytes 663560 | tf_op jit(solution)/shard_map/ppermute | solution.py:119
  121.4 12.6 %collective-permute-start.21 = (bf16[576,384]{1,0:T(8,128)(2,1)S(1)}, bf16[576,384]{1,0:T(8,128)(2,1)S(1)}, u32[]{:S(2)}, u32[]{:S(2)}) collective-permute-start(bf16[576,384]{1,0:T(8,128)(2,1)S(1)} %get-tuple-element.74.refs_0_.refs_8_), channel_id=1, source_target_pairs={{0,2},{1,5},{2,0},{3,7},{4,6},{5,1},{6,4},{7,3},{8,10},{9,13},{10,... | collective-permute-start | bytes 1327112 | tf_op jit(solution)/shard_map/ppermute | solution.py:119
  122.7 9.1 %collective-permute-start.23 = (bf16[256,768]{1,0:T(8,128)(2,1)S(1)}, bf16[256,768]{1,0:T(8,128)(2,1)S(1)}, u32[]{:S(2)}, u32[]{:S(2)}) collective-permute-start(bf16[256,768]{1,0:T(8,128)(2,1)S(1)} %get-tuple-element.76), channel_id=1, source_target_pairs={{0,1},{1,0},{2,3},{3,2},{4,5},{5,4},{6,7},{7,6},{8,9},{9,8},{10,11... | collective-permute-start | bytes 1179656 | tf_op jit(solution)/shard_map/ppermute | solution.py:119
  122.7 11.3 %collective-permute-start.24 = (bf16[256,768]{1,0:T(8,128)(2,1)S(1)}, bf16[256,768]{1,0:T(8,128)(2,1)S(1)}, u32[]{:S(2)}, u32[]{:S(2)}) collective-permute-start(bf16[256,768]{1,0:T(8,128)(2,1)S(1)} %get-tuple-element.77), channel_id=1, source_target_pairs={{0,2},{1,5},{2,0},{3,7},{4,6},{5,1},{6,4},{7,3},{8,10},{9,13},{10,... | collective-permute-start | bytes 1179656 | tf_op jit(solution)/shard_map/ppermute | solution.py:119
  123.5 8.3 %collective-permute-start.22 = (bf16[288,384]{1,0:T(8,128)(2,1)S(1)}, bf16[288,384]{1,0:T(8,128)(2,1)S(1)}, u32[]{:S(2)}, u32[]{:S(2)}) collective-permute-start(bf16[288,384]{1,0:T(8,128)(2,1)S(1)} %bitcast.16), channel_id=1, source_target_pairs={{0,8},{1,9},{2,10},{3,11},{4,12},{5,13},{6,14},{7,15},{8,0},{9,1},... | collective-permute-start | bytes 663560 | tf_op jit(solution)/shard_map/ppermute | solution.py:119
  134.8 12.3 %collective-permute-start.25 = (bf16[576,384]{1,0:T(8,128)(2,1)S(1)}, bf16[576,384]{1,0:T(8,128)(2,1)S(1)}, u32[]{:S(2)}, u32[]{:S(2)}) collective-permute-start(bf16[576,384]{1,0:T(8,128)(2,1)S(1)} %get-tuple-element.78.refs_0_), channel_id=1, source_target_pairs={{0,2},{1,5},{2,0},{3,7},{4,6},{5,1},{6,4},{7,3},{8,10},{9,13},{10,... | collective-permute-start | bytes 1327112 | tf_op jit(solution)/shard_map/ppermute | solution.py:119
  136.1 9.4 %collective-permute-start.27 = (bf16[256,768]{1,0:T(8,128)(2,1)S(1)}, bf16[256,768]{1,0:T(8,128)(2,1)S(1)}, u32[]{:S(2)}, u32[]{:S(2)}) collective-permute-start(bf16[256,768]{1,0:T(8,128)(2,1)S(1)} %get-tuple-element.81), channel_id=1, source_target_pairs={{0,8},{1,9},{2,10},{3,11},{4,12},{5,13},{6,14},{7,15},{8,0},{9,1},... | collective-permute-start | bytes 1179656 | tf_op jit(solution)/shard_map/ppermute | solution.py:119
  136.1 9.4 %collective-permute-start.26 = (bf16[256,768]{1,0:T(8,128)(2,1)S(1)}, bf16[256,768]{1,0:T(8,128)(2,1)S(1)}, u32[]{:S(2)}, u32[]{:S(2)}) collective-permute-start(bf16[256,768]{1,0:T(8,128)(2,1)S(1)} %get-tuple-element.79.refs_2_), channel_id=1, source_target_pairs={{0,1},{1,0},{2,3},{3,2},{4,5},{5,4},{6,7},{7,6},{8,9},{9,8},{10,11... | collective-permute-start | bytes 1179656 | tf_op jit(solution)/shard_map/ppermute | solution.py:119
  136.1 25.6 %collective-permute-start.30 = (bf16[1152,384]{1,0:T(8,128)(2,1)S(1)}, bf16[1152,384]{1,0:T(8,128)(2,1)S(1)}, u32[]{:S(2)}, u32[]{:S(2)}) collective-permute-start(bf16[1152,384]{1,0:T(8,128)(2,1)S(1)} %get-tuple-element.82.refs_6_.refs_0_), channel_id=1, source_target_pairs={{0,4},{1,3},{2,6},{3,1},{4,0},{5,7},{6,2},{7,5},{8,12},{9,11},{10,... | collective-permute-start | bytes 2654216 | tf_op jit(solution)/shard_map/ppermute | solution.py:119
  148.8 13.0 %collective-permute-start.31 = (bf16[1152,384]{1,0:T(8,128)(2,1)S(1)}, bf16[1152,384]{1,0:T(8,128)(2,1)S(1)}, u32[]{:S(2)}, u32[]{:S(2)}) collective-permute-start(bf16[1152,384]{1,0:T(8,128)(2,1)S(1)} %get-tuple-element.85.refs_2_), channel_id=1, source_target_pairs={{0,4},{1,3},{2,6},{3,1},{4,0},{5,7},{6,2},{7,5},{8,12},{9,11},{10,... | collective-permute-start | bytes 2654216 | tf_op jit(solution)/shard_map/ppermute | solution.py:119
  149.9 8.5 %collective-permute-start.28 = (bf16[128,768]{1,0:T(8,128)(2,1)S(1)}, bf16[128,768]{1,0:T(8,128)(2,1)S(1)}, u32[]{:S(2)}, u32[]{:S(2)}) collective-permute-start(bf16[128,768]{1,0:T(8,128)(2,1)S(1)} %get-tuple-element.84), channel_id=1, source_target_pairs={{0,16},{1,17},{2,18},{3,19},{4,20},{5,21},{6,22},{7,23},{8,24},{9,... | collective-permute-start | bytes 589832 | tf_op jit(solution)/shard_map/ppermute | solution.py:119
  158.9 1.5 collective-permute-start.29
